TPU v7x, 32 devices: a whole 2x2x4 slice. The times are simulated.
32 devices in a mesh: member: 2 (over x), lat: 8 (over z, y), lon: 2 (over core).
Axes of the slice: x: 2, y: 2, z: 4, core: 2. Of those that a mesh axis runs over, the one named last changes fastest.
Arguments:
- tokens: bfloat16 [128, 192, 1024], P(('member', 'lat'), 'lon'), parts along dimension 0, may hold values from -6 to 6
- ln_gain: float32 [1024], replicated, may hold values from 0.5 to 1.5
- w_query: bfloat16 [1024, 1024], replicated, may hold values from -3 to 3
- w_keyval: bfloat16 [1024, 2048], replicated, may hold values from -3 to 3
- w_out: bfloat16 [1024, 1024], replicated, may hold values from -0.1875 to 0.1875
- w_dec: bfloat16 [1024, 512], replicated, may hold values from -0.1875 to 0.1875
- nudge: float32 [32], replicated, may hold values from 0.2 to 1
- state: float32 [32, 512, 768], P(None, ('member', 'lat'), 'lon'), parts along dimension 1, may hold values from -6 to 6
Outputs:
- advanced: float32 [32, 512, 768], P(None, ('member', 'lat', 'lon')), parts along dimension 1
There are 2 independent parts, one for each index of `member`. A program takes and returns all parts, laid end to end along the dimension named above; an argument that names none is the same for every part. Nothing has to cross between parts.
All inputs are finite; a program needn't handle non-finite values.
Results may differ from a plain program's by a relative error of at most 0.003.
Values may be sent and summed in bfloat16 or wider, within the bound.
No kernel may reach another device: no remote copies, remote signals or barrier semaphores. Data moves between devices by JAX's collectives and lax.ppermute only.
A program may use at most 128 MiB of HBM per device.

v0:
```python
import math

import jax
import jax.numpy as jnp
from jax import lax
from jax.sharding import PartitionSpec as P

HEADS = 16
WIN = 8
PATCH = 4
VARS = 4
LEV = 8
LON_PIX = 768
KEEP = 256


time_step = 0.1
diffusion = 0.5
epsilon = 1e-05


def padded_2(x, sides, width, wrap):
    for axis, dim in sides:
        size, length = (lax.axis_size(axis), x.shape[dim])
        up = [(i, (i + 1) % size) for i in range(size if wrap else size - 1)]
        down = [(j, i) for i, j in up]
        last = lax.slice_in_dim(x, length - width, length, axis=dim)
        first = lax.slice_in_dim(x, 0, width, axis=dim)
        before = lax.ppermute(last, axis, up)
        after = lax.ppermute(first, axis, down)
        x = jnp.concatenate([before, x, after], axis=dim)
    return x


def layer_norm(inputs, gain_vector):
    centred = inputs - jnp.mean(inputs, axis=-1, keepdims=True)
    variance = jnp.mean(centred * centred, axis=-1, keepdims=True)
    return (centred * lax.rsqrt(variance + epsilon) * gain_vector).astype(jnp.bfloat16)


def to_windows(tensor, row_blocks, col_blocks):
    features = tensor.shape[-1]
    shaped = tensor.reshape(row_blocks, WIN, col_blocks, WIN, features)
    return shaped.transpose(0, 2, 1, 3, 4).reshape(row_blocks * col_blocks, WIN * WIN, features)


def from_windows(tensor, row_blocks, col_blocks):
    features = tensor.shape[-1]
    shaped = tensor.reshape(row_blocks, col_blocks, WIN, WIN, features)
    return shaped.transpose(0, 2, 1, 3, 4).reshape(row_blocks * WIN, col_blocks * WIN, features)


def window_attention(queries, keyval_win, key_valid):
    windows_count, window_cells, model_width = queries.shape
    head_size = model_width // HEADS
    query_heads = queries.reshape(windows_count, window_cells, HEADS, head_size)
    key_heads = keyval_win[..., :model_width].reshape(windows_count, window_cells, HEADS, head_size)
    value_heads = keyval_win[..., model_width:].reshape(
        windows_count, window_cells, HEADS, head_size
    )
    scores = jnp.einsum(
        "wqhd,wkhd->whqk", query_heads, key_heads, preferred_element_type=jnp.float32
    ) / math.sqrt(head_size)
    scores = jnp.where(key_valid[:, None, None, :], scores, -1e30)
    peak_score = jnp.max(scores, axis=-1, keepdims=True)
    weights = jnp.exp(scores - peak_score)
    weights = (weights / jnp.sum(weights, axis=-1, keepdims=True)).astype(jnp.bfloat16)
    mixed_out = jnp.einsum(
        "whqk,wkhd->wqhd", weights, value_heads, preferred_element_type=jnp.float32
    )
    return mixed_out.astype(jnp.bfloat16).reshape(windows_count, window_cells, model_width)


def zonal_basis(length, kept_waves):
    columns = jnp.arange(length, dtype=jnp.int32)
    wave_index = jnp.arange(kept_waves, dtype=jnp.int32)
    winding = columns[:, None] * wave_index[None, :] % length
    phases = winding.astype(jnp.float32) * (2.0 * math.pi / length)
    basis_table = jnp.concatenate([jnp.cos(phases), jnp.sin(phases)], axis=1)
    factor = jnp.where(wave_index == 0, 1.0, 2.0).astype(jnp.float32) / length
    return (basis_table, jnp.concatenate([factor, factor]))


def tendency(padded):
    centre = padded[:, 1:-1, 1:-1]
    east_cell = padded[:, 1:-1, 2:]
    west_cell = padded[:, 1:-1, :-2]
    north_cell = padded[:, 2:, 1:-1]
    south_cell = padded[:, :-2, 1:-1]
    field_shape = (VARS, LEV) + centre.shape[1:]
    wind_u = centre[:LEV][None]
    wind_v = centre[LEV : 2 * LEV][None]
    advection = wind_u * (east_cell - west_cell).reshape(field_shape) * 0.5
    advection = advection + wind_v * (north_cell - south_cell).reshape(field_shape) * 0.5
    spread_term = diffusion * (east_cell + west_cell + north_cell + south_cell - 4.0 * centre)
    return spread_term - advection.reshape(centre.shape)


def row_mask(padded, first_row, total_rows, depth):
    row_ids = first_row - depth + jnp.arange(padded.shape[1], dtype=jnp.int32)
    inside = ((row_ids >= 0) & (row_ids < total_rows)).astype(jnp.float32)
    return padded * inside[None, :, None]


def wrap_columns(padded, depth):
    return jnp.concatenate([padded[..., -depth:], padded, padded[..., :depth]], axis=2)


def advance(nudged, extend_one, first_row, total_rows):
    first_section = nudged + time_step * tendency(
        row_mask(extend_one(nudged), first_row, total_rows, 1)
    )
    second = tendency(row_mask(extend_one(first_section), first_row, total_rows, 1))
    return 0.5 * (nudged + first_section + time_step * second)


def decoded_coeffs(decoded_flat, patch_basis):
    channels_all = decoded_flat.shape[0] // (PATCH * PATCH)
    shaped = decoded_flat.reshape(
        channels_all, PATCH, PATCH, decoded_flat.shape[1], decoded_flat.shape[2]
    )
    result = jnp.einsum(
        "kabrc,bcw->kraw",
        shaped,
        patch_basis,
        precision=lax.Precision.HIGHEST,
        preferred_element_type=jnp.float32,
    )
    return result.reshape(-1, patch_basis.shape[2])


def body(tokens, ln_gain, w_query, w_keyval, w_out, w_dec, nudge, state):
    tok_rows, tok_cols, model_width = tokens.shape
    half_win = WIN // 2
    inputs = tokens.astype(jnp.float32)
    normed = layer_norm(inputs, ln_gain)
    flat_rows = normed.reshape(tok_rows * tok_cols, model_width)
    queries = jnp.dot(flat_rows, w_query, preferred_element_type=jnp.float32).astype(jnp.bfloat16)
    queries = queries.reshape(tok_rows, tok_cols, model_width)
    rim_tokens = padded_2(normed, (("lat", 0), ("lon", 1)), half_win, True)
    keyval = jnp.dot(
        rim_tokens.reshape(-1, model_width), w_keyval, preferred_element_type=jnp.float32
    ).astype(jnp.bfloat16)
    keyval = keyval.reshape(tok_rows + WIN, tok_cols + WIN, 2 * model_width)
    row_blocks = tok_rows // WIN + 1
    col_blocks = tok_cols // WIN + 1
    padded_queries = jnp.pad(queries, ((half_win, half_win), (half_win, half_win), (0, 0)))
    global_row = (
        lax.axis_index("lat") * tok_rows - half_win + jnp.arange(tok_rows + WIN, dtype=jnp.int32)
    )
    inside = ((global_row >= 0) & (global_row < tok_rows * lax.axis_size("lat"))).astype(jnp.int32)
    inside_grid = jnp.broadcast_to(inside[:, None, None], (tok_rows + WIN, tok_cols + WIN, 1))
    key_valid = to_windows(inside_grid, row_blocks, col_blocks)[..., 0] > 0
    attended = window_attention(
        to_windows(padded_queries, row_blocks, col_blocks),
        to_windows(keyval, row_blocks, col_blocks),
        key_valid,
    )
    attended = from_windows(attended, row_blocks, col_blocks)
    attended = attended[half_win : half_win + tok_rows, half_win : half_win + tok_cols]
    update = jnp.dot(attended.reshape(-1, model_width), w_out, preferred_element_type=jnp.float32)
    layer_out = (inputs.reshape(-1, model_width) + update).astype(jnp.bfloat16)
    decoded = jnp.einsum(
        "dm,rcd->mrc",
        w_dec,
        layer_out.reshape(tok_rows, tok_cols, model_width),
        preferred_element_type=jnp.float32,
    )
    basis_table, factor = zonal_basis(LON_PIX, KEEP)
    total_cols = LON_PIX // PATCH
    patch_basis = basis_table.reshape(total_cols, PATCH, 2 * KEEP).transpose(1, 0, 2)
    nudge_scale = nudge[:, None, None]
    band_dec, band_state = (
        lax.all_to_all(decoded, "lon", split_axis=1, concat_axis=2, tiled=True),
        lax.all_to_all(state, "lon", split_axis=1, concat_axis=2, tiled=True),
    )
    band_rows = band_state.shape[1]
    state_coeffs = jnp.dot(
        band_state.reshape(-1, band_state.shape[2]),
        basis_table,
        precision=lax.Precision.HIGHEST,
        preferred_element_type=jnp.float32,
    )
    coefficients = decoded_coeffs(band_dec, patch_basis) - state_coeffs
    filtered = jnp.dot(
        coefficients * factor,
        basis_table.T,
        precision=lax.Precision.HIGHEST,
        preferred_element_type=jnp.float32,
    )
    nudged = band_state + nudge_scale * filtered.reshape(band_state.shape)

    def extend_one(field):
        rows_added = padded_2(field.astype(jnp.bfloat16), ((("lat", "lon"), 1),), 1, False).astype(
            field.dtype
        )
        return wrap_columns(rows_added, 1)

    return advance(
        nudged,
        extend_one,
        lax.axis_index(("lat", "lon")) * band_rows,
        band_rows * lax.axis_size(("lat", "lon")),
    )


def solution(mesh):
    in_specs = (
        P(("member", "lat"), "lon", None),
        P(),
        P(),
        P(),
        P(),
        P(),
        P(),
        P(None, ("member", "lat"), "lon"),
    )
    out_specs = P(None, ("member", "lat", "lon"), None)
    return jax.shard_map(body, mesh=mesh, in_specs=in_specs, out_specs=out_specs, check_vma=False)
```

profile of v0, /device:TPU:15, one launch (start us, length us, event | category | flops | bytes accessed | tf_op | source)
XLA Modules:
  0.0 216.8 jit_solution(11118138513977932381)
XLA Ops:
  0.0 1.8 convert_reduce_fusion
  3.2 1.1 copy-done.2
  4.3 1.3 fusion.67
  5.6 1.2 collective-permute-start
  7.1 2.1 copy.49
  9.1 6.0 %all-to-all-start = ((f32[32,32,384]{2,0,1:T(8,128)}), f32[32,32,384]{2,0,1:T(8,128)}, u32[]{:S(2)}, u32[]{:S(2)}) async-start(f32[32,32,384]{2,0,1:T(8,128)} %copy.49), calls=%async_computation | async-start | bytes 3145728 | tf_op jit(solution)/shard_map/all_to_all | solution.py:175
  15.2 4.2 %fusion.43 = (f32[768,256]{1,0:T(8,128)S(1)}, f32[768,256]{1,0:T(8,128)}) fusion(), kind=kLoop, calls=%fused_computation.70 | loop fusion | flops 1769472 | bytes 1572864 | tf_op jit(solution)/shard_map/sin | solution.py:79
  19.3 4.6 %fusion.48 = (f32[192,4,256]{2,0,1:T(8,128)}, f32[192,4,256]{2,0,1:T(8,128)}) fusion(s32[192,4]{0,1:T(4,128)S(1)} %multiply_add_fusion.1), kind=kLoop, calls=%fused_computation.76 | loop fusion | flops 1769472 | bytes 1575936 | tf_op jit(solution)/shard_map/cos | solution.py:79
  23.9 4.5 %convolution_convert_fusion.2 = bf16[768,1024]{1,0:T(8,128)(2,1)} fusion(bf16[768,1024]{1,0:T(8,128)(2,1)} %bitcast.98, bf16[1024,1024]{1,0:T(8,128)(2,1)S(1)} %copy-done), kind=kOutput, calls=%fused_computation.25 | convolution fusion | flops 1611399168 | bytes 5242880 | tf_op jit(solution)/shard_map/dot_general | solution.py:138
  28.4 12.7 %collective-permute-done = bf16[4,96,1024]{2,1,0:T(8,128)(2,1)} collective-permute-done((bf16[4,96,1024]{2,1,0:T(8,128)(2,1)}, bf16[4,96,1024]{2,1,0:T(8,128)(2,1)}, u32[]{:S(2)}, u32[]{:S(2)}) %collective-permute-start) | collective-permute-done | bytes 786464 | tf_op jit(solution)/shard_map/ppermute | solution.py:29
  41.2 1.0 pad_maximum_fusion.6
  42.2 1.6 collective-permute-start.2
  44.6 2.1 copy.53
  46.7 9.6 %reshape_reshape.10 = bf16[26,64,16,64]{3,2,1,0:T(8,128)(2,1)} reshape(bf16[2,13,8,8,1024]{4,3,2,1,0:T(8,128)(2,1)} %copy.53) | data formatting | bytes 6815744 | tf_op jit(solution)/shard_map/reshape;reshape | solution.py:56
  56.5 2.6 %copy.85 = f32[32,2,16,384]{3,1,2,0:T(2,128)S(1)} copy(f32[32,2,16,384]{3,0,2,1:T(8,128)} %bitcast) | data formatting | bytes 3145728 | tf_op jit(solution)/shard_map/all_to_all | solution.py:175
  59.1 1.1 copy-done.7
  60.3 1.3 copy.66
  61.5 3.5 %all_to_all.27 = f32[32,16,768]{2,1,0:T(8,128)} reshape(f32[32,16,2,384]{3,2,1,0:T(2,128)} %bitcast.100) | data formatting | bytes 3145728 | tf_op jit(solution)/shard_map/all_to_all | solution.py:175
  65.0 3.2 %pad_maximum_fusion = bf16[16,104,1024]{2,1,0:T(8,128)(2,1)S(1)} fusion(bf16[16,4,1024]{2,1,0:T(4,128)(2,1)S(1)} %collective-permute-done.3, bf16[4,96,1024]{2,1,0:T(8,128)(2,1)} %collective-permute-done.1, bf16[8,96,1024]{2,1,0:T(8,128)(2,1)S(1)} %copy-done.4, bf16[4,96,1024]{2,1,0:T(8,128)(2,1)} %collective-permute-done, ...), kind=kLoop, calls=%fused_computation.15 | loop fusion | flops 17039360 | bytes 6815744 | tf_op jit(solution)/shard_map/concatenate | solution.py:31
  68.3 9.8 %convolution_convert_fusion = bf16[1664,2048]{1,0:T(8,128)(2,1)} fusion(bf16[1664,1024]{1,0:T(8,128)(2,1)S(1)} %bitcast.110, bf16[1024,2048]{1,0:T(8,128)(2,1)S(1)} %copy-done.14), kind=kOutput, calls=%fused_computation.5 | convolution fusion | flops 6982729728 | bytes 14417920 | tf_op jit(solution)/shard_map/dot_general | solution.py:141
  78.0 3.8 %copy.51 = bf16[2,8,13,8,2048]{4,3,1,2,0:T(8,128)(2,1)S(1)} copy(bf16[2,8,13,8,2048]{4,3,2,1,0:T(8,128)(2,1)} %bitcast.106) | data formatting | bytes 13631488 | tf_op jit(solution)/shard_map/reshape;reshape | solution.py:43
  81.8 3.6 %fusion.61 = (bf16[26,64,1024]{2,1,0:T(8,128)(2,1)}, bf16[26,64,1024]{2,1,0:T(8,128)(2,1)}) fusion(bf16[26,64,2048]{2,1,0:T(8,128)(2,1)S(1)} %bitcast.97), kind=kLoop, calls=%fused_computation.99 | loop fusion | bytes 13631488 | tf_op jit(solution)/shard_map/slice | solution.py:57
  85.4 9.6 %reshape.135 = bf16[26,64,16,64]{3,2,1,0:T(8,128)(2,1)} reshape(bf16[26,64,1024]{2,1,0:T(8,128)(2,1)} %get-tuple-element.9) | data formatting | bytes 6815744 | tf_op jit(solution)/shard_map/reshape | solution.py:57
  95.0 7.3 %copy.52 = bf16[26,64,1024]{1,2,0:T(8,128)(2,1)} copy(bf16[26,64,1024]{2,1,0:T(8,128)(2,1)} %get-tuple-element.10) | data formatting | bytes 6815744 | tf_op jit(solution)/shard_map/slice | solution.py:58
  102.4 13.4 %fusion.70 = (f32[26,16,64]{2,1,0:T(8,128)S(1)}, f32[26,16,64,64]{2,3,1,0:T(8,128)}) fusion(pred[26,64]{1,0:T(8,128)(4,1)S(1)} %gt.13, bf16[26,64,16,64]{3,2,1,0:T(8,128)(2,1)} %reshape.135, bf16[26,64,16,64]{3,2,1,0:T(8,128)(2,1)} %reshape_reshape.10), kind=kOutput, calls=%fused_computation.108 | convolution fusion | flops 224919616 | bytes 13739648 | tf_op jit(solution)/shard_map/sub | solution.py:66
  115.7 11.5 %fusion.9 = bf16[26,64,16,64]{1,3,2,0:T(8,128)(2,1)} fusion(bf16[26,64,16,64]{1,3,2,0:T(8,128)(2,1)} %bitcast.105, f32[26,16,64,64]{2,3,1,0:T(8,128)} %get-tuple-element.32, f32[26,16,64]{2,1,0:T(8,128)S(1)} %get-tuple-element.31), kind=kOutput, calls=%fused_computation.14 | convolution fusion | flops 223215616 | bytes 13737984 | tf_op jit(solution)/shard_map/whqk,wkhd->wqhd/dot_general | solution.py:68
  127.2 10.5 %copy.57 = bf16[26,64,16,64]{3,2,1,0:T(8,128)(2,1)} copy(bf16[26,64,16,64]{1,3,2,0:T(8,128)(2,1)} %fusion.9) | data formatting | bytes 6815744 | tf_op jit(solution)/shard_map/convert_element_type | solution.py:71
  137.7 9.9 %reshape_reshape.11 = bf16[2,13,8,8,1024]{4,3,2,1,0:T(8,128)(2,1)} reshape(bf16[26,64,16,64]{3,2,1,0:T(8,128)(2,1)} %copy.57) | data formatting | bytes 6815744 | tf_op jit(solution)/shard_map/reshape;reshape | solution.py:49
  147.6 2.5 %copy.58 = bf16[2,8,13,8,1024]{4,3,2,1,0:T(8,128)(2,1)S(1)} copy(bf16[2,8,13,8,1024]{4,3,1,2,0:T(8,128)(2,1)} %bitcast.101) | data formatting | bytes 6815744 | tf_op jit(solution)/shard_map/transpose | solution.py:50
  150.5 1.0 copy-done.6
  151.5 1.8 fusion.10
  153.3 1.0 convolution_bitcast_fusion
  154.3 5.9 %all_to_all.33 = f32[512,8,96]{0,2,1:T(8,128)} all-to-all(f32[512,8,96]{0,2,1:T(8,128)S(1)} %convolution_bitcast_fusion), channel_id=1, replica_groups=mesh['member'=2,'lat'=8,'lon'=2] {'lon'}, dimensions={1} | all-to-all | bytes 3145728 | tf_op jit(solution)/shard_map/all_to_all | solution.py:174
  160.2 3.1 %copy.59 = f32[512,2,4,96]{3,1,2,0:T(2,128)S(1)} copy(f32[512,2,4,96]{0,3,2,1:T(8,128)} %bitcast.107) | data formatting | bytes 3145728 | tf_op jit(solution)/shard_map/all_to_all | solution.py:174
  163.3 2.8 %reshape.139 = f32[32,4,4,4,192]{4,3,2,1,0:T(4,128)} reshape(f32[512,4,2,96]{3,2,1,0:T(2,128)S(1)} %bitcast.103) | data formatting | bytes 3145728 | tf_op jit(solution)/shard_map/reshape | solution.py:119
  166.1 5.8 %fusion.30 = f32[32,4,4,512]{3,0,1,2:T(8,128)S(1)} fusion(f32[32,4,4,4,192]{4,3,2,1,0:T(4,128)} %reshape.139, f32[192,4,256]{2,0,1:T(8,128)} %get-tuple-element.30, f32[192,4,256]{2,0,1:T(8,128)} %get-tuple-element.29), kind=kOutput, calls=%fused_computation.53 | convolution fusion | flops 2416312320 | bytes 4194304 | tf_op jit(solution)/shard_map/kabrc,bcw->kraw/dot_general | solution.py:122
  172.6 1.3 reshape.140
  173.9 1.6 copy.62
  175.5 6.5 %fusion.34 = f32[512,512]{0,1:T(8,128)S(1)} fusion(f32[512,512]{0,1:T(8,128)S(1)} %copy.62, f32[512,768]{1,0:T(8,128)} %bitcast.108, f32[768,256]{1,0:T(8,128)S(1)} %get-tuple-element.33, f32[768,256]{1,0:T(8,128)S(1)} %copy-done.8, f32[512]{0:T(512)S(1)} %pad_maximum_fusion.7), kind=kOutput, calls=%fused_computation.56 | convolution fusion | flops 2416836608 | bytes 5244928 | tf_op jit(solution)/shard_map/dot_general | solution.py:178
  182.1 5.4 %fusion.35 = f32[512,768]{1,0:T(8,128)S(1)} fusion(f32[512,512]{0,1:T(8,128)S(1)} %fusion.34, f32[768,256]{1,0:T(8,128)S(1)} %get-tuple-element.33, f32[768,256]{1,0:T(8,128)S(1)} %copy-done.8), kind=kOutput, calls=%fused_computation.57 | convolution fusion | flops 2416312320 | bytes 4194304 | tf_op jit(solution)/shard_map/dot_general | solution.py:185
  187.9 4.3 %collective-permute-start.4 = (bf16[32,1,768]{2,1,0:T(2,128)(2,1)S(1)}, bf16[32,1,768]{2,1,0:T(2,128)(2,1)S(1)}, u32[]{:S(2)}, u32[]{:S(2)}) collective-permute-start(bf16[32,1,768]{2,1,0:T(2,128)(2,1)S(1)} %get-tuple-element.27), channel_id=1, source_target_pairs={{0,1},{1,2},{2,3},{3,4},{4,5},{5,6},{6,7},{7,8},{8,9},{9,10},{10,1... | collective-permute-start | bytes 147464 | tf_op jit(solution)/shard_map/ppermute | solution.py:29
  192.2 1.9 collective-permute-start.5
  194.2 4.9 %collective-permute-done.5 = bf16[32,1,768]{2,1,0:T(2,128)(2,1)S(1)} collective-permute-done((bf16[32,1,768]{2,1,0:T(2,128)(2,1)S(1)}, bf16[32,1,768]{2,1,0:T(2,128)(2,1)S(1)}, u32[]{:S(2)}, u32[]{:S(2)}) %collective-permute-start.5) | collective-permute-done | bytes 49184 | tf_op jit(solution)/shard_map/ppermute | solution.py:30
  201.0 1.8 fusion.58
  203.0 1.9 collective-permute-start.6
  204.9 2.4 %collective-permute-start.7 = (bf16[32,1,768]{2,1,0:T(2,128)(2,1)S(1)}, bf16[32,1,768]{2,1,0:T(2,128)(2,1)S(1)}, u32[]{:S(2)}, u32[]{:S(2)}) collective-permute-start(bf16[32,1,768]{2,1,0:T(2,128)(2,1)S(1)} %get-tuple-element.26), channel_id=1, source_target_pairs={{1,0},{2,1},{3,2},{4,3},{5,4},{6,5},{7,6},{8,7},{9,8},{10,9},{11,1... | collective-permute-start | bytes 147464 | tf_op jit(solution)/shard_map/ppermute | solution.py:30
  207.3 4.4 %collective-permute-done.7 = bf16[32,1,768]{2,1,0:T(2,128)(2,1)S(1)} collective-permute-done((bf16[32,1,768]{2,1,0:T(2,128)(2,1)S(1)}, bf16[32,1,768]{2,1,0:T(2,128)(2,1)S(1)}, u32[]{:S(2)}, u32[]{:S(2)}) %collective-permute-start.7) | collective-permute-done | bytes 49184 | tf_op jit(solution)/shard_map/ppermute | solution.py:30
  213.6 3.0 %fusion.18 = f32[32,16,768]{2,1,0:T(8,128)} fusion(f32[32,18,770]{2,1,0:T(8,128)S(1)} %maximum_multiply_fusion.1, f32[32,16,768]{2,1,0:T(8,128)S(1)} %get-tuple-element.8, f32[32,16,768]{2,1,0:T(8,128)S(1)} %get-tuple-element.6, f32[8,16,768]{2,1,0:T(8,128)S(1)} %get-tuple-element.14, f32[8,16,768]{2,1,0:T(8,128)S(1)} %get-tuple-element.13), kind=kLoop, calls=%fused_computation.32 | loop fusion | flops 6684672 | bytes 13369344 | tf_op jit(solution)/shard_map/mul | solution.py:114
  (64 shorter events, 7.9 us)
Async XLA Ops:
  0.0 23.9 %copy-start = (bf16[1024,1024]{1,0:T(8,128)(2,1)S(1)}, bf16[1024,1024]{1,0:T(8,128)(2,1)}, u32[]{:S(2)}) copy-start(bf16[1024,1024]{1,0:T(8,128)(2,1)} %param.10) | copy-start | bytes 6291460
  0.0 2.0 copy-start.5
  0.0 2.6 %copy-start.12 = (f32[1024]{0:T(1024)S(1)}, f32[1024]{0:T(1024)}, u32[]{:S(2)}) copy-start(f32[1024]{0:T(1024)} %param.9) | copy-start | bytes 12292
  3.2 1.2 copy-start.2
  4.3 2.7 %copy-start.11 = (f32[32,32,384]{2,1,0:T(8,128)S(1)}, f32[32,32,384]{2,1,0:T(8,128)}, u32[]{:S(2)}) copy-start(f32[32,32,384]{2,1,0:T(8,128)} %param.15) | copy-start | bytes 4718596
  5.6 35.6 %collective-permute-start = (bf16[4,96,1024]{2,1,0:T(8,128)(2,1)}, bf16[4,96,1024]{2,1,0:T(8,128)(2,1)}, u32[]{:S(2)}, u32[]{:S(2)}) collective-permute-start(bf16[4,96,1024]{2,1,0:T(8,128)(2,1)} %get-tuple-element.23), channel_id=1, source_target_pairs={{0,2},{2,4},{4,6},{6,8},{8,10},{10,12},{12,14},{14,0},{1,3},{3,5},... | collective-permute-start | bytes 2359304 | tf_op jit(solution)/shard_map/ppermute | solution.py:29
  6.8 34.3 %collective-permute-start.1 = (bf16[4,96,1024]{2,1,0:T(8,128)(2,1)}, bf16[4,96,1024]{2,1,0:T(8,128)(2,1)}, u32[]{:S(2)}, u32[]{:S(2)}) collective-permute-start(bf16[4,96,1024]{2,1,0:T(8,128)(2,1)} %get-tuple-element.24), channel_id=1, source_target_pairs={{2,0},{4,2},{6,4},{8,6},{10,8},{12,10},{14,12},{0,14},{3,1},{5,3},... | collective-permute-start | bytes 2359304 | tf_op jit(solution)/shard_map/ppermute | solution.py:30
  9.1 47.4 %all-to-all-start = ((f32[32,32,384]{2,0,1:T(8,128)}), f32[32,32,384]{2,0,1:T(8,128)}, u32[]{:S(2)}, u32[]{:S(2)}) async-start(f32[32,32,384]{2,0,1:T(8,128)} %copy.49), calls=%async_computation | async-start | bytes 3145728 | tf_op jit(solution)/shard_map/all_to_all | solution.py:175
  23.9 17.2 %copy-start.3 = (bf16[8,96,1024]{2,1,0:T(8,128)(2,1)S(1)}, bf16[8,96,1024]{2,1,0:T(8,128)(2,1)}, u32[]{:S(2)}) copy-start(bf16[8,96,1024]{2,1,0:T(8,128)(2,1)} %copy-done.2) | copy-start | bytes 4718596
  28.4 15.5 %copy-start.10 = (bf16[768,1024]{1,0:T(8,128)(2,1)S(1)}, bf16[768,1024]{1,0:T(8,128)(2,1)}, u32[]{:S(2)}) copy-start(bf16[768,1024]{1,0:T(8,128)(2,1)} %convolution_convert_fusion.2) | copy-start | bytes 4718596
  42.2 22.8 %collective-permute-start.2 = (bf16[16,4,1024]{2,1,0:T(4,128)(2,1)S(1)}, bf16[16,4,1024]{2,1,0:T(4,128)(2,1)S(1)}, u32[]{:S(2)}, u32[]{:S(2)}) collective-permute-start(bf16[16,4,1024]{2,1,0:T(4,128)(2,1)S(1)} %get-tuple-element.11), channel_id=1, source_target_pairs={{0,1},{1,0},{2,3},{3,2},{4,5},{5,4},{6,7},{7,6},{8,9},{9,8},{10,11... | collective-permute-start | bytes 393224 | tf_op jit(solution)/shard_map/ppermute | solution.py:29
  43.8 21.2 %collective-permute-start.3 = (bf16[16,4,1024]{2,1,0:T(4,128)(2,1)S(1)}, bf16[16,4,1024]{2,1,0:T(4,128)(2,1)S(1)}, u32[]{:S(2)}, u32[]{:S(2)}) collective-permute-start(bf16[16,4,1024]{2,1,0:T(4,128)(2,1)S(1)} %get-tuple-element.12), channel_id=1, source_target_pairs={{1,0},{0,1},{3,2},{2,3},{5,4},{4,5},{7,6},{6,7},{9,8},{8,9},{11,10... | collective-permute-start | bytes 393224 | tf_op jit(solution)/shard_map/ppermute | solution.py:30
  59.1 1.1 copy-start.7
  61.5 3.5 %copy-start.4 = (bf16[8,96,1024]{2,1,0:T(8,128)(2,1)S(1)}, bf16[8,96,1024]{2,1,0:T(8,128)(2,1)}, u32[]{:S(2)}) copy-start(bf16[8,96,1024]{2,1,0:T(8,128)(2,1)} %copy-done.2) | copy-start | bytes 4718596
  65.0 3.2 %copy-start.14 = (bf16[1024,2048]{1,0:T(8,128)(2,1)S(1)}, bf16[1024,2048]{1,0:T(8,128)(2,1)}, u32[]{:S(2)}) copy-start(bf16[1024,2048]{1,0:T(8,128)(2,1)} %param.11) | copy-start | bytes 12582916
  147.6 2.9 %copy-start.15 = (bf16[1024,1024]{1,0:T(8,128)(2,1)S(1)}, bf16[1024,1024]{1,0:T(8,128)(2,1)}, u32[]{:S(2)}) copy-start(bf16[1024,1024]{1,0:T(8,128)(2,1)} %param.12) | copy-start | bytes 6291460
  150.0 1.4 copy-start.6
  151.5 1.8 copy-start.16
  172.6 2.9 %copy-start.8 = (f32[768,256]{1,0:T(8,128)S(1)}, f32[768,256]{1,0:T(8,128)}, u32[]{:S(2)}) copy-start(f32[768,256]{1,0:T(8,128)} %get-tuple-element.34) | copy-start | bytes 2359300
  182.1 5.4 %copy-start.9 = (f32[32,16,768]{2,1,0:T(8,128)S(1)}, f32[32,16,768]{2,1,0:T(8,128)}, u32[]{:S(2)}) copy-start(f32[32,16,768]{2,1,0:T(8,128)} %all_to_all.27) | copy-start | bytes 4718596
  182.1 5.4 %copy-start.13 = (f32[32]{0:T(128)S(1)}, f32[32]{0:T(128)}, u32[]{:S(2)}) copy-start(f32[32]{0:T(128)} %param.14) | copy-start | bytes 388
  187.9 6.3 %collective-permute-start.4 = (bf16[32,1,768]{2,1,0:T(2,128)(2,1)S(1)}, bf16[32,1,768]{2,1,0:T(2,128)(2,1)S(1)}, u32[]{:S(2)}, u32[]{:S(2)}) collective-permute-start(bf16[32,1,768]{2,1,0:T(2,128)(2,1)S(1)} %get-tuple-element.27), channel_id=1, source_target_pairs={{0,1},{1,2},{2,3},{3,4},{4,5},{5,6},{6,7},{7,8},{8,9},{9,10},{10,1... | collective-permute-start | bytes 147464 | tf_op jit(solution)/shard_map/ppermute | solution.py:29
  192.2 6.8 %collective-permute-start.5 = (bf16[32,1,768]{2,1,0:T(2,128)(2,1)S(1)}, bf16[32,1,768]{2,1,0:T(2,128)(2,1)S(1)}, u32[]{:S(2)}, u32[]{:S(2)}) collective-permute-start(bf16[32,1,768]{2,1,0:T(2,128)(2,1)S(1)} %get-tuple-element.28), channel_id=1, source_target_pairs={{1,0},{2,1},{3,2},{4,3},{5,4},{6,5},{7,6},{8,7},{9,8},{10,9},{11,1... | collective-permute-start | bytes 147464 | tf_op jit(solution)/shard_map/ppermute | solution.py:30
  203.0 4.3 %collective-permute-start.6 = (bf16[32,1,768]{2,1,0:T(2,128)(2,1)S(1)}, bf16[32,1,768]{2,1,0:T(2,128)(2,1)S(1)}, u32[]{:S(2)}, u32[]{:S(2)}) collective-permute-start(bf16[32,1,768]{2,1,0:T(2,128)(2,1)S(1)} %get-tuple-element.25), channel_id=1, source_target_pairs={{0,1},{1,2},{2,3},{3,4},{4,5},{5,6},{6,7},{7,8},{8,9},{9,10},{10,1... | collective-permute-start | bytes 147464 | tf_op jit(solution)/shard_map/ppermute | solution.py:29
  204.9 6.8 %collective-permute-start.7 = (bf16[32,1,768]{2,1,0:T(2,128)(2,1)S(1)}, bf16[32,1,768]{2,1,0:T(2,128)(2,1)S(1)}, u32[]{:S(2)}, u32[]{:S(2)}) collective-permute-start(bf16[32,1,768]{2,1,0:T(2,128)(2,1)S(1)} %get-tuple-element.26), channel_id=1, source_target_pairs={{1,0},{2,1},{3,2},{4,3},{5,4},{6,5},{7,6},{8,7},{9,8},{10,9},{11,1... | collective-permute-start | bytes 147464 | tf_op jit(solution)/shard_map/ppermute | solution.py:30
  213.6 3.0 %copy-start.1 = (bf16[1024,1024]{1,0:T(8,128)(2,1)S(1)}, bf16[1024,1024]{1,0:T(8,128)(2,1)}, u32[]{:S(2)}) copy-start(bf16[1024,1024]{1,0:T(8,128)(2,1)} %param.10) | copy-start | bytes 6291460
where the time goes:
time: 221 us; the launch traced here: 217 us
  local copies, waits for them, and re-layouts  85 us (38%)
  matrix products  59.7 us (27%)
  other arithmetic  23.8 us (11%)
  waiting for transfers between devices  22 us (10%)
  starting transfers between devices  19.8 us (9%)
  blocking collectives  5.9 us (3%)
    sub x1, matrix products, window_attention(): weights = jnp.exp(scores - peak_score)  13.4 us
    ppermute x4, waiting for transfers between devices, padded_2(): before = lax.ppermute(last, axis, up)  12.7 us
    dot_general x1, matrix products, window_attention(): jnp.einsum('whqk,wkhd->wqhd', weights, value_heads, preferred_element_typ...  11.5 us
    convert_element_type x1, local copies, waits for them, and re-layouts, window_attention(): mixed_out.astype(jnp.bfloat16)  10.5 us
    another operation x1, local copies, waits for them, and re-layouts, from_windows(): shaped = tensor.reshape(row_blocks, col_blocks, WIN, WIN, features)  9.87 us
    dot_general x1, matrix products, body(): jnp.dot(rim_tokens.reshape(-1, model_width), w_keyval, preferred_element_...  9.76 us
    reshape x1, local copies, waits for them, and re-layouts, window_attention(): keyval_win[..., :model_width]  9.63 us
    another operation x1, local copies, waits for them, and re-layouts, window_attention(): query_heads = queries.reshape(windows_count, window_cells, HEADS, head_size)  9.6 us
  transfers between devices with their start and end apart: 9, of which 3 were waited for; matrix products, arithmetic and copies ran while one was open for 15% of the time, Pallas kernels for 0%

commit v1 on v0

v1 whole, which is shorter than its diff:
```python
import functools
import math

import jax
import jax.numpy as jnp
import ml_dtypes
import numpy as np
from jax import lax
from jax.experimental import pallas as pl
from jax.experimental.pallas import tpu as pltpu
from jax.sharding import PartitionSpec as P

HEADS = 16
WIN = 8
PATCH = 4
VARS = 4
LEV = 8
KEEP = 256

time_step = 0.1
diffusion = 0.5
epsilon = 1e-05
HALF = WIN // 2
GROUP = 4
MIB = 1 << 20
F32 = jnp.float32
BF16 = jnp.bfloat16


def zonal_filter(length, kept_waves):
    lag = np.arange(length, dtype=np.float64)
    waves = np.arange(1, kept_waves, dtype=np.float64)
    kernel = 1.0 + 2.0 * np.cos(2.0 * np.pi / length * lag[:, None] * waves[None, :]).sum(1)
    at = (np.arange(length)[:, None] - np.arange(length)[None, :]) % length
    return (kernel / length)[at]


def split_high_low(matrix):
    high = matrix.astype(ml_dtypes.bfloat16)
    low = (matrix - high.astype(np.float64)).astype(ml_dtypes.bfloat16)
    return high, low


def decoded_order(total_cols, parts):
    cols = total_cols // parts
    group_cols = GROUP * WIN
    rows = []
    for part in range(parts):
        lanes = []
        for group in range(cols // group_cols):
            for b in range(PATCH):
                for place in range(group_cols):
                    col = part * cols + group * group_cols + place
                    if place % WIN < HALF:
                        col += WIN
                    lanes.append((col % total_cols) * PATCH + b)
        rows.append(lanes)
    return np.array(rows)


def dot(a, b):
    return lax.dot_general(a, b, (((1,), (0,)), ((), ())), preferred_element_type=F32)


def dot_nt(a, b):
    return lax.dot_general(a, b, (((1,), (1,)), ((), ())), preferred_element_type=F32)


def window_tokens(load, load_next, cols, emit):
    lead = lax.broadcasted_iota(jnp.int32, (2 * WIN, 1), 0) % WIN < HALF
    pairs = cols // (2 * WIN)
    for pair in range(pairs):
        for duo in range(HALF // 2):
            rows = []
            for r in (2 * duo, 2 * duo + 1):
                here = load(r, pair * 2 * WIN).astype(F32)
                if pair + 1 < pairs:
                    after = load(r, (pair + 1) * 2 * WIN).astype(F32)[:WIN]
                else:
                    after = load_next(r).astype(F32)
                shifted = jnp.concatenate([here[WIN:], after], axis=0)
                rows.append(jnp.where(lead, shifted, here))
            for side in range(2):
                part = slice(side * WIN, (side + 1) * WIN)
                emit(2 * pair + side, duo, jnp.concatenate([rows[0][part], rows[1][part]], axis=0))


def normalise(block, gain):
    centred = block - jnp.mean(block, axis=-1, keepdims=True)
    variance = jnp.mean(centred * centred, axis=-1, keepdims=True)
    return (centred * lax.rsqrt(variance + epsilon) * gain).astype(BF16)


def place_tokens(load, load_next, cols, gain, raw_ref, normed_ref):
    def emit(window, duo, block):
        at = window * WIN * HALF + duo * 2 * WIN
        raw_ref[at : at + 2 * WIN, :] = block.astype(BF16)
        normed_ref[at : at + 2 * WIN, :] = normalise(block, gain)

    window_tokens(load, load_next, cols, emit)


def project(normed_ref, wq_ref, wkv_ref, qkv_ref):
    width = wq_ref.shape[0]
    normed = normed_ref[...]
    qkv_ref[:, :width] = dot(normed, wq_ref[...]).astype(BF16)
    qkv_ref[:, width : 2 * width] = dot(normed, wkv_ref[:, :width]).astype(BF16)
    qkv_ref[:, 2 * width :] = dot(normed, wkv_ref[:, width:]).astype(BF16)


def own_kernel(where_ref, tok_ref, next_ref, gain_ref, wq_ref, wkv_ref, raw_ref, qkv_ref, normed_ref):
    first = HALF * where_ref[0]
    place_tokens(
        lambda r, c: tok_ref[first + r, c : c + 2 * WIN, :],
        lambda r: next_ref[r],
        tok_ref.shape[1],
        gain_ref[...],
        raw_ref,
        normed_ref,
    )
    project(normed_ref, wq_ref, wkv_ref, qkv_ref)


def main_kernel(
    where_ref,
    x_ref,
    next_ref,
    gain_ref,
    raw_own_ref,
    qkv_own_ref,
    wq_ref,
    wkv_ref,
    wout_ref,
    wdec_ref,
    keep_ref,
    send_ref,
    raw_ref,
    normed_ref,
    qkv_ref,
    prob_ref,
    att_ref,
):
    cols, width = x_ref.shape[1:]
    head_size = width // HEADS
    half_cells = HALF * WIN
    cells = 2 * half_cells
    lanes = 4 * head_size
    place_tokens(
        lambda r, c: x_ref[r, c : c + 2 * WIN, :],
        lambda r: next_ref[r],
        cols,
        gain_ref[...],
        raw_ref,
        normed_ref,
    )
    project(normed_ref, wq_ref, wkv_ref, qkv_ref)

    def iota(shape, dim):
        return lax.broadcasted_iota(jnp.int32, shape, dim)

    blocks = (iota((lanes, lanes), 0) // head_size == iota((lanes, lanes), 1) // head_size).astype(F32).astype(BF16)
    split_rows = iota((cells, 2 * cells), 0) // half_cells != iota((cells, 2 * cells), 1) % cells // half_cells
    bias = jnp.where(split_rows & (where_ref[1] > 0), -1e30, 0.0)
    first_head = iota((cells, 2 * cells), 1) < cells
    scale = 1.0 / math.sqrt(head_size)
    token_rows = GROUP * WIN

    def one_group(group, _):
        for quad in range(HEADS // 4):
            at = quad * lanes

            def part(window, offset):
                rows = pl.ds(pl.multiple_of((group * GROUP + window) * half_cells, half_cells), half_cells)
                columns = slice(offset + at, offset + at + lanes)
                return jnp.concatenate([qkv_own_ref[rows, columns], qkv_ref[rows, columns]], axis=0)

            for window in range(GROUP):
                keys = jnp.concatenate([part(window, width)] * 4, axis=0) * blocks
                scores = dot_nt(part(window, 0), keys)
                for side in range(2):
                    two = scores[:, side * 2 * cells : (side + 1) * 2 * cells] + bias
                    left = jnp.max(jnp.where(first_head, two, -jnp.inf), axis=-1, keepdims=True)
                    right = jnp.max(jnp.where(first_head, -jnp.inf, two), axis=-1, keepdims=True)
                    peak = jnp.where(first_head, left, right)
                    prob_ref[window * cells : (window + 1) * cells, side * 2 * cells : (side + 1) * 2 * cells] = jnp.exp(
                        (two - peak) * scale
                    ).astype(BF16)
            sums = dot(prob_ref[...], blocks)
            for window in range(GROUP):
                values = jnp.concatenate([part(window, 2 * width)] * 4, axis=0) * blocks
                rows = slice(window * cells, (window + 1) * cells)
                att_ref[rows, at : at + lanes] = (dot(prob_ref[rows, :], values) / sums[rows]).astype(BF16)
        update = dot(att_ref[...], wout_ref[...])
        pieces = []
        for half in range(2):
            for r in range(HALF):
                for window in range(GROUP):
                    inside = half * half_cells + r * WIN
                    pieces.append((window, inside))
        raws = []
        for window in range(GROUP):
            rows = pl.ds(pl.multiple_of((group * GROUP + window) * half_cells, half_cells), half_cells)
            raws.append(
                jnp.concatenate([raw_own_ref[rows, :].astype(F32), raw_ref[rows, :].astype(F32)], axis=0)
            )
        layer_out = jnp.concatenate(
            [
                raws[w][i : i + WIN] + update[w * cells + i : w * cells + i + WIN]
                for w, i in pieces
            ],
            axis=0,
        ).astype(BF16)
        decoded = dot_nt(wdec_ref[...], layer_out)
        band = decoded.shape[0] // PATCH
        lane_part = iota((band, HALF * token_rows), 1) // token_rows
        out_lanes = pl.ds(pl.multiple_of(group * (PATCH * token_rows), PATCH * token_rows), PATCH * token_rows)
        for half, out_ref in ((0, keep_ref), (1, send_ref)):
            from_b = [
                decoded[b * band : (b + 1) * band, half * HALF * token_rows : (half + 1) * HALF * token_rows]
                for b in range(PATCH)
            ]
            for r in range(HALF):
                total = None
                for b in range(PATCH):
                    moved = from_b[b]
                    if b != r:
                        moved = pltpu.roll(moved, (b - r) % PATCH * token_rows, axis=1)
                    total = moved if total is None else jnp.where(lane_part == b, moved, total)
                out_ref[r * band : (r + 1) * band, out_lanes] = total.astype(BF16)
        return 0

    lax.fori_loop(0, cols // token_rows, one_group, 0)


def state_kernel(where_ref, state_ref, got_ref, nudge_ref, high_ref, low_ref, out_ref, whole_ref):
    lon = where_ref[0]
    channels, own_rows, cols = got_ref.shape
    own_lanes = pl.ds(pl.multiple_of(lon * cols, 128), cols)
    got_lanes = pl.ds(pl.multiple_of((1 - lon) * cols, 128), cols)
    for y in range(0, own_rows, 8):
        own_part = pl.ds(pl.multiple_of(lon * own_rows + y, 8), 8)
        for ch in range(0, channels, 8):
            own = jnp.swapaxes(state_ref[ch : ch + 8, own_part, :], 0, 1)
            got = jnp.swapaxes(got_ref[ch : ch + 8, y : y + 8, :], 0, 1)
            for i in range(8):
                rows = slice((y + i) * channels + ch, (y + i) * channels + ch + 8)
                whole_ref[rows, own_lanes] = own[i]
                whole_ref[rows, got_lanes] = got[i]
    step = nudge_ref.shape[0]
    for at in range(0, out_ref.shape[0], step):
        field = whole_ref[at : at + step, :]
        high = field.astype(BF16)
        low = (field - high.astype(F32)).astype(BF16)
        smooth = dot(high, high_ref[...]) + (dot(high, low_ref[...]) + dot(low, high_ref[...]))
        out_ref[at : at + step, :] = field - nudge_ref[...] * smooth


def filter_kernel(where_ref, base_ref, keep_ref, got_ref, nudge_ref, high_ref, low_ref, out_ref, lon_ref, lat_ref):
    lon = where_ref[0]
    keep, got = keep_ref[...], got_ref[...]
    smooth = dot(keep, high_ref[lon]) + dot(got, high_ref[1 - lon])
    smooth = smooth + (dot(keep, low_ref[lon]) + dot(got, low_ref[1 - lon]))
    step = nudge_ref.shape[0]
    total = out_ref.shape[0]
    for at in range(0, total, step):
        out_ref[at : at + step, :] = base_ref[at : at + step, :] + nudge_ref[...] * smooth[at : at + step]
    edge = lon_ref.shape[0]
    inner = pl.ds(pl.multiple_of((1 - lon) * (total - edge), edge), edge)
    outer = pl.ds(pl.multiple_of(lon * (total - edge), edge), edge)
    lon_ref[...] = out_ref[inner, :].astype(BF16)
    lat_ref[...] = out_ref[outer, :].astype(BF16)


def advance_kernel(where_ref, field_ref, lon_ref, lat_ref, out_ref, ext_ref, first_ref, last_ref):
    total, length = field_ref.shape
    edge = lon_ref.shape[0]
    channels = edge // 2
    rows = total // channels
    is_top = where_ref[0] == 0
    pole = where_ref[1] > 0
    from_lon, from_lat = lon_ref[...].astype(F32), lat_ref[...].astype(F32)
    ext_ref[:edge, :] = jnp.where(is_top, from_lat, from_lon)
    ext_ref[edge : edge + total, :] = field_ref[...]
    ext_ref[edge + total :, :] = jnp.where(is_top, from_lon, from_lat)

    def sections(ref, row, use):
        def tile(y, var):
            return ref[pl.ds(pl.multiple_of(y * channels + var * LEV, LEV), LEV), :]

        wind_u, wind_v = tile(row + 1, 0), tile(row + 1, 1)
        push_u, push_v = (0.5 * time_step) * wind_u, (0.5 * time_step) * wind_v
        calm = diffusion * time_step
        east, west, north, south = calm - push_u, calm + push_u, calm - push_v, calm + push_v
        for var in range(VARS):
            centre = tile(row + 1, var)
            step = east * pltpu.roll(centre, length - 1, axis=1) + west * pltpu.roll(centre, 1, axis=1)
            step = step + (north * tile(row + 2, var) + south * tile(row, var))
            use(row, var, centre, step - (4.0 * calm) * centre)

    def put_first(row, var, centre, step):
        at = pl.ds(pl.multiple_of(row * channels + var * LEV, LEV), LEV)
        first_ref[at, :] = centre + step

    def put_out(row, var, centre, step):
        nudged = ext_ref[pl.ds(pl.multiple_of((row + 2) * channels + var * LEV, LEV), LEV), :]
        at = pl.ds(pl.multiple_of(row * channels + var * LEV, LEV), LEV)
        last_ref[at, :] = 0.5 * (nudged + centre + step)

    def first_row(row, _):
        sections(ext_ref, row, put_first)
        return 0

    lax.fori_loop(0, rows + 2, first_row, 0)

    @pl.when(pole & is_top)
    def _():
        first_ref[:channels, :] = jnp.zeros((channels, length), F32)

    @pl.when(pole & jnp.logical_not(is_top))
    def _():
        first_ref[(rows + 1) * channels :, :] = jnp.zeros((channels, length), F32)

    def second_row(row, _):
        sections(first_ref, row, put_out)
        return 0

    lax.fori_loop(0, rows, second_row, 0)
    for y in range(0, rows, 8):
        for ch in range(0, channels, 8):
            block = [last_ref[(y + i) * channels + ch : (y + i) * channels + ch + 8, :][None] for i in range(8)]
            out_ref[ch : ch + 8, y : y + 8, :] = jnp.swapaxes(jnp.concatenate(block, axis=0), 0, 1)


def call(kernel, out_shape, n_in, scratch=(), vmem=56):
    vmem_spec = pl.BlockSpec(memory_space=pltpu.VMEM)
    many = isinstance(out_shape, (tuple, list))
    return pl.pallas_call(
        kernel,
        out_shape=out_shape,
        in_specs=[pl.BlockSpec(memory_space=pltpu.SMEM)] + [vmem_spec] * n_in,
        out_specs=[vmem_spec] * len(out_shape) if many else vmem_spec,
        scratch_shapes=list(scratch),
        compiler_params=pltpu.CompilerParams(vmem_limit_bytes=vmem * MIB),
    )


def body(tokens, ln_gain, w_query, w_keyval, w_out, w_dec, nudge, state):
    tok_rows, tok_cols, width = tokens.shape
    channels, state_rows, state_cols = state.shape
    n_lat, n_lon = lax.axis_size("lat"), lax.axis_size("lon")
    lat, lon = lax.axis_index("lat"), lax.axis_index("lon")
    total_cols = tok_cols * n_lon
    length = state_cols * n_lon
    band_rows = state_rows // n_lon
    both = ("lat", "lon")
    tokens_half = tok_cols * HALF
    decoded_lanes = tok_cols * PATCH
    band = band_rows * channels

    pole = ((lat == 0) & (lon == 0)) | ((lat == n_lat - 1) & (lon == 1))
    where = jnp.stack([lon, pole.astype(jnp.int32)]).astype(jnp.int32)

    def at(row, col):
        return row * n_lon + col

    last = n_lat - 1
    swap = [(0, 1), (1, 0)]
    shift = [(at(i, 0), at(i + 1, 0)) for i in range(last)] + [(at(last, 0), at(last, 1))]
    shift += [(at(i, 1), at(i - 1, 1)) for i in range(1, n_lat)] + [(at(0, 1), at(0, 0))]
    meet = [(at(i, 1), at(i + 1, 0)) for i in range(last)] + [(at(i + 1, 0), at(i, 1)) for i in range(last)]
    meet_all = meet + [(at(0, 0), at(0, 0)), (at(last, 1), at(last, 1))]

    give = lax.dynamic_slice_in_dim(tokens, HALF * (1 - lon), HALF, 0)
    own_first = lax.dynamic_slice(tokens, (HALF * lon, 0, 0), (HALF, WIN, width))
    got_tokens = lax.ppermute(give, both, shift)
    own_next = lax.ppermute(give[:, :WIN], "lon", swap)
    got_next = lax.ppermute(own_first, both, meet_all)
    give_state = lax.dynamic_slice_in_dim(state, band_rows * (1 - lon), band_rows, 1)
    got_state = lax.ppermute(give_state, "lon", swap)

    gain = ln_gain[None, :]
    nudge_rows = jnp.tile(nudge[:, None], (PATCH, 1))
    matrix = zonal_filter(length, KEEP)
    high, low = (jnp.asarray(m) for m in split_high_low(matrix))
    order = decoded_order(total_cols, n_lon)
    dec_high, dec_low = (jnp.asarray(m) for m in split_high_low(matrix[order]))
    w_dec_t = w_dec.reshape(width, channels, PATCH, PATCH).transpose(3, 2, 1, 0).reshape(-1, width)

    raw_own, qkv_own = call(
        own_kernel,
        (
            jax.ShapeDtypeStruct((tokens_half, width), BF16),
            jax.ShapeDtypeStruct((tokens_half, 3 * width), BF16),
        ),
        5,
        [pltpu.VMEM((tokens_half, width), BF16)],
    )(where, tokens, own_next, gain, w_query, w_keyval)

    base = call(
        state_kernel,
        jax.ShapeDtypeStruct((band, length), F32),
        5,
        [pltpu.VMEM((band, length), F32)],
    )(where, state, got_state, nudge_rows, high, low)

    decoded_shape = jax.ShapeDtypeStruct((band, decoded_lanes), BF16)
    window_cells = GROUP * WIN * WIN
    keep, send = call(
        main_kernel,
        (decoded_shape, decoded_shape),
        9,
        [
            pltpu.VMEM((tokens_half, width), BF16),
            pltpu.VMEM((tokens_half, width), BF16),
            pltpu.VMEM((tokens_half, 3 * width), BF16),
            pltpu.VMEM((window_cells, 4 * width // HEADS), BF16),
            pltpu.VMEM((window_cells, width), BF16),
        ],
    )(where, got_tokens, got_next, gain, raw_own, qkv_own, w_query, w_keyval, w_out, w_dec_t)

    got = lax.ppermute(send, both, meet_all)

    edge = jax.ShapeDtypeStruct((2 * channels, length), BF16)
    nudged, to_lon, to_lat = call(
        filter_kernel,
        (jax.ShapeDtypeStruct((band, length), F32), edge, edge),
        6,
    )(where, base, keep, got, nudge_rows, dec_high, dec_low)

    from_lat = lax.ppermute(to_lat, both, meet)
    from_lon = lax.ppermute(to_lon, "lon", swap)

    return call(
        advance_kernel,
        jax.ShapeDtypeStruct((channels, band_rows, length), F32),
        3,
        [
            pltpu.VMEM((band + 4 * channels, length), F32),
            pltpu.VMEM((band + 2 * channels, length), F32),
            pltpu.VMEM((band, length), F32),
        ],
    )(where, nudged, from_lon, from_lat)


def solution(mesh):
    in_specs = (
        P(("member", "lat"), "lon", None),
        P(),
        P(),
        P(),
        P(),
        P(),
        P(),
        P(None, ("member", "lat"), "lon"),
    )
    out_specs = P(None, ("member", "lat", "lon"), None)
    return jax.shard_map(body, mesh=mesh, in_specs=in_specs, out_specs=out_specs, check_vma=False)
```

time: 221 us -> 77.3 us (0.35); the launches traced: 217 us -> 76.7 us
  local copies, waits for them, and re-layouts: 85 us -> 9.95 us
  matrix products: 59.7 us -> 0 us
  Pallas kernels: 0 us -> 44.4 us
  other arithmetic: 23.8 us -> 0.66 us
  waiting for transfers between devices: 22 us -> 3.38 us
  blocking collectives: 5.9 us -> 0 us
    dot_general x8 -> x0, matrix products: 46.3 us -> none  [the longest x1 11.5 us: window_attention(): jnp.einsum('whqk,wkhd->wqhd', weights, value_heads, preferred_element_typ...]
    pallas_call x0 -> x5, Pallas kernels: none -> 44.4 us  [the longest x1 18.1 us: body(): call(main_kernel, (decoded_shape, decoded_shape), 9, [pltpu.VMEM((tokens_...]
    another operation x3 -> x2, local copies, waits for them, and re-layouts: 23.3 us -> 0.73 us  [body(): nudge_rows = jnp.tile(nudge[:, None], (PATCH, 1))]
    ppermute x8 -> x7, waiting for transfers between devices: 22 us -> 3.38 us  [the longest x1 3.34 us: body(): from_lat = lax.ppermute(to_lat, both, meet)]
    reshape x4 -> x1, local copies, waits for them, and re-layouts: 15.3 us -> 0.43 us  [body(): w_dec.reshape(width, channels, PATCH, PATCH).transpose(3, 2, 1, 0)]
    sub x1 -> x0, matrix products: 13.4 us -> none  [window_attention(): weights = jnp.exp(scores - peak_score)]
    slice x10 -> x1, local copies, waits for them, and re-layouts: 13.8 us -> 0.88 us  [body(): own_next = lax.ppermute(give[:, :WIN], 'lon', swap)]
    convert_element_type x1 -> x0, local copies, waits for them, and re-layouts: 10.5 us -> none  [window_attention(): mixed_out.astype(jnp.bfloat16)]
  transfers between devices with their start and end apart: 9 -> 7, of which waited for: 3 -> 1; matrix products, arithmetic and copies ran while one was open for 15% -> 7% of each run, Pallas kernels for 0% -> 41%
where the time goes in v1:
time: 77.3 us; the launch traced here: 76.7 us
  Pallas kernels  44.4 us (57%)
  starting transfers between devices  18.2 us (24%)
  local copies, waits for them, and re-layouts  9.95 us (13%)
  waiting for transfers between devices  3.38 us (4%)
    pallas_call x1, Pallas kernels, body(): call(main_kernel, (decoded_shape, decoded_shape), 9, [pltpu.VMEM((tokens_...  18.1 us
    pallas_call x1, Pallas kernels, body(): call(own_kernel, (jax.ShapeDtypeStruct((tokens_half, width), BF16), jax.S...  7.83 us
    pallas_call x1, Pallas kernels, body(): call(advance_kernel, jax.ShapeDtypeStruct((channels, band_rows, length),...  7.31 us
    pallas_call x1, Pallas kernels, body(): call(state_kernel, jax.ShapeDtypeStruct((band, length), F32), 5, [pltpu.V...  5.8 us
    pallas_call x1, Pallas kernels, body(): call(filter_kernel, (jax.ShapeDtypeStruct((band, length), F32), edge, edg...  5.4 us
    ppermute x1, starting transfers between devices, body(): got = lax.ppermute(send, both, meet_all)  4.91 us
    ppermute x1, starting transfers between devices, body(): from_lon = lax.ppermute(to_lon, 'lon', swap)  3.83 us
    ppermute x1, starting transfers between devices, body(): from_lat = lax.ppermute(to_lat, both, meet)  3.66 us
  transfers between devices with their start and end apart: 7, of which 1 were waited for; matrix products, arithmetic and copies ran while one was open for 7% of the time, Pallas kernels for 41%

profile of v1, /device:TPU:15, one launch (start us, length us, event | category | flops | bytes accessed | tf_op | source)
XLA Modules:
  0.0 76.7 jit_solution(4051391661603809765)
XLA Ops:
  0.0 0.0 copy-start
  0.0 0.0 copy-start.1
  0.0 2.3 %constant_dynamic-slice_fusion.2 = bf16[4,96,1024]{2,1,0:T(8,128)(2,1)} fusion(bf16[8,96,1024]{2,1,0:T(8,128)(2,1)} %tok_ref.1, s32[]{:T(128)S(6)} %select_n.10), kind=kLoop, calls=%fused_computation.2 | loop fusion | bytes 1572868 | tf_op jit(solution)/shard_map/dynamic_slice | solution.py:373
  2.3 0.2 collective-permute-start.1
  2.5 0.0 copy-done
  2.5 0.9 %constant_dynamic-slice_fusion.3 = f32[32,16,384]{2,1,0:T(8,128)} fusion(f32[32,32,384]{2,1,0:T(8,128)S(1)} %copy-done, s32[]{:T(128)S(6)} %select_n.9), kind=kLoop, calls=%fused_computation.3 | loop fusion | bytes 1572868 | tf_op jit(solution)/shard_map/dynamic_slice | solution.py:378
  3.4 2.0 %collective-permute-start = (f32[32,16,384]{2,1,0:T(8,128)}, f32[32,16,384]{2,1,0:T(8,128)}, u32[]{:S(2)}, u32[]{:S(2)}) collective-permute-start(f32[32,16,384]{2,1,0:T(8,128)} %constant_dynamic-slice_fusion.3), channel_id=1, source_target_pairs={{0,1},{1,0},{2,3},{3,2},{4,5},{5,4},{6,7},{7,6},{8,9},{9,8},{10,11... | collective-permute-start | bytes 2359304 | tf_op jit(solution)/shard_map/ppermute | solution.py:379
  5.4 0.9 %constant_dynamic-slice_fusion = (bf16[4,8,1024]{2,1,0:T(8,128)(2,1)S(1)}, bf16[4,8,1024]{2,1,0:T(8,128)(2,1)S(1)}) fusion(bf16[8,96,1024]{2,1,0:T(8,128)(2,1)} %tok_ref.1, s32[]{:T(128)S(6)} %select_n.10, s32[]{:T(128)S(6)} %select_n.11), kind=kLoop, calls=%fused_computation | loop fusion | bytes 262152 | tf_op jit(solution)/shard_map/slice | solution.py:376
  6.3 0.1 collective-permute-start.3
  6.4 3.5 %collective-permute-start.2 = (bf16[4,8,1024]{2,1,0:T(8,128)(2,1)S(1)}, bf16[4,8,1024]{2,1,0:T(8,128)(2,1)S(1)}, u32[]{:S(2)}, u32[]{:S(2)}) collective-permute-start(bf16[4,8,1024]{2,1,0:T(8,128)(2,1)S(1)} %get-tuple-element.20), channel_id=1, source_target_pairs={{1,2},{3,4},{5,6},{7,8},{9,10},{11,12},{13,14},{2,1},{4,3},{6,5},{... | collective-permute-start | bytes 196616 | tf_op jit(solution)/shard_map/ppermute | solution.py:377
  9.9 0.0 copy-done.1
  9.9 0.5 copy.17
  10.4 0.4 reshape.12
  10.9 1.5 %copy.18 = bf16[4,4,32,1024]{3,2,1,0:T(8,128)(2,1)} copy(bf16[4,4,32,1024]{3,0,1,2:T(4,128)(2,1)S(1)} %bitcast.8) | data formatting | bytes 2097152 | tf_op jit(solution)/shard_map/transpose | solution.py:387
  12.4 0.7 pad_add_fusion.where_ref
  13.1 0.0 collective-permute-done.3.next_ref
  13.1 0.0 copy-start.6
  13.1 0.6 copy-done.6
  13.7 7.8 %shard_map.119 = (bf16[384,1024]{1,0:T(8,128)(2,1)}, bf16[384,3072]{1,0:T(8,128)(2,1)}) custom-call(s32[2]{0:T(128)} %pad_add_fusion.where_ref, bf16[8,96,1024]{2,1,0:T(8,128)(2,1)} %tok_ref.1, bf16[4,8,1024]{2,1,0:T(8,128)(2,1)} %copy-done.6, f32[1,1024]{1,0:T(1,128)} %bitcast.9, bf16[1024,1024]{1,0:T(8,128)(2,1)} %wq_ref.3, bf16[1024,2048]{1,0:T(8,128)(2,1)} %wkv_ref.3), custom_call_target="tpu_custom_call" | custom-call | tf_op jit(solution)/shard_map/pallas_call | solution.py:389
  21.5 0.0 collective-permute-done.2.next_ref
  21.5 0.0 copy-start.5
  21.5 0.0 collective-permute-done.1.x_ref
  21.6 0.6 copy-done.5
  22.2 0.0 copy-start.7
  22.2 18.1 %shard_map.120 = (bf16[512,384]{1,0:T(8,128)(2,1)}, bf16[512,384]{1,0:T(8,128)(2,1)}) custom-call(s32[2]{0:T(128)} %pad_add_fusion.where_ref, bf16[4,96,1024]{2,1,0:T(8,128)(2,1)} %collective-permute-done.1.x_ref, bf16[4,8,1024]{2,1,0:T(8,128)(2,1)} %copy-done.5, f32[1,1024]{1,0:T(1,128)} %bitcast.10, bf16[384,1024]{1,0:T(8,128)(2,1)} %get-tuple-element.12.raw_own_ref, ...), custom_call_target="tpu_custom_call" | custom-call | tf_op jit(solution)/shard_map/pallas_call | solution.py:408
  40.2 4.9 %collective-permute-start.4 = (bf16[512,384]{1,0:T(8,128)(2,1)}, bf16[512,384]{1,0:T(8,128)(2,1)S(1)}, u32[]{:S(2)}, u32[]{:S(2)}) collective-permute-start(bf16[512,384]{1,0:T(8,128)(2,1)} %get-tuple-element.15), channel_id=1, source_target_pairs={{1,2},{3,4},{5,6},{7,8},{9,10},{11,12},{13,14},{2,1},{4,3},{6,5},{... | collective-permute-start | bytes 1179656 | tf_op jit(solution)/shard_map/ppermute | solution.py:421
  45.1 0.0 copy-done.7
  45.2 0.7 tile.10.nudge_ref
  45.9 0.0 collective-permute-done.got_ref
  45.9 5.8 %shard_map.118.base_ref = f32[512,768]{1,0:T(8,128)} custom-call(s32[2]{0:T(128)} %pad_add_fusion.where_ref, f32[32,32,384]{2,1,0:T(8,128)} %state_ref.1, f32[32,16,384]{2,1,0:T(8,128)} %collective-permute-done.got_ref, f32[128,1]{1,0:T(8,128)} %tile.10.nudge_ref, bf16[768,768]{1,0:T(8,128)(2,1)} %constant.30.clone.high_ref, ...), custom_call_target="tpu_custom_call" | custom-call | tf_op jit(solution)/shard_map/pallas_call | solution.py:399
  51.7 0.0 collective-permute-done.4.got_ref
  51.7 0.0 copy-start.2
  51.7 0.8 copy-done.2
  52.5 5.4 %shard_map.121 = (f32[512,768]{1,0:T(8,128)}, bf16[64,768]{1,0:T(8,128)(2,1)}, bf16[64,768]{1,0:T(8,128)(2,1)}) custom-call(s32[2]{0:T(128)} %pad_add_fusion.where_ref, f32[512,768]{1,0:T(8,128)} %shard_map.118.base_ref, bf16[512,384]{1,0:T(8,128)(2,1)} %get-tuple-element.14.keep_ref, bf16[512,384]{1,0:T(8,128)(2,1)} %copy-done.2, f32[128,1]{1,0:T(8,128)} %tile.10.nudge_ref, ...), custom_call_target="tpu_custom_call" | custom-call | tf_op jit(solution)/shard_map/pallas_call | solution.py:424
  57.9 3.8 %collective-permute-start.5 = (bf16[64,768]{1,0:T(8,128)(2,1)}, bf16[64,768]{1,0:T(8,128)(2,1)S(1)}, u32[]{:S(2)}, u32[]{:S(2)}) collective-permute-start(bf16[64,768]{1,0:T(8,128)(2,1)} %get-tuple-element.17), channel_id=1, source_target_pairs={{0,1},{1,0},{2,3},{3,2},{4,5},{5,4},{6,7},{7,6},{8,9},{9,8},{10,11... | collective-permute-start | bytes 294920 | tf_op jit(solution)/shard_map/ppermute | solution.py:431
  61.7 3.7 %collective-permute-start.6 = (bf16[64,768]{1,0:T(8,128)(2,1)}, bf16[64,768]{1,0:T(8,128)(2,1)S(1)}, u32[]{:S(2)}, u32[]{:S(2)}) collective-permute-start(bf16[64,768]{1,0:T(8,128)(2,1)} %get-tuple-element.18), channel_id=1, source_target_pairs={{1,2},{3,4},{5,6},{7,8},{9,10},{11,12},{13,14},{2,1},{4,3},{6,5},{... | collective-permute-start | bytes 294920 | tf_op jit(solution)/shard_map/ppermute | solution.py:430
  65.4 0.0 collective-permute-done.5.lon_ref
  65.4 0.0 copy-start.3
  65.4 3.3 %collective-permute-done.6.lat_ref = bf16[64,768]{1,0:T(8,128)(2,1)S(1)} collective-permute-done((bf16[64,768]{1,0:T(8,128)(2,1)}, bf16[64,768]{1,0:T(8,128)(2,1)S(1)}, u32[]{:S(2)}, u32[]{:S(2)}) %collective-permute-start.6) | collective-permute-done | bytes 98336 | tf_op jit(solution)/shard_map/ppermute | solution.py:430
  68.7 0.0 copy-start.4
  68.7 0.0 copy-done.3
  68.7 0.6 copy-done.4
  69.4 7.3 %shard_map.122 = f32[32,16,768]{2,1,0:T(8,128)} custom-call(s32[2]{0:T(128)} %pad_add_fusion.where_ref, f32[512,768]{1,0:T(8,128)} %get-tuple-element.16.field_ref, bf16[64,768]{1,0:T(8,128)(2,1)} %copy-done.3, bf16[64,768]{1,0:T(8,128)(2,1)} %copy-done.4), custom_call_target="tpu_custom_call" | custom-call | tf_op jit(solution)/shard_map/pallas_call | solution.py:433
  (1 shorter events, 0.0 us)
Async XLA Ops:
  0.0 2.5 %copy-start = (f32[32,32,384]{2,1,0:T(8,128)S(1)}, f32[32,32,384]{2,1,0:T(8,128)}, u32[]{:S(2)}) copy-start(f32[32,32,384]{2,1,0:T(8,128)} %state_ref.1) | copy-start | bytes 4718596
  0.0 9.9 %copy-start.1 = (bf16[1024,512]{1,0:T(8,128)(2,1)S(1)}, bf16[1024,512]{1,0:T(8,128)(2,1)}, u32[]{:S(2)}) copy-start(bf16[1024,512]{1,0:T(8,128)(2,1)} %param.17) | copy-start | bytes 3145732
  2.3 19.3 %collective-permute-start.1 = (bf16[4,96,1024]{2,1,0:T(8,128)(2,1)}, bf16[4,96,1024]{2,1,0:T(8,128)(2,1)}, u32[]{:S(2)}, u32[]{:S(2)}) collective-permute-start(bf16[4,96,1024]{2,1,0:T(8,128)(2,1)} %constant_dynamic-slice_fusion.2), channel_id=1, source_target_pairs={{0,2},{2,4},{4,6},{6,8},{8,10},{10,12},{12,14},{14,15},{3,1},{5,3}... | collective-permute-start | bytes 2359304 | tf_op jit(solution)/shard_map/ppermute | solution.py:375
  3.4 42.5 %collective-permute-start = (f32[32,16,384]{2,1,0:T(8,128)}, f32[32,16,384]{2,1,0:T(8,128)}, u32[]{:S(2)}, u32[]{:S(2)}) collective-permute-start(f32[32,16,384]{2,1,0:T(8,128)} %constant_dynamic-slice_fusion.3), channel_id=1, source_target_pairs={{0,1},{1,0},{2,3},{3,2},{4,5},{5,4},{6,7},{7,6},{8,9},{9,8},{10,11... | collective-permute-start | bytes 2359304 | tf_op jit(solution)/shard_map/ppermute | solution.py:379
  6.3 6.8 %collective-permute-start.3 = (bf16[4,8,1024]{2,1,0:T(8,128)(2,1)S(1)}, bf16[4,8,1024]{2,1,0:T(8,128)(2,1)S(1)}, u32[]{:S(2)}, u32[]{:S(2)}) collective-permute-start(bf16[4,8,1024]{2,1,0:T(8,128)(2,1)S(1)} %get-tuple-element.19), channel_id=1, source_target_pairs={{0,1},{1,0},{2,3},{3,2},{4,5},{5,4},{6,7},{7,6},{8,9},{9,8},{10,11... | collective-permute-start | bytes 196616 | tf_op jit(solution)/shard_map/ppermute | solution.py:376
  6.4 15.2 %collective-permute-start.2 = (bf16[4,8,1024]{2,1,0:T(8,128)(2,1)S(1)}, bf16[4,8,1024]{2,1,0:T(8,128)(2,1)S(1)}, u32[]{:S(2)}, u32[]{:S(2)}) collective-permute-start(bf16[4,8,1024]{2,1,0:T(8,128)(2,1)S(1)} %get-tuple-element.20), channel_id=1, source_target_pairs={{1,2},{3,4},{5,6},{7,8},{9,10},{11,12},{13,14},{2,1},{4,3},{6,5},{... | collective-permute-start | bytes 196616 | tf_op jit(solution)/shard_map/ppermute | solution.py:377
  13.1 0.6 copy-start.6
  21.5 0.6 copy-start.5
  22.2 23.0 %copy-start.7 = (f32[32]{0:T(128)S(1)}, f32[32]{0:T(128)}, u32[]{:S(2)}) copy-start(f32[32]{0:T(128)} %param.18) | copy-start | bytes 388
  40.2 11.5 %collective-permute-start.4 = (bf16[512,384]{1,0:T(8,128)(2,1)}, bf16[512,384]{1,0:T(8,128)(2,1)S(1)}, u32[]{:S(2)}, u32[]{:S(2)}) collective-permute-start(bf16[512,384]{1,0:T(8,128)(2,1)} %get-tuple-element.15), channel_id=1, source_target_pairs={{1,2},{3,4},{5,6},{7,8},{9,10},{11,12},{13,14},{2,1},{4,3},{6,5},{... | collective-permute-start | bytes 1179656 | tf_op jit(solution)/shard_map/ppermute | solution.py:421
  51.7 0.8 copy-start.2
  57.9 7.5 %collective-permute-start.5 = (bf16[64,768]{1,0:T(8,128)(2,1)}, bf16[64,768]{1,0:T(8,128)(2,1)S(1)}, u32[]{:S(2)}, u32[]{:S(2)}) collective-permute-start(bf16[64,768]{1,0:T(8,128)(2,1)} %get-tuple-element.17), channel_id=1, source_target_pairs={{0,1},{1,0},{2,3},{3,2},{4,5},{5,4},{6,7},{7,6},{8,9},{9,8},{10,11... | collective-permute-start | bytes 294920 | tf_op jit(solution)/shard_map/ppermute | solution.py:431
  61.7 7.0 %collective-permute-start.6 = (bf16[64,768]{1,0:T(8,128)(2,1)}, bf16[64,768]{1,0:T(8,128)(2,1)S(1)}, u32[]{:S(2)}, u32[]{:S(2)}) collective-permute-start(bf16[64,768]{1,0:T(8,128)(2,1)} %get-tuple-element.18), channel_id=1, source_target_pairs={{1,2},{3,4},{5,6},{7,8},{9,10},{11,12},{13,14},{2,1},{4,3},{6,5},{... | collective-permute-start | bytes 294920 | tf_op jit(solution)/shard_map/ppermute | solution.py:430
  65.4 3.4 %copy-start.3 = (bf16[64,768]{1,0:T(8,128)(2,1)}, bf16[64,768]{1,0:T(8,128)(2,1)S(1)}, u32[]{:S(2)}) copy-start(bf16[64,768]{1,0:T(8,128)(2,1)S(1)} %collective-permute-done.5.lon_ref) | copy-start | bytes 294916
  68.7 0.7 copy-start.4

commit v2 on v1

--- a/solution.py
+++ b/solution.py
@@ -56,6 +56,19 @@
                     lanes.append((col % total_cols) * PATCH + b)
         rows.append(lanes)
     return np.array(rows)
+
+
+def place():
+    lat, lon = lax.axis_index("lat"), lax.axis_index("lon")
+    return lon, ((lat == 0) & (lon == 0)) | ((lat == lax.axis_size("lat") - 1) & (lon == 1))
+
+
+def nudge_column(nudge_ref, rows):
+    channels = nudge_ref.shape[1]
+    picked = lax.broadcasted_iota(jnp.int32, (rows, channels), 0) % channels == lax.broadcasted_iota(
+        jnp.int32, (rows, channels), 1
+    )
+    return jnp.sum(jnp.where(picked, nudge_ref[...], 0.0), axis=1, keepdims=True)
 
 
 def dot(a, b):
@@ -108,8 +121,8 @@
     qkv_ref[:, 2 * width :] = dot(normed, wkv_ref[:, width:]).astype(BF16)
 
 
-def own_kernel(where_ref, tok_ref, next_ref, gain_ref, wq_ref, wkv_ref, raw_ref, qkv_ref, normed_ref):
-    first = HALF * where_ref[0]
+def own_kernel(tok_ref, next_ref, gain_ref, wq_ref, wkv_ref, raw_ref, qkv_ref, normed_ref):
+    first = HALF * place()[0]
     place_tokens(
         lambda r, c: tok_ref[first + r, c : c + 2 * WIN, :],
         lambda r: next_ref[r],
@@ -122,7 +135,6 @@
 
 
 def main_kernel(
-    where_ref,
     x_ref,
     next_ref,
     gain_ref,
@@ -160,7 +172,7 @@
 
     blocks = (iota((lanes, lanes), 0) // head_size == iota((lanes, lanes), 1) // head_size).astype(F32).astype(BF16)
     split_rows = iota((cells, 2 * cells), 0) // half_cells != iota((cells, 2 * cells), 1) % cells // half_cells
-    bias = jnp.where(split_rows & (where_ref[1] > 0), -1e30, 0.0)
+    bias = jnp.where(split_rows & place()[1], -1e30, 0.0)
     first_head = iota((cells, 2 * cells), 1) < cells
     scale = 1.0 / math.sqrt(head_size)
     token_rows = GROUP * WIN
@@ -232,8 +244,8 @@
     lax.fori_loop(0, cols // token_rows, one_group, 0)
 
 
-def state_kernel(where_ref, state_ref, got_ref, nudge_ref, high_ref, low_ref, out_ref, whole_ref):
-    lon = where_ref[0]
+def state_kernel(state_ref, got_ref, nudge_ref, high_ref, low_ref, out_ref, whole_ref):
+    lon = place()[0]
     channels, own_rows, cols = got_ref.shape
     own_lanes = pl.ds(pl.multiple_of(lon * cols, 128), cols)
     got_lanes = pl.ds(pl.multiple_of((1 - lon) * cols, 128), cols)
@@ -246,24 +258,26 @@
                 rows = slice((y + i) * channels + ch, (y + i) * channels + ch + 8)
                 whole_ref[rows, own_lanes] = own[i]
                 whole_ref[rows, got_lanes] = got[i]
-    step = nudge_ref.shape[0]
+    step = PATCH * channels
+    strength = nudge_column(nudge_ref, step)
     for at in range(0, out_ref.shape[0], step):
         field = whole_ref[at : at + step, :]
         high = field.astype(BF16)
         low = (field - high.astype(F32)).astype(BF16)
         smooth = dot(high, high_ref[...]) + (dot(high, low_ref[...]) + dot(low, high_ref[...]))
-        out_ref[at : at + step, :] = field - nudge_ref[...] * smooth
-
-
-def filter_kernel(where_ref, base_ref, keep_ref, got_ref, nudge_ref, high_ref, low_ref, out_ref, lon_ref, lat_ref):
-    lon = where_ref[0]
+        out_ref[at : at + step, :] = field - strength * smooth
+
+
+def filter_kernel(base_ref, keep_ref, got_ref, nudge_ref, high_ref, low_ref, out_ref, lon_ref, lat_ref):
+    lon = place()[0]
     keep, got = keep_ref[...], got_ref[...]
     smooth = dot(keep, high_ref[lon]) + dot(got, high_ref[1 - lon])
     smooth = smooth + (dot(keep, low_ref[lon]) + dot(got, low_ref[1 - lon]))
-    step = nudge_ref.shape[0]
+    step = PATCH * nudge_ref.shape[1]
+    strength = nudge_column(nudge_ref, step)
     total = out_ref.shape[0]
     for at in range(0, total, step):
-        out_ref[at : at + step, :] = base_ref[at : at + step, :] + nudge_ref[...] * smooth[at : at + step]
+        out_ref[at : at + step, :] = base_ref[at : at + step, :] + strength * smooth[at : at + step]
     edge = lon_ref.shape[0]
     inner = pl.ds(pl.multiple_of((1 - lon) * (total - edge), edge), edge)
     outer = pl.ds(pl.multiple_of(lon * (total - edge), edge), edge)
@@ -271,13 +285,13 @@
     lat_ref[...] = out_ref[outer, :].astype(BF16)
 
 
-def advance_kernel(where_ref, field_ref, lon_ref, lat_ref, out_ref, ext_ref, first_ref, last_ref):
+def advance_kernel(field_ref, lon_ref, lat_ref, out_ref, ext_ref, first_ref, last_ref):
     total, length = field_ref.shape
     edge = lon_ref.shape[0]
     channels = edge // 2
     rows = total // channels
-    is_top = where_ref[0] == 0
-    pole = where_ref[1] > 0
+    lon, pole = place()
+    is_top = lon == 0
     from_lon, from_lat = lon_ref[...].astype(F32), lat_ref[...].astype(F32)
     ext_ref[:edge, :] = jnp.where(is_top, from_lat, from_lon)
     ext_ref[edge : edge + total, :] = field_ref[...]
@@ -331,13 +345,13 @@
             out_ref[ch : ch + 8, y : y + 8, :] = jnp.swapaxes(jnp.concatenate(block, axis=0), 0, 1)
 
 
-def call(kernel, out_shape, n_in, scratch=(), vmem=56):
+def call(kernel, out_shape, n_in, scratch=(), vmem=24):
     vmem_spec = pl.BlockSpec(memory_space=pltpu.VMEM)
     many = isinstance(out_shape, (tuple, list))
     return pl.pallas_call(
         kernel,
         out_shape=out_shape,
-        in_specs=[pl.BlockSpec(memory_space=pltpu.SMEM)] + [vmem_spec] * n_in,
+        in_specs=[vmem_spec] * n_in,
         out_specs=[vmem_spec] * len(out_shape) if many else vmem_spec,
         scratch_shapes=list(scratch),
         compiler_params=pltpu.CompilerParams(vmem_limit_bytes=vmem * MIB),
@@ -348,7 +362,7 @@
     tok_rows, tok_cols, width = tokens.shape
     channels, state_rows, state_cols = state.shape
     n_lat, n_lon = lax.axis_size("lat"), lax.axis_size("lon")
-    lat, lon = lax.axis_index("lat"), lax.axis_index("lon")
+    lon = lax.axis_index("lon")
     total_cols = tok_cols * n_lon
     length = state_cols * n_lon
     band_rows = state_rows // n_lon
@@ -357,8 +371,6 @@
     decoded_lanes = tok_cols * PATCH
     band = band_rows * channels
 
-    pole = ((lat == 0) & (lon == 0)) | ((lat == n_lat - 1) & (lon == 1))
-    where = jnp.stack([lon, pole.astype(jnp.int32)]).astype(jnp.int32)
 
     def at(row, col):
         return row * n_lon + col
@@ -379,7 +391,7 @@
     got_state = lax.ppermute(give_state, "lon", swap)
 
     gain = ln_gain[None, :]
-    nudge_rows = jnp.tile(nudge[:, None], (PATCH, 1))
+    nudge_row = nudge[None, :]
     matrix = zonal_filter(length, KEEP)
     high, low = (jnp.asarray(m) for m in split_high_low(matrix))
     order = decoded_order(total_cols, n_lon)
@@ -394,14 +406,14 @@
         ),
         5,
         [pltpu.VMEM((tokens_half, width), BF16)],
-    )(where, tokens, own_next, gain, w_query, w_keyval)
+    )(tokens, own_next, gain, w_query, w_keyval)
 
     base = call(
         state_kernel,
         jax.ShapeDtypeStruct((band, length), F32),
         5,
         [pltpu.VMEM((band, length), F32)],
-    )(where, state, got_state, nudge_rows, high, low)
+    )(state, got_state, nudge_row, high, low)
 
     decoded_shape = jax.ShapeDtypeStruct((band, decoded_lanes), BF16)
     window_cells = GROUP * WIN * WIN
@@ -416,7 +428,7 @@
             pltpu.VMEM((window_cells, 4 * width // HEADS), BF16),
             pltpu.VMEM((window_cells, width), BF16),
         ],
-    )(where, got_tokens, got_next, gain, raw_own, qkv_own, w_query, w_keyval, w_out, w_dec_t)
+    )(got_tokens, got_next, gain, raw_own, qkv_own, w_query, w_keyval, w_out, w_dec_t)
 
     got = lax.ppermute(send, both, meet_all)
 
@@ -425,7 +437,7 @@
         filter_kernel,
         (jax.ShapeDtypeStruct((band, length), F32), edge, edge),
         6,
-    )(where, base, keep, got, nudge_rows, dec_high, dec_low)
+    )(base, keep, got, nudge_row, dec_high, dec_low)
 
     from_lat = lax.ppermute(to_lat, both, meet)
     from_lon = lax.ppermute(to_lon, "lon", swap)
@@ -439,7 +451,7 @@
             pltpu.VMEM((band + 2 * channels, length), F32),
             pltpu.VMEM((band, length), F32),
         ],
-    )(where, nudged, from_lon, from_lat)
+    )(nudged, from_lon, from_lat)
 
 
 def solution(mesh):

time: 77.3 us -> 66 us (0.85)
  Pallas kernels: 44.4 us -> 28.3 us
  local copies, waits for them, and re-layouts: 9.95 us -> 11.9 us
  waiting for transfers between devices: 3.38 us -> 5.22 us
  starting transfers between devices: 18.2 us -> 19.8 us
    pallas_call x1, Pallas kernels: 7.83 us -> 3.05 us  [body(): call(own_kernel, (jax.ShapeDtypeStruct((tokens_half, width), BF16), jax.S...]
    pallas_call x1, Pallas kernels: 18.1 us -> 13.6 us  [body(): call(main_kernel, (decoded_shape, decoded_shape), 9, [pltpu.VMEM((tokens_...]
    pallas_call x1, Pallas kernels: 5.4 us -> 1.86 us  [body(): call(filter_kernel, (jax.ShapeDtypeStruct((band, length), F32), edge, edg...]
    reshape x1, local copies, waits for them, and re-layouts: 0.43 us -> 2.26 us  [body(): w_dec.reshape(width, channels, PATCH, PATCH).transpose(3, 2, 1, 0)]
    pallas_call x1, Pallas kernels: 5.8 us -> 3.97 us  [body(): call(state_kernel, jax.ShapeDtypeStruct((band, length), F32), 5, [pltpu.V...]
    pallas_call x1, Pallas kernels: 7.31 us -> 5.84 us  [body(): call(advance_kernel, jax.ShapeDtypeStruct((channels, band_rows, length),...]
    unnamed x17 -> x25, local copies, waits for them, and re-layouts: 3.18 us -> 4.5 us
    ppermute x1, waiting for transfers between devices: 0.01 us -> 1.32 us  [body(): got = lax.ppermute(send, both, meet_all)]
  transfers between devices with their start and end apart: 7 -> 7, of which waited for: 1 -> 3; matrix products, arithmetic and copies ran while one was open for 7% -> 11% of each run, Pallas kernels for 41% -> 31%
where the time goes in v2:
time: 66 us; the launch traced here: 65.5 us
  Pallas kernels  28.3 us (43%)
  starting transfers between devices  19.8 us (30%)
  local copies, waits for them, and re-layouts  11.9 us (18%)
  waiting for transfers between devices  5.22 us (8%)
    pallas_call x1, Pallas kernels, body(): call(main_kernel, (decoded_shape, decoded_shape), 9, [pltpu.VMEM((tokens_...  13.6 us
    pallas_call x1, Pallas kernels, body(): call(advance_kernel, jax.ShapeDtypeStruct((channels, band_rows, length),...  5.84 us
    ppermute x1, starting transfers between devices, body(): got = lax.ppermute(send, both, meet_all)  5.51 us
    ppermute x1, starting transfers between devices, body(): from_lon = lax.ppermute(to_lon, 'lon', swap)  4.87 us
    unnamed x25, local copies, waits for them, and re-layouts  4.5 us
    pallas_call x1, Pallas kernels, body(): call(state_kernel, jax.ShapeDtypeStruct((band, length), F32), 5, [pltpu.V...  3.97 us
    ppermute x1, starting transfers between devices, body(): from_lat = lax.ppermute(to_lat, both, meet)  3.66 us
    ppermute x1, starting transfers between devices, body(): got_next = lax.ppermute(own_first, both, meet_all)  3.52 us
  transfers between devices with their start and end apart: 7, of which 3 were waited for; matrix products, arithmetic and copies ran while one was open for 11% of the time, Pallas kernels for 31%

profile of v2, /device:TPU:15, one launch (start us, length us, event | category | flops | bytes accessed | tf_op | source)
XLA Modules:
  0.0 65.5 jit_solution(2128651209868113786)
XLA Ops:
  0.0 0.0 copy-start.4
  0.0 0.0 copy-start.3
  0.0 2.2 %constant_dynamic-slice_fusion.2 = bf16[4,96,1024]{2,1,0:T(8,128)(2,1)} fusion(bf16[8,96,1024]{2,1,0:T(8,128)(2,1)} %tok_ref.1, s32[]{:T(128)S(6)} %select_n.10), kind=kLoop, calls=%fused_computation.2 | loop fusion | bytes 1572868 | tf_op jit(solution)/shard_map/dynamic_slice | solution.py:385
  2.2 0.2 collective-permute-start.1
  2.5 0.0 copy-done.4
  2.5 1.0 %constant_dynamic-slice_fusion.3 = f32[32,16,384]{2,1,0:T(8,128)} fusion(f32[32,32,384]{2,1,0:T(8,128)S(1)} %copy-done.4, s32[]{:T(128)S(6)} %select_n.9), kind=kLoop, calls=%fused_computation.3 | loop fusion | bytes 1572868 | tf_op jit(solution)/shard_map/dynamic_slice | solution.py:390
  3.4 2.0 %collective-permute-start = (f32[32,16,384]{2,1,0:T(8,128)}, f32[32,16,384]{2,1,0:T(8,128)}, u32[]{:S(2)}, u32[]{:S(2)}) collective-permute-start(f32[32,16,384]{2,1,0:T(8,128)} %constant_dynamic-slice_fusion.3), channel_id=1, source_target_pairs={{0,1},{1,0},{2,3},{3,2},{4,5},{5,4},{6,7},{7,6},{8,9},{9,8},{10,11... | collective-permute-start | bytes 2359304 | tf_op jit(solution)/shard_map/ppermute | solution.py:391
  5.4 0.0 copy-done.3
  5.4 0.1 collective-permute-start.3
  5.5 3.5 %collective-permute-start.2 = (bf16[4,8,1024]{2,1,0:T(8,128)(2,1)S(1)}, bf16[4,8,1024]{2,1,0:T(8,128)(2,1)S(1)}, u32[]{:S(2)}, u32[]{:S(2)}) collective-permute-start(bf16[4,8,1024]{2,1,0:T(8,128)(2,1)S(1)} %get-tuple-element.20), channel_id=1, source_target_pairs={{1,2},{3,4},{5,6},{7,8},{9,10},{11,12},{13,14},{2,1},{4,3},{6,5},{... | collective-permute-start | bytes 196616 | tf_op jit(solution)/shard_map/ppermute | solution.py:389
  9.0 2.3 %copy.14 = bf16[1024,512]{0,1:T(8,128)(2,1)} copy(bf16[1024,512]{1,0:T(8,128)(2,1)} %param.17) | data formatting | bytes 2097152 | tf_op args[5]
  11.3 0.0 copy-start.10
  11.3 2.3 %reshape.6 = bf16[1024,32,4,4]{0,3,2,1:T(4,128)(2,1)} reshape(bf16[1024,512]{0,1:T(8,128)(2,1)} %copy.14) | data formatting | bytes 2097152 | tf_op jit(solution)/shard_map/reshape | solution.py:399
  13.5 0.0 copy-start.2
  13.5 2.0 %copy.15 = bf16[4,4,32,1024]{3,2,1,0:T(8,128)(2,1)S(1)} copy(bf16[4,4,32,1024]{3,0,1,2:T(4,128)(2,1)} %bitcast.11) | data formatting | bytes 2097152 | tf_op jit(solution)/shard_map/transpose | solution.py:399
  15.5 0.0 collective-permute-done.3.next_ref
  15.5 0.0 copy-done.10
  15.5 0.0 copy-done.2
  15.5 0.0 copy-start
  15.5 2.2 %copy-done = bf16[1024,2048]{1,0:T(8,128)(2,1)S(1)} copy-done((bf16[1024,2048]{1,0:T(8,128)(2,1)S(1)}, bf16[1024,2048]{1,0:T(8,128)(2,1)}, u32[]{:S(2)}) %copy-start) | copy-done | bytes 4194328
  17.7 0.0 copy-start.1
  17.7 0.0 copy-start.5
  17.7 3.1 %shard_map.119 = (bf16[384,1024]{1,0:T(8,128)(2,1)S(1)}, bf16[384,3072]{1,0:T(8,128)(2,1)S(1)}) custom-call(bf16[8,96,1024]{2,1,0:T(8,128)(2,1)S(1)} %copy-done.3, bf16[4,8,1024]{2,1,0:T(8,128)(2,1)S(1)} %collective-permute-done.3.next_ref, f32[1,1024]{1,0:T(1,128)S(1)} %bitcast.7, bf16[1024,1024]{1,0:T(8,128)(2,1)S(1)} %copy-done.2, ...), custom_call_target="tpu_custom_call" | custom-call | tf_op jit(solution)/shard_map/pallas_call | solution.py:401
  20.8 0.0 collective-permute-done.2.next_ref
  20.8 0.7 %collective-permute-done.1.x_ref = bf16[4,96,1024]{2,1,0:T(8,128)(2,1)} collective-permute-done((bf16[4,96,1024]{2,1,0:T(8,128)(2,1)}, bf16[4,96,1024]{2,1,0:T(8,128)(2,1)}, u32[]{:S(2)}, u32[]{:S(2)}) %collective-permute-start.1) | collective-permute-done | bytes 786464 | tf_op jit(solution)/shard_map/ppermute | solution.py:387
  21.5 0.0 copy-done.1
  21.5 0.0 copy-done.5
  21.5 0.0 copy-start.8
  21.5 0.0 copy-start.9
  21.5 0.0 copy-start.11
  21.6 13.6 %shard_map.120 = (bf16[512,384]{1,0:T(8,128)(2,1)S(1)}, bf16[512,384]{1,0:T(8,128)(2,1)S(1)}) custom-call(bf16[4,96,1024]{2,1,0:T(8,128)(2,1)} %collective-permute-done.1.x_ref, bf16[4,8,1024]{2,1,0:T(8,128)(2,1)S(1)} %collective-permute-done.2.next_ref, f32[1,1024]{1,0:T(1,128)S(1)} %bitcast.8, bf16[384,1024]{1,0:T(8,128)(2,1)S(1)} %get-tuple-element.12.raw_own_ref, ...), custom_call_target="tpu_custom_call" | custom-call | tf_op jit(solution)/shard_map/pallas_call | solution.py:420
  35.2 5.5 %collective-permute-start.4 = (bf16[512,384]{1,0:T(8,128)(2,1)S(1)}, bf16[512,384]{1,0:T(8,128)(2,1)S(1)}, u32[]{:S(2)}, u32[]{:S(2)}) collective-permute-start(bf16[512,384]{1,0:T(8,128)(2,1)S(1)} %get-tuple-element.15), channel_id=1, source_target_pairs={{1,2},{3,4},{5,6},{7,8},{9,10},{11,12},{13,14},{2,1},{4,3},{6,5},{... | collective-permute-start | bytes 1179656 | tf_op jit(solution)/shard_map/ppermute | solution.py:433
  40.7 0.0 collective-permute-done.got_ref
  40.7 0.0 copy-done.8
  40.7 0.0 copy-done.9
  40.7 0.0 copy-done.11
  40.7 0.0 copy-start.6
  40.7 0.0 copy-start.7
  40.8 4.0 %shard_map.118.base_ref = f32[512,768]{1,0:T(8,128)S(1)} custom-call(f32[32,32,384]{2,1,0:T(8,128)S(1)} %copy-done.4, f32[32,16,384]{2,1,0:T(8,128)} %collective-permute-done.got_ref, f32[1,32]{1,0:T(1,128)S(1)} %bitcast.9, bf16[768,768]{1,0:T(8,128)(2,1)S(1)} %copy-done.8, bf16[768,768]{1,0:T(8,128)(2,1)S(1)} %copy-done.9), custom_call_target="tpu_custom_call" | custom-call | tf_op jit(solution)/shard_map/pallas_call | solution.py:411
  44.7 1.3 %collective-permute-done.4.got_ref = bf16[512,384]{1,0:T(8,128)(2,1)S(1)} collective-permute-done((bf16[512,384]{1,0:T(8,128)(2,1)S(1)}, bf16[512,384]{1,0:T(8,128)(2,1)S(1)}, u32[]{:S(2)}, u32[]{:S(2)}) %collective-permute-start.4) | collective-permute-done | bytes 393248 | tf_op jit(solution)/shard_map/ppermute | solution.py:433
  46.1 0.0 copy-done.6
  46.1 0.0 copy-done.7
  46.1 1.9 %shard_map.121 = (f32[512,768]{1,0:T(8,128)S(1)}, bf16[64,768]{1,0:T(8,128)(2,1)S(1)}, bf16[64,768]{1,0:T(8,128)(2,1)S(1)}) custom-call(f32[512,768]{1,0:T(8,128)S(1)} %shard_map.118.base_ref, bf16[512,384]{1,0:T(8,128)(2,1)S(1)} %get-tuple-element.14.keep_ref, bf16[512,384]{1,0:T(8,128)(2,1)S(1)} %collective-permute-done.4.got_ref, f32[1,32]{1,0:T(1,128)S(1)} %bitcast.10, ...), custom_call_target="tpu_custom_call" | custom-call | tf_op jit(solution)/shard_map/pallas_call | solution.py:436
  47.9 4.9 %collective-permute-start.5 = (bf16[64,768]{1,0:T(8,128)(2,1)S(1)}, bf16[64,768]{1,0:T(8,128)(2,1)S(1)}, u32[]{:S(2)}, u32[]{:S(2)}) collective-permute-start(bf16[64,768]{1,0:T(8,128)(2,1)S(1)} %get-tuple-element.17), channel_id=1, source_target_pairs={{0,1},{1,0},{2,3},{3,2},{4,5},{5,4},{6,7},{7,6},{8,9},{9,8},{10,11... | collective-permute-start | bytes 294920 | tf_op jit(solution)/shard_map/ppermute | solution.py:443
  52.8 3.7 %collective-permute-start.6 = (bf16[64,768]{1,0:T(8,128)(2,1)S(1)}, bf16[64,768]{1,0:T(8,128)(2,1)S(1)}, u32[]{:S(2)}, u32[]{:S(2)}) collective-permute-start(bf16[64,768]{1,0:T(8,128)(2,1)S(1)} %get-tuple-element.18), channel_id=1, source_target_pairs={{1,2},{3,4},{5,6},{7,8},{9,10},{11,12},{13,14},{2,1},{4,3},{6,5},{... | collective-permute-start | bytes 294920 | tf_op jit(solution)/shard_map/ppermute | solution.py:442
  56.5 0.0 collective-permute-done.5.lon_ref
  56.5 3.1 %collective-permute-done.6.lat_ref = bf16[64,768]{1,0:T(8,128)(2,1)S(1)} collective-permute-done((bf16[64,768]{1,0:T(8,128)(2,1)S(1)}, bf16[64,768]{1,0:T(8,128)(2,1)S(1)}, u32[]{:S(2)}, u32[]{:S(2)}) %collective-permute-start.6) | collective-permute-done | bytes 98336 | tf_op jit(solution)/shard_map/ppermute | solution.py:442
  59.6 5.8 %shard_map.122 = f32[32,16,768]{2,1,0:T(8,128)} custom-call(f32[512,768]{1,0:T(8,128)S(1)} %get-tuple-element.16.field_ref, bf16[64,768]{1,0:T(8,128)(2,1)S(1)} %collective-permute-done.5.lon_ref, bf16[64,768]{1,0:T(8,128)(2,1)S(1)} %collective-permute-done.6.lat_ref), custom_call_target="tpu_custom_call" | custom-call | tf_op jit(solution)/shard_map/pallas_call | solution.py:445
  (1 shorter events, 0.0 us)
Async XLA Ops:
  0.0 2.5 %copy-start.4 = (f32[32,32,384]{2,1,0:T(8,128)S(1)}, f32[32,32,384]{2,1,0:T(8,128)}, u32[]{:S(2)}) copy-start(f32[32,32,384]{2,1,0:T(8,128)} %state_ref.1) | copy-start | bytes 4718596
  0.0 5.4 %copy-start.3 = (bf16[8,96,1024]{2,1,0:T(8,128)(2,1)S(1)}, bf16[8,96,1024]{2,1,0:T(8,128)(2,1)}, u32[]{:S(2)}) copy-start(bf16[8,96,1024]{2,1,0:T(8,128)(2,1)} %tok_ref.1) | copy-start | bytes 4718596
  2.2 19.3 %collective-permute-start.1 = (bf16[4,96,1024]{2,1,0:T(8,128)(2,1)}, bf16[4,96,1024]{2,1,0:T(8,128)(2,1)}, u32[]{:S(2)}, u32[]{:S(2)}) collective-permute-start(bf16[4,96,1024]{2,1,0:T(8,128)(2,1)} %constant_dynamic-slice_fusion.2), channel_id=1, source_target_pairs={{0,2},{2,4},{4,6},{6,8},{8,10},{10,12},{12,14},{14,15},{3,1},{5,3}... | collective-permute-start | bytes 2359304 | tf_op jit(solution)/shard_map/ppermute | solution.py:387
  3.4 37.3 %collective-permute-start = (f32[32,16,384]{2,1,0:T(8,128)}, f32[32,16,384]{2,1,0:T(8,128)}, u32[]{:S(2)}, u32[]{:S(2)}) collective-permute-start(f32[32,16,384]{2,1,0:T(8,128)} %constant_dynamic-slice_fusion.3), channel_id=1, source_target_pairs={{0,1},{1,0},{2,3},{3,2},{4,5},{5,4},{6,7},{7,6},{8,9},{9,8},{10,11... | collective-permute-start | bytes 2359304 | tf_op jit(solution)/shard_map/ppermute | solution.py:391
  5.4 10.1 %collective-permute-start.3 = (bf16[4,8,1024]{2,1,0:T(8,128)(2,1)S(1)}, bf16[4,8,1024]{2,1,0:T(8,128)(2,1)S(1)}, u32[]{:S(2)}, u32[]{:S(2)}) collective-permute-start(bf16[4,8,1024]{2,1,0:T(8,128)(2,1)S(1)} %get-tuple-element.19), channel_id=1, source_target_pairs={{0,1},{1,0},{2,3},{3,2},{4,5},{5,4},{6,7},{7,6},{8,9},{9,8},{10,11... | collective-permute-start | bytes 196616 | tf_op jit(solution)/shard_map/ppermute | solution.py:388
  5.5 15.3 %collective-permute-start.2 = (bf16[4,8,1024]{2,1,0:T(8,128)(2,1)S(1)}, bf16[4,8,1024]{2,1,0:T(8,128)(2,1)S(1)}, u32[]{:S(2)}, u32[]{:S(2)}) collective-permute-start(bf16[4,8,1024]{2,1,0:T(8,128)(2,1)S(1)} %get-tuple-element.20), channel_id=1, source_target_pairs={{1,2},{3,4},{5,6},{7,8},{9,10},{11,12},{13,14},{2,1},{4,3},{6,5},{... | collective-permute-start | bytes 196616 | tf_op jit(solution)/shard_map/ppermute | solution.py:389
  11.3 4.2 %copy-start.10 = (f32[1024]{0:T(1024)S(1)}, f32[1024]{0:T(1024)}, u32[]{:S(2)}) copy-start(f32[1024]{0:T(1024)} %param.13) | copy-start | bytes 12292
  13.5 2.0 %copy-start.2 = (bf16[1024,1024]{1,0:T(8,128)(2,1)S(1)}, bf16[1024,1024]{1,0:T(8,128)(2,1)}, u32[]{:S(2)}) copy-start(bf16[1024,1024]{1,0:T(8,128)(2,1)} %wq_ref.3) | copy-start | bytes 6291460
  15.5 2.2 %copy-start = (bf16[1024,2048]{1,0:T(8,128)(2,1)S(1)}, bf16[1024,2048]{1,0:T(8,128)(2,1)}, u32[]{:S(2)}) copy-start(bf16[1024,2048]{1,0:T(8,128)(2,1)} %wkv_ref.3) | copy-start | bytes 12582916
  17.7 3.8 %copy-start.1 = (bf16[1024,2048]{1,0:T(8,128)(2,1)S(1)}, bf16[1024,2048]{1,0:T(8,128)(2,1)}, u32[]{:S(2)}) copy-start(bf16[1024,2048]{1,0:T(8,128)(2,1)} %wkv_ref.3) | copy-start | bytes 12582916
  17.7 3.8 %copy-start.5 = (bf16[1024,1024]{1,0:T(8,128)(2,1)S(1)}, bf16[1024,1024]{1,0:T(8,128)(2,1)}, u32[]{:S(2)}) copy-start(bf16[1024,1024]{1,0:T(8,128)(2,1)} %wout_ref.1) | copy-start | bytes 6291460
  21.5 19.2 %copy-start.8 = (bf16[768,768]{1,0:T(8,128)(2,1)S(1)}, bf16[768,768]{1,0:T(8,128)(2,1)}, u32[]{:S(2)}) copy-start(bf16[768,768]{1,0:T(8,128)(2,1)} %constant.24.clone.high_ref) | copy-start | bytes 3538948
  21.5 19.2 %copy-start.9 = (bf16[768,768]{1,0:T(8,128)(2,1)S(1)}, bf16[768,768]{1,0:T(8,128)(2,1)}, u32[]{:S(2)}) copy-start(bf16[768,768]{1,0:T(8,128)(2,1)} %constant.25.clone.low_ref) | copy-start | bytes 3538948
  21.5 19.2 %copy-start.11 = (f32[32]{0:T(128)S(1)}, f32[32]{0:T(128)}, u32[]{:S(2)}) copy-start(f32[32]{0:T(128)} %param.18) | copy-start | bytes 388
  35.2 10.9 %collective-permute-start.4 = (bf16[512,384]{1,0:T(8,128)(2,1)S(1)}, bf16[512,384]{1,0:T(8,128)(2,1)S(1)}, u32[]{:S(2)}, u32[]{:S(2)}) collective-permute-start(bf16[512,384]{1,0:T(8,128)(2,1)S(1)} %get-tuple-element.15), channel_id=1, source_target_pairs={{1,2},{3,4},{5,6},{7,8},{9,10},{11,12},{13,14},{2,1},{4,3},{6,5},{... | collective-permute-start | bytes 1179656 | tf_op jit(solution)/shard_map/ppermute | solution.py:433
  40.7 5.3 %copy-start.6 = (bf16[2,384,768]{2,1,0:T(8,128)(2,1)S(1)}, bf16[2,384,768]{2,1,0:T(8,128)(2,1)}, u32[]{:S(2)}) copy-start(bf16[2,384,768]{2,1,0:T(8,128)(2,1)} %constant.26.clone.high_ref) | copy-start | bytes 3538948
  40.7 5.3 %copy-start.7 = (bf16[2,384,768]{2,1,0:T(8,128)(2,1)S(1)}, bf16[2,384,768]{2,1,0:T(8,128)(2,1)}, u32[]{:S(2)}) copy-start(bf16[2,384,768]{2,1,0:T(8,128)(2,1)} %constant.27.clone.low_ref) | copy-start | bytes 3538948
  47.9 8.5 %collective-permute-start.5 = (bf16[64,768]{1,0:T(8,128)(2,1)S(1)}, bf16[64,768]{1,0:T(8,128)(2,1)S(1)}, u32[]{:S(2)}, u32[]{:S(2)}) collective-permute-start(bf16[64,768]{1,0:T(8,128)(2,1)S(1)} %get-tuple-element.17), channel_id=1, source_target_pairs={{0,1},{1,0},{2,3},{3,2},{4,5},{5,4},{6,7},{7,6},{8,9},{9,8},{10,11... | collective-permute-start | bytes 294920 | tf_op jit(solution)/shard_map/ppermute | solution.py:443
  52.8 6.8 %collective-permute-start.6 = (bf16[64,768]{1,0:T(8,128)(2,1)S(1)}, bf16[64,768]{1,0:T(8,128)(2,1)S(1)}, u32[]{:S(2)}, u32[]{:S(2)}) collective-permute-start(bf16[64,768]{1,0:T(8,128)(2,1)S(1)} %get-tuple-element.18), channel_id=1, source_target_pairs={{1,2},{3,4},{5,6},{7,8},{9,10},{11,12},{13,14},{2,1},{4,3},{6,5},{... | collective-permute-start | bytes 294920 | tf_op jit(solution)/shard_map/ppermute | solution.py:442

commit v3 on v2

v3 whole, which is shorter than its diff:
```python
import functools
import math

import jax
import jax.numpy as jnp
import ml_dtypes
import numpy as np
from jax import lax
from jax.experimental import pallas as pl
from jax.experimental.pallas import tpu as pltpu
from jax.sharding import PartitionSpec as P

HEADS = 16
WIN = 8
PATCH = 4
VARS = 4
LEV = 8
KEEP = 256

time_step = 0.1
diffusion = 0.5
epsilon = 1e-05
HALF = WIN // 2
GROUP = 4
MIB = 1 << 20
F32 = jnp.float32
BF16 = jnp.bfloat16


def zonal_filter(length, kept_waves):
    lag = np.arange(length, dtype=np.float64)
    waves = np.arange(1, kept_waves, dtype=np.float64)
    kernel = 1.0 + 2.0 * np.cos(2.0 * np.pi / length * lag[:, None] * waves[None, :]).sum(1)
    at = (np.arange(length)[:, None] - np.arange(length)[None, :]) % length
    return (kernel / length)[at]


def split_high_low(matrix):
    high = matrix.astype(ml_dtypes.bfloat16)
    low = (matrix - high.astype(np.float64)).astype(ml_dtypes.bfloat16)
    return high, low


def decoded_order(total_cols, parts):
    cols = total_cols // parts
    group_cols = GROUP * WIN
    rows = []
    for part in range(parts):
        lanes = []
        for group in range(cols // group_cols):
            for b in range(PATCH):
                for place in range(group_cols):
                    col = part * cols + group * group_cols + place
                    if place % WIN < HALF:
                        col += WIN
                    lanes.append((col % total_cols) * PATCH + b)
        rows.append(lanes)
    return np.array(rows)


def place():
    lat, lon = lax.axis_index("lat"), lax.axis_index("lon")
    return lon, ((lat == 0) & (lon == 0)) | ((lat == lax.axis_size("lat") - 1) & (lon == 1))


def nudge_column(nudge_ref, rows):
    channels = nudge_ref.shape[1]
    picked = lax.broadcasted_iota(jnp.int32, (rows, channels), 0) % channels == lax.broadcasted_iota(
        jnp.int32, (rows, channels), 1
    )
    return jnp.sum(jnp.where(picked, nudge_ref[...], 0.0), axis=1, keepdims=True)


def dot(a, b):
    return lax.dot_general(a, b, (((1,), (0,)), ((), ())), preferred_element_type=F32)


def dot_nt(a, b):
    return lax.dot_general(a, b, (((1,), (1,)), ((), ())), preferred_element_type=F32)


def window_tokens(load, first, cols, emit):
    lead = lax.broadcasted_iota(jnp.int32, (2 * WIN, 1), 0) % WIN < HALF
    for pair in range(cols // (2 * WIN)):
        col = first + pair * 2 * WIN
        for r in range(HALF):
            here = load(r, col, 2 * WIN).astype(F32)
            after = load(r, col + 2 * WIN, WIN).astype(F32)
            emit(pair, r, jnp.where(lead, jnp.concatenate([here[WIN:], after], axis=0), here))


def normalise(block, gain):
    centred = block - jnp.mean(block, axis=-1, keepdims=True)
    variance = jnp.mean(centred * centred, axis=-1, keepdims=True)
    return centred * lax.rsqrt(variance + epsilon) * gain


def place_tokens(load, first, cols, gain, raw_ref, normed_ref):
    held = {}

    def emit(pair, r, block):
        group, inside = divmod(pair * 2, GROUP)
        at = (group * HALF + r) * GROUP * WIN + inside * WIN
        raw_ref[at : at + 2 * WIN, :] = block.astype(BF16)
        held[r % 2] = normalise(block, gain)
        if r % 2:
            for side in range(2):
                part = slice(side * WIN, (side + 1) * WIN)
                at = (2 * pair + side) * WIN * HALF + (r - 1) * WIN
                both = jnp.concatenate([held[0][part], held[1][part]], axis=0)
                normed_ref[at : at + 2 * WIN, :] = both.astype(BF16)

    window_tokens(load, first, cols, emit)


def project(normed_ref, wq_ref, wkv_ref, qkv_ref, copies=()):
    width = wq_ref.shape[0]
    normed = normed_ref[...]
    for i in range(3):
        if copies:
            copies[i].wait()
        weights = wq_ref[...] if i == 0 else wkv_ref[:, (i - 1) * width : i * width]
        qkv_ref[:, i * width : (i + 1) * width] = dot(normed, weights).astype(BF16)


def run_copies(sems, pairs):
    copies = [pltpu.make_async_copy(source, target, sems.at[i]) for i, (source, target) in enumerate(pairs)]
    for copy in copies:
        copy.start()
    return copies


def pack_kernel(pieces, tok_ref, state_ref, *refs):
    *give_refs, edge_ref, give_state_ref, sems = refs
    lon = place()[0]
    rows = give_state_ref.shape[1]
    pairs = []
    for give_ref, (start, size) in zip(give_refs, pieces):
        pairs.append((tok_ref.at[pl.ds(HALF * (1 - lon), HALF), pl.ds(start, size), :], give_ref))
    pairs.append((tok_ref.at[:, pl.ds(0, edge_ref.shape[1]), :], edge_ref))
    pairs.append((state_ref.at[:, pl.ds(pl.multiple_of(rows * (1 - lon), 8), rows), :], give_state_ref))
    for copy in run_copies(sems, pairs):
        copy.wait()


def own_kernel(
    tok_hbm,
    edge_ref,
    gain_ref,
    wq_hbm,
    wkv_hbm,
    wout_hbm,
    wdec_hbm,
    qkv_ref,
    wdec_t_ref,
    wmix_t_ref,
    decoded_ref,
    wq_ref,
    wkv_ref,
    tok_ref,
    raw_ref,
    normed_ref,
    wdec_ref,
    wout_ref,
    sems,
):
    lon = place()[0]
    cols = tok_ref.shape[1]
    width = wq_ref.shape[0]
    keys, values = pl.ds(0, width), pl.ds(width, width)
    own_rows = pl.ds(HALF * lon, HALF)
    copies = run_copies(
        sems,
        [
            (tok_hbm.at[own_rows], tok_ref),
            (wq_hbm, wq_ref),
            (wkv_hbm.at[:, keys], wkv_ref.at[:, keys]),
            (wkv_hbm.at[:, values], wkv_ref.at[:, values]),
            (wdec_hbm, wdec_ref),
            (wout_hbm, wout_ref),
        ],
    )

    def load(r, c, size):
        if c == cols:
            return edge_ref[HALF * lon + r, :size, :]
        return tok_ref[r, c : c + size, :]

    copies[0].wait()
    place_tokens(load, 0, cols, gain_ref[...], raw_ref, normed_ref)
    project(normed_ref, wq_ref, wkv_ref, qkv_ref, copies[1:4])
    outs = wdec_ref.shape[1]
    band = outs // PATCH
    channels = band // PATCH
    row = lax.broadcasted_iota(jnp.int32, (outs, 1), 0)
    source = (row % channels) * PATCH * PATCH + (row % band // channels) * PATCH + row // band
    pick = (lax.broadcasted_iota(jnp.int32, (outs, outs), 1) == source).astype(F32).astype(BF16)
    copies[4].wait()
    wdec_t_ref[...] = dot_nt(pick, wdec_ref[...]).astype(BF16)
    decoded_ref[...] = dot_nt(wdec_t_ref[...], raw_ref[...])
    copies[5].wait()
    wmix_t_ref[...] = dot_nt(wdec_t_ref[...], wout_ref[...]).astype(BF16)


def main_kernel(first, starts, *refs):
    x_refs, refs = refs[: len(starts)], refs[len(starts) :]
    gain_ref, qkv_own_ref, decoded_own_ref, wq_ref, wkv_ref, wmix_ref, wdec_ref, *refs = refs
    keep_ref, send_ref, raw_ref, normed_ref, qkv_ref, att_ref, decoded_ref = refs
    width = raw_ref.shape[1]
    head_size = width // HEADS
    half_cells = HALF * WIN
    cells = 2 * half_cells
    lanes = 4 * head_size
    quads = HEADS // 4
    cols = raw_ref.shape[0] // HALF
    base = first * HALF
    group_cols = GROUP * WIN
    group_half = GROUP * half_cells

    def load(r, c, size):
        which = max(i for i in range(len(starts)) if starts[i] <= c)
        return x_refs[which][r, c - starts[which] : c - starts[which] + size, :]

    def iota(shape, dim):
        return lax.broadcasted_iota(jnp.int32, shape, dim)

    blocks = (iota((lanes, lanes), 0) // head_size == iota((lanes, lanes), 1) // head_size).astype(F32).astype(BF16)
    split_rows = iota((cells, 2 * cells), 0) // half_cells != iota((cells, 2 * cells), 1) % cells // half_cells
    bias = jnp.where(split_rows & place()[1], -1e30, 0.0)
    first_head = iota((cells, 2 * cells), 1) < cells
    scale = 1.0 / (math.sqrt(head_size) * math.log(2.0))

    def project_quad(quad):
        normed = normed_ref[...]
        at = quad * lanes
        for offset, weights in (
            (0, wq_ref[:, at : at + lanes]),
            (width, wkv_ref[:, at : at + lanes]),
            (2 * width, wkv_ref[:, width + at : width + at + lanes]),
        ):
            qkv_ref[:, offset + at : offset + at + lanes] = dot(normed, weights).astype(BF16)

    def part(window, quad, offset):
        columns = slice(offset + quad * lanes, offset + (quad + 1) * lanes)
        got = slice(window * half_cells, (window + 1) * half_cells)
        own = slice(base + got.start, base + got.stop)
        return jnp.concatenate([qkv_own_ref[own, columns], qkv_ref[got, columns]], axis=0)

    def score(window, quad):
        keys = jnp.concatenate([part(window, quad, width)] * 4, axis=0) * blocks
        return dot_nt(part(window, quad, 0), keys)

    def weigh(scores):
        outs = []
        for side in range(2):
            two = scores[:, side * 2 * cells : (side + 1) * 2 * cells] + bias
            left = jnp.max(jnp.where(first_head, two, -jnp.inf), axis=-1, keepdims=True)
            right = jnp.max(jnp.where(first_head, -jnp.inf, two), axis=-1, keepdims=True)
            peak = jnp.where(first_head, left, right)
            outs.append(jnp.exp2((two - peak) * scale).astype(BF16))
        return jnp.concatenate(outs, axis=1)

    def mix(group, quad, weights):
        sums = dot(jnp.concatenate(weights, axis=0), blocks)
        mixed = []
        for i in range(GROUP):
            values = jnp.concatenate([part(group * GROUP + i, quad, 2 * width)] * 4, axis=0) * blocks
            mixed.append(dot(weights[i], values) / sums[i * cells : (i + 1) * cells])
        tiles = [mixed[i][at : at + WIN] for at in range(0, cells, WIN) for i in range(GROUP)]
        rows = slice(group * 2 * group_half, (group + 1) * 2 * group_half)
        att_ref[rows, quad * lanes : (quad + 1) * lanes] = jnp.concatenate(tiles, axis=0).astype(BF16)

    def decode(group):
        rows = slice(group * 2 * group_half, (group + 1) * 2 * group_half)
        decoded = dot_nt(wmix_ref[...], att_ref[rows, :])
        got = slice(group * group_half, (group + 1) * group_half)
        own = slice(base + got.start, base + got.stop)
        band = decoded.shape[0] // PATCH
        out_lanes = slice(group * group_cols * PATCH, (group + 1) * group_cols * PATCH)
        lane_part = iota((band, group_half), 1) // group_cols
        for half, more, out_ref in ((0, decoded_own_ref[:, own], keep_ref), (1, decoded_ref[:, got], send_ref)):
            total = decoded[:, half * group_half : (half + 1) * group_half] + more
            from_b = [total[b * band : (b + 1) * band] for b in range(PATCH)]
            for r in range(HALF):
                placed = None
                for b in range(PATCH):
                    moved = from_b[b]
                    if b != r:
                        moved = pltpu.roll(moved, (b - r) % PATCH * group_cols, axis=1)
                    placed = moved if placed is None else jnp.where(lane_part == b, moved, placed)
                out_ref[r * band : (r + 1) * band, out_lanes] = placed.astype(BF16)

    place_tokens(load, first, cols, gain_ref[...], raw_ref, normed_ref)
    project_quad(0)
    units = [(group, quad) for group in range(cols // group_cols) for quad in range(quads)]
    weights = None
    for i in range(len(units) + 1):
        if i < len(units):
            group, quad = units[i]
            scores = [score(group * GROUP + w, quad) for w in range(GROUP)]
            if group == 0 and quad + 1 < quads:
                project_quad(quad + 1)
            if i == quads - 1:
                decoded_ref[...] = dot_nt(wdec_ref[...], raw_ref[...])
        if i > 0:
            mix(*units[i - 1], weights)
            if units[i - 1][1] == quads - 1:
                decode(units[i - 1][0])
        if i < len(units):
            weights = [weigh(x) for x in scores]

    lon = place()[0]
    total_rows = keep_ref.shape[0]
    edge = send_ref.shape[0] - total_rows
    near = pl.ds(pl.multiple_of(lon * (total_rows - edge), edge), edge)
    send_ref[total_rows:, :] = keep_ref[near, :]


def unfiltered(field, high_ref, low_ref, strength):
    high = field.astype(BF16)
    low = (field - high.astype(F32)).astype(BF16)
    smooth = dot(high, high_ref[...]) + (dot(high, low_ref[...]) + dot(low, high_ref[...]))
    return field - strength * smooth


def state_kernel(state_ref, got_ref, nudge_ref, high_ref, low_ref, out_ref, edge_ref, whole_ref):
    lon = place()[0]
    channels, own_rows, cols = got_ref.shape
    own_lanes = pl.ds(pl.multiple_of(lon * cols, 128), cols)
    got_lanes = pl.ds(pl.multiple_of((1 - lon) * cols, 128), cols)
    for y in range(0, own_rows, 8):
        own_part = pl.ds(pl.multiple_of(lon * own_rows + y, 8), 8)
        for ch in range(0, channels, 8):
            own = jnp.swapaxes(state_ref[ch : ch + 8, own_part, :], 0, 1)
            got = jnp.swapaxes(got_ref[ch : ch + 8, y : y + 8, :], 0, 1)
            for i in range(8):
                rows = slice((y + i) * channels + ch, (y + i) * channels + ch + 8)
                whole_ref[rows, own_lanes] = own[i]
                whole_ref[rows, got_lanes] = got[i]
    step = PATCH * channels
    strength = nudge_column(nudge_ref, step)
    for at in range(0, out_ref.shape[0], step):
        out_ref[at : at + step, :] = unfiltered(whole_ref[at : at + step, :], high_ref, low_ref, strength)
    edge = edge_ref.shape[0]
    near = pl.ds(pl.multiple_of(lon * (out_ref.shape[0] - edge), edge), edge)
    edge_ref[...] = out_ref[near, :].astype(BF16)


def filter_rows(dec, first, high_ref, low_ref):
    rows = pl.ds(pl.multiple_of(first, 128), dec.shape[1])
    return dot(dec, high_ref[rows, :]) + dot(dec, low_ref[rows, :])


def early_kernel(chunks, base_ref, base_edge_ref, nudge_ref, high_ref, low_ref, *refs):
    keep_refs, send_refs, got_refs, out_ref = refs[:chunks], refs[chunks : 2 * chunks], refs[2 * chunks : -1], refs[-1]
    lon = place()[0]
    total = base_ref.shape[0]
    edge = base_edge_ref.shape[0]
    far = pl.ds(pl.multiple_of((1 - lon) * (total - edge), edge), edge)
    own = [jnp.concatenate([keep[...], send[far, :]], axis=0) for keep, send in zip(keep_refs, send_refs)]
    decoded = jnp.concatenate(own + [got[...] for got in got_refs], axis=1)
    smooth = filter_rows(decoded, lon * (high_ref.shape[0] // 3), high_ref, low_ref)
    step = PATCH * nudge_ref.shape[1]
    strength = nudge_column(nudge_ref, step)
    for at in range(0, total, step):
        out_ref[at : at + step, :] = base_ref[at : at + step, :] + strength * smooth[at : at + step]
    out_ref[total:, :] = base_edge_ref[...].astype(F32) + strength[:edge] * smooth[total:]


def late_kernel(early_ref, got_ref, nudge_ref, high_ref, low_ref, out_ref, near_ref, lat_ref):
    lon = place()[0]
    total = out_ref.shape[0]
    edge = lat_ref.shape[0]
    part = high_ref.shape[0] // 3
    smooth = filter_rows(got_ref[...], lon * part + 2 * part - got_ref.shape[1], high_ref, low_ref)
    step = PATCH * nudge_ref.shape[1]
    strength = nudge_column(nudge_ref, step)
    for at in range(0, total, step):
        out_ref[at : at + step, :] = early_ref[at : at + step, :] + strength * smooth[at : at + step]
    lat_ref[...] = early_ref[total:, :] + strength[:edge] * smooth[total:]
    far = pl.ds(pl.multiple_of((1 - lon) * (total - edge), edge), edge)
    near_ref[...] = out_ref[far, :].astype(BF16)


def row_tile(ref, row, var):
    at = row * (VARS * LEV) + var * LEV
    return pl.ds(at if isinstance(at, int) else pl.multiple_of(at, LEV), LEV)


def tendency_row(south, centre, north, use):
    push_u, push_v = (0.5 * time_step) * centre(0), (0.5 * time_step) * centre(1)
    calm = diffusion * time_step
    to_east, to_west, to_north, to_south = calm - push_u, calm + push_u, calm - push_v, calm + push_v
    for var in range(VARS):
        field = centre(var)
        length = field.shape[1]
        step = to_east * pltpu.roll(field, length - 1, axis=1) + to_west * pltpu.roll(field, 1, axis=1)
        step = step + (to_north * north(var) + to_south * south(var))
        use(var, field, step - (4.0 * calm) * field)


def inner_kernel(field_ref, first_ref, last_ref):
    rows = field_ref.shape[0] // (VARS * LEV)

    def reader(ref, row):
        return lambda var: ref[row_tile(ref, row, var), :]

    def section(ref, row, use):
        tendency_row(reader(ref, row - 1), reader(ref, row), reader(ref, row + 1), use)

    def first_row(row, _):
        def put(var, field, step):
            first_ref[row_tile(first_ref, row, var), :] = field + step

        section(field_ref, row, put)
        return 0

    def last_row(row, _):
        def put(var, field, step):
            nudged = field_ref[row_tile(field_ref, row, var), :]
            last_ref[row_tile(last_ref, row, var), :] = 0.5 * (nudged + field + step)

        section(first_ref, row, put)
        return 0

    lax.fori_loop(1, rows - 1, first_row, 0)
    lax.fori_loop(2, rows - 2, last_row, 0)


def outer_kernel(field_ref, first_ref, last_ref, lon_ref, lat_ref, out_ref, ext_ref, edge_ref):
    channels, rows, length = out_ref.shape
    lon, pole = place()
    is_top = lon == 0
    from_lon = lon_ref[...].astype(F32)
    from_lat = jnp.where(pole, 0.0, lat_ref[...])
    edge = from_lon.shape[0]
    ext_ref[:edge, :] = jnp.where(is_top, from_lat, from_lon)
    ext_ref[edge:, :] = jnp.where(is_top, from_lon, from_lat)

    def field(row):
        def read(var):
            if row < 0:
                return ext_ref[row_tile(ext_ref, row + 2, var), :]
            if row >= rows:
                return ext_ref[row_tile(ext_ref, row - rows + 2, var), :]
            return field_ref[row_tile(field_ref, row, var), :]

        return read

    def first(row):
        def read(var):
            if row < 1:
                return edge_ref[row_tile(edge_ref, row + 1, var), :]
            if row >= rows - 1:
                return edge_ref[row_tile(edge_ref, row - rows + 3, var), :]
            return first_ref[row_tile(first_ref, row, var), :]

        return read

    outside = jnp.where(pole, 0.0, 1.0)
    for row in (-1, 0, rows - 1, rows):
        keep = None
        if row < 0:
            keep = jnp.where(is_top, outside, 1.0)
        if row >= rows:
            keep = jnp.where(is_top, 1.0, outside)

        def put(var, value, step):
            total = value + step
            at = row + 1 if row < 1 else row - rows + 3
            edge_ref[row_tile(edge_ref, at, var), :] = total if keep is None else total * keep

        tendency_row(field(row - 1), field(row), field(row + 1), put)
    outer = {}
    for row in (0, 1, rows - 2, rows - 1):

        def put(var, value, step):
            outer[row, var] = 0.5 * (field(row)(var) + value + step)

        tendency_row(first(row - 1), first(row), first(row + 1), put)
    for y in range(0, rows, 8):
        for var in range(VARS):
            block = []
            for row in range(y, y + 8):
                tile = outer[row, var] if (row, var) in outer else last_ref[row_tile(last_ref, row, var), :]
                block.append(tile[None])
            out_ref[var * LEV : (var + 1) * LEV, y : y + 8, :] = jnp.swapaxes(jnp.concatenate(block, axis=0), 0, 1)


def work(micros):
    return pl.CostEstimate(flops=int(micros * 1e9), bytes_accessed=int(micros * 1e6), transcendentals=0)


def call(kernel, out_shape, n_in, scratch=(), vmem=24, micros=1.0):
    vmem_spec = pl.BlockSpec(memory_space=pltpu.VMEM)
    many = isinstance(out_shape, (tuple, list))
    return pl.pallas_call(
        kernel,
        out_shape=out_shape,
        in_specs=[vmem_spec] * n_in,
        out_specs=[vmem_spec] * len(out_shape) if many else vmem_spec,
        scratch_shapes=list(scratch),
        cost_estimate=work(micros),
        compiler_params=pltpu.CompilerParams(vmem_limit_bytes=vmem * MIB),
    )


def body(tokens, ln_gain, w_query, w_keyval, w_out, w_dec, nudge, state):
    tok_rows, tok_cols, width = tokens.shape
    channels, state_rows, state_cols = state.shape
    n_lat, n_lon = lax.axis_size("lat"), lax.axis_size("lon")
    lon = lax.axis_index("lon")
    total_cols = tok_cols * n_lon
    length = state_cols * n_lon
    band_rows = state_rows // n_lon
    both = ("lat", "lon")
    tokens_half = tok_cols * HALF
    band = band_rows * channels


    def at(row, col):
        return row * n_lon + col

    last = n_lat - 1
    swap = [(0, 1), (1, 0)]
    shift = [(at(i, 0), at(i + 1, 0)) for i in range(last)] + [(at(last, 0), at(last, 1))]
    shift += [(at(i, 1), at(i - 1, 1)) for i in range(1, n_lat)] + [(at(0, 1), at(0, 0))]
    meet = [(at(i, 1), at(i + 1, 0)) for i in range(last)] + [(at(i + 1, 0), at(i, 1)) for i in range(last)]
    meet_all = meet + [(at(0, 0), at(0, 0)), (at(last, 1), at(last, 1))]

    step = GROUP * WIN
    split = max(tok_cols - step, step)
    chunks = [(0, split)] + ([(split, step)] if split < tok_cols else [])
    cuts = [0] + [split + 2 * WIN] * (len(chunks) - 1) + [tok_cols]
    pieces = [(cuts[i], cuts[i + 1] - cuts[i]) for i in range(len(chunks))]

    hbm, vmem = pl.BlockSpec(memory_space=pltpu.HBM), pl.BlockSpec(memory_space=pltpu.VMEM)
    in_hbm = functools.partial(pltpu.with_memory_space_constraint, memory_space=pltpu.HBM)
    shapes = [pltpu.VMEM((HALF, size, width), BF16) for _, size in pieces]
    shapes.append(pltpu.VMEM((tok_rows, 2 * WIN, width), BF16))
    shapes.append(pltpu.VMEM((channels, band_rows, state_cols), F32))
    *give, give_edge, give_state = pl.pallas_call(
        functools.partial(pack_kernel, pieces),
        out_shape=shapes,
        in_specs=[hbm, hbm],
        out_specs=[vmem] * len(shapes),
        scratch_shapes=[pltpu.SemaphoreType.DMA((len(shapes),))],
        compiler_params=pltpu.CompilerParams(vmem_limit_bytes=8 * MIB),
    )(in_hbm(tokens), in_hbm(state))
    edge_tokens = lax.ppermute(give_edge, "lon", swap)
    their_edge = lax.dynamic_slice(edge_tokens, (HALF * (1 - lon), 0, 0), (HALF, WIN, width))
    give[-1] = jnp.concatenate([give[-1], their_edge], axis=1)
    got_tokens = [lax.ppermute(give[0], both, shift)]
    got_state = lax.ppermute(give_state, "lon", swap)

    gain = ln_gain[None, :]
    nudge_row = nudge[None, :]
    matrix = zonal_filter(length, KEEP)
    high, low = (jnp.asarray(m) for m in split_high_low(matrix))
    order = decoded_order(total_cols, n_lon)
    order = np.concatenate([order[0], order[1], order[0]])
    dec_high, dec_low = (jnp.asarray(m) for m in split_high_low(matrix[order]))

    n_out = w_dec.shape[1]
    qkv_own, w_dec_t, w_mix_t, decoded_own, *weights = pl.pallas_call(
        own_kernel,
        out_shape=[
            pltpu.VMEM((tokens_half, 3 * width), BF16),
            pltpu.VMEM((n_out, width), BF16),
            pltpu.VMEM((n_out, width), BF16),
            pltpu.VMEM((n_out, tokens_half), F32),
            pltpu.VMEM(w_query.shape, BF16),
            pltpu.VMEM(w_keyval.shape, BF16),
        ],
        in_specs=[hbm, vmem, vmem, hbm, hbm, hbm, hbm],
        out_specs=[vmem] * 6,
        scratch_shapes=[
            pltpu.VMEM((HALF, tok_cols, width), BF16),
            pltpu.VMEM((tokens_half, width), BF16),
            pltpu.VMEM((tokens_half, width), BF16),
            pltpu.VMEM(w_dec.shape, BF16),
            pltpu.VMEM(w_out.shape, BF16),
            pltpu.SemaphoreType.DMA((6,)),
        ],
        cost_estimate=work(7.5),
        compiler_params=pltpu.CompilerParams(vmem_limit_bytes=32 * MIB),
    )(in_hbm(tokens), edge_tokens, gain, in_hbm(w_query), in_hbm(w_keyval), in_hbm(w_out), in_hbm(w_dec))

    edge_rows = 2 * channels
    got_state, qkv_own = lax.optimization_barrier((got_state, qkv_own))
    base, base_edge = call(
        state_kernel,
        (pltpu.VMEM((band, length), F32), pltpu.VMEM((edge_rows, length), BF16)),
        5,
        [pltpu.VMEM((band, length), F32)],
        micros=2.7,
    )(state, got_state, nudge_row, high, low)
    got_base_edge = lax.ppermute(base_edge, both, meet)
    gain, base, *give[1:] = lax.optimization_barrier((gain, base, *give[1:]))
    got_tokens += [lax.ppermute(part, both, shift) for part in give[1:]]

    keep, send, got = [], [], []
    for i, (first, cols) in enumerate(chunks):
        kept, sent = call(
            functools.partial(main_kernel, first, cuts[: i + 1]),
            (pltpu.VMEM((band, cols * PATCH), BF16), pltpu.VMEM((band + edge_rows, cols * PATCH), BF16)),
            7 + i + 1,
            [
                pltpu.VMEM((cols * HALF, width), BF16),
                pltpu.VMEM((cols * HALF, width), BF16),
                pltpu.VMEM((cols * HALF, 3 * width), BF16),
                pltpu.VMEM((cols * WIN, width), BF16),
                pltpu.VMEM((n_out, cols * HALF), F32),
            ],
            micros=3.0 * (cols // step),
        )(*got_tokens[: i + 1], gain, qkv_own, decoded_own, *weights, w_mix_t, w_dec_t)
        gain, kept = lax.optimization_barrier((gain, kept))
        if i == 0:
            gain, got_base_edge = lax.optimization_barrier((gain, got_base_edge))
        keep.append(kept)
        send.append(sent)
        got.append(lax.ppermute(sent, both, meet_all))

    early = call(
        functools.partial(early_kernel, len(chunks)),
        pltpu.VMEM((band + edge_rows, length), F32),
        5 + 3 * len(chunks) - 1,
        micros=1.6,
    )(base, got_base_edge, nudge_row, dec_high, dec_low, *keep, *send, *got[:-1])
    nudged, to_lon, from_lat = call(
        late_kernel,
        (
            pltpu.VMEM((band, length), F32),
            pltpu.VMEM((edge_rows, length), BF16),
            pltpu.VMEM((edge_rows, length), F32),
        ),
        5,
    )(early, got[-1], nudge_row, dec_high, dec_low)
    from_lon = lax.ppermute(to_lon, "lon", swap)

    field = pltpu.VMEM((band, length), F32)
    first, last_rows = call(inner_kernel, (field, field), 1, micros=4.0)(nudged)
    return call(
        outer_kernel,
        jax.ShapeDtypeStruct((channels, band_rows, length), F32),
        5,
        [pltpu.VMEM((2 * edge_rows, length), F32), pltpu.VMEM((2 * edge_rows, length), F32)],
        micros=2.2,
    )(nudged, first, last_rows, from_lon, from_lat)


def solution(mesh):
    in_specs = (
        P(("member", "lat"), "lon", None),
        P(),
        P(),
        P(),
        P(),
        P(),
        P(),
        P(None, ("member", "lat"), "lon"),
    )
    out_specs = P(None, ("member", "lat", "lon"), None)
    return jax.shard_map(body, mesh=mesh, in_specs=in_specs, out_specs=out_specs, check_vma=False)
```

time: 66 us -> 46.8 us (0.71)
  local copies, waits for them, and re-layouts: 11.9 us -> 0.05 us
  starting transfers between devices: 19.8 us -> 13.1 us
  waiting for transfers between devices: 5.22 us -> 3.77 us
    unnamed x25 -> x14, local copies, waits for them, and re-layouts: 4.5 us -> 0.04 us
    ppermute x1, starting transfers between devices: 4.87 us -> 0.8 us  [body(): from_lon = lax.ppermute(to_lon, 'lon', swap)]
    dynamic_slice x2 -> x1, local copies, waits for them, and re-layouts: 3.19 us -> 0.01 us  [body(): lax.dynamic_slice(edge_tokens, (HALF * (1 - lon), 0, 0), (HALF, WIN, width))]
    reshape x1 -> x0, local copies, waits for them, and re-layouts: 2.26 us -> none  [body(): w_dec.reshape(width, channels, PATCH, PATCH).transpose(3, 2, 1, 0)]
    ppermute x5 -> x6, starting transfers between devices: 13 us -> 10.9 us  [the longest x2 6.46 us: body(): got.append(lax.ppermute(sent, both, meet_all))]
    transpose x1 -> x0, local copies, waits for them, and re-layouts: 1.95 us -> none  [body(): w_dec.reshape(width, channels, PATCH, PATCH).transpose(3, 2, 1, 0)]
    ppermute x5 -> x6, waiting for transfers between devices: 5.22 us -> 3.77 us  [the longest x2 3.76 us: body(): got.append(lax.ppermute(sent, both, meet_all))]
    pallas_call x5 -> x9, Pallas kernels: 28.3 us -> 28.9 us  [the longest x2 9.44 us: body(): call(functools.partial(main_kernel, first, cuts[:i + 1]), (pltpu.VMEM((ba...]
  transfers between devices with their start and end apart: 7 -> 8, of which waited for: 3 -> 1; matrix products, arithmetic and copies ran while one was open for 11% -> 0% of each run, Pallas kernels for 31% -> 54%
where the time goes in v3:
time: 46.8 us; the launch traced here: 46.1 us
  Pallas kernels  28.9 us (62%)
  starting transfers between devices  13.1 us (28%)
  waiting for transfers between devices  3.77 us (8%)
    pallas_call x2, Pallas kernels, body(): call(functools.partial(main_kernel, first, cuts[:i + 1]), (pltpu.VMEM((ba...  9.44 us
    pallas_call x1, Pallas kernels, body(): pl.pallas_call(own_kernel, out_shape=[pltpu.VMEM((tokens_half, 3 * width)...  7.76 us
    ppermute x2, starting transfers between devices, body(): got.append(lax.ppermute(sent, both, meet_all))  6.46 us
    ppermute x2, waiting for transfers between devices, body(): got.append(lax.ppermute(sent, both, meet_all))  3.76 us
    pallas_call x1, Pallas kernels, body(): first, last_rows = call(inner_kernel, (field, field), 1, micros=4.0)(nudged)  3.29 us
    ppermute x1, starting transfers between devices, body(): got_base_edge = lax.ppermute(base_edge, both, meet)  3.07 us
    pallas_call x1, Pallas kernels, body(): call(state_kernel, (pltpu.VMEM((band, length), F32), pltpu.VMEM((edge_row...  2.8 us
    pallas_call x1, Pallas kernels, body(): call(outer_kernel, jax.ShapeDtypeStruct((channels, band_rows, length), F3...  1.93 us
  transfers between devices with their start and end apart: 8, of which 1 were waited for; matrix products, arithmetic and copies ran while one was open for 0% of the time, Pallas kernels for 54%

profile of v3, /device:TPU:15, one launch (start us, length us, event | category | flops | bytes accessed | tf_op | source)
XLA Modules:
  0.0 46.1 jit_solution(1266893799595765901)
XLA Ops:
  0.0 0.0 copy-start.3
  0.0 1.5 %shard_map.118 = (bf16[4,80,1024]{2,1,0:T(8,128)(2,1)S(1)}, bf16[4,16,1024]{2,1,0:T(8,128)(2,1)S(1)}, bf16[8,16,1024]{2,1,0:T(8,128)(2,1)S(1)}, f32[32,16,384]{2,1,0:T(8,128)S(1)}) custom-call(bf16[8,96,1024]{2,1,0:T(8,128)(2,1)} %tok_hbm.1, f32[32,32,384]{2,1,0:T(8,128)} %state_ref.3), custom_call_target="tpu_custom_call" | custom-call | tf_op jit(solution)/shard_map/pallas_call | solution.py:542
  1.5 0.7 %collective-permute-start.1 = (bf16[8,16,1024]{2,1,0:T(8,128)(2,1)S(1)}, bf16[8,16,1024]{2,1,0:T(8,128)(2,1)S(1)}, u32[]{:S(2)}, u32[]{:S(2)}) collective-permute-start(bf16[8,16,1024]{2,1,0:T(8,128)(2,1)S(1)} %get-tuple-element.37), channel_id=1, source_target_pairs={{0,1},{1,0},{2,3},{3,2},{4,5},{5,4},{6,7},{7,6},{8,9},{9,8},{10,11... | collective-permute-start | bytes 786440 | tf_op jit(solution)/shard_map/ppermute | solution.py:550
  2.2 0.2 collective-permute-start.2
  2.5 1.4 %collective-permute-start = (f32[32,16,384]{2,1,0:T(8,128)S(1)}, f32[32,16,384]{2,1,0:T(8,128)S(1)}, u32[]{:S(2)}, u32[]{:S(2)}) collective-permute-start(f32[32,16,384]{2,1,0:T(8,128)S(1)} %get-tuple-element.36), channel_id=1, source_target_pairs={{0,1},{1,0},{2,3},{3,2},{4,5},{5,4},{6,7},{7,6},{8,9},{9,8},{10,11... | collective-permute-start | bytes 2359304 | tf_op jit(solution)/shard_map/ppermute | solution.py:554
  3.8 0.0 collective-permute-done.1.edge_ref
  3.8 0.0 copy-done.3
  3.8 0.0 copy-start.2
  3.8 0.0 copy-start.4
  3.9 0.0 copy-start.5
  3.9 0.0 copy-start.6
  3.9 7.8 %shard_map.119 = (bf16[384,3072]{1,0:T(8,128)(2,1)S(1)}, bf16[512,1024]{1,0:T(8,128)(2,1)S(1)}, bf16[512,1024]{1,0:T(8,128)(2,1)S(1)}, f32[512,384]{1,0:T(8,128)...) custom-call(bf16[8,96,1024]{2,1,0:T(8,128)(2,1)} %tok_hbm.1, ...), custom_call_target="tpu_custom_call" | custom-call | flops 7500000256 | bytes 7500000 | tf_op jit(solution)/shard_map/pallas_call | solution.py:565
  11.7 0.0 collective-permute-done.got_ref
  11.7 0.0 copy-done.2
  11.7 0.0 copy-done.4
  11.7 0.0 copy-done.5
  11.7 0.0 copy-done.6
  11.7 2.8 %shard_map.120 = (f32[512,768]{1,0:T(8,128)S(1)}, bf16[64,768]{1,0:T(8,128)(2,1)S(1)}) custom-call(f32[32,32,384]{2,1,0:T(8,128)S(1)} %copy-done.2, f32[32,16,384]{2,1,0:T(8,128)S(1)} %collective-permute-done.got_ref, f32[1,32]{1,0:T(1,128)S(1)} %bitcast.5, bf16[768,768]{1,0:T(8,128)(2,1)S(1)} %copy-done.6, bf16[768,768]{1,0:T(8,128)(2,1)S(1)} %copy-done.5), custom_call_target="tpu_custom_call" | custom-call | flops 2700000000 | bytes 2700000 | tf_op jit(solution)/shard_map/pallas_call | solution.py:591
  14.5 3.1 %collective-permute-start.3 = (bf16[64,768]{1,0:T(8,128)(2,1)S(1)}, bf16[64,768]{1,0:T(8,128)(2,1)S(1)}, u32[]{:S(2)}, u32[]{:S(2)}) collective-permute-start(bf16[64,768]{1,0:T(8,128)(2,1)S(1)} %get-tuple-element.53), channel_id=1, source_target_pairs={{1,2},{3,4},{5,6},{7,8},{9,10},{11,12},{13,14},{2,1},{4,3},{6,5},{... | collective-permute-start | bytes 294920 | tf_op jit(solution)/shard_map/ppermute | solution.py:598
  17.6 0.4 collective-permute-start.4
  18.1 0.0 collective-permute-done.2.refs_0_
  18.1 6.1 %shard_map.121 = (bf16[512,256]{1,0:T(8,128)(2,1)S(1)}, bf16[576,256]{1,0:T(8,128)(2,1)S(1)}) custom-call(bf16[4,80,1024]{2,1,0:T(8,128)(2,1)S(1)} %collective-permute-done.2.refs_0_, f32[1,1024]{1,0:T(1,128)S(1)} %bitcast.3, bf16[384,3072]{1,0:T(8,128)(2,1)S(1)} %get-tuple-element.45.refs_2_.refs_3_, f32[512,384]{1,0:T(8,128)S(1)} %get-tuple-element.46.refs_3_.refs_4_, ...), custom_call_target="tpu_custom_call" | custom-call | flops 6000000000 | bytes 6000000 | tf_op jit(solution)/shard_map/pallas_call | solution.py:604
  24.2 4.4 %collective-permute-start.5 = (bf16[576,256]{1,0:T(8,128)(2,1)S(1)}, bf16[576,256]{1,0:T(8,128)(2,1)S(1)}, u32[]{:S(2)}, u32[]{:S(2)}) collective-permute-start(bf16[576,256]{1,0:T(8,128)(2,1)S(1)} %get-tuple-element.60.refs_2_), channel_id=1, source_target_pairs={{1,2},{3,4},{5,6},{7,8},{9,10},{11,12},{13,14},{2,1},{4,3},{6,5},{... | collective-permute-start | bytes 884744 | tf_op jit(solution)/shard_map/ppermute | solution.py:622
  28.5 0.0 copy-start
  28.6 0.0 copy-start.1
  28.6 0.0 collective-permute-done.3.base_edge_ref
  28.6 0.0 collective-permute-done.4.refs_1_
  28.6 3.3 %shard_map.122 = (bf16[512,128]{1,0:T(8,128)(2,1)S(1)}, bf16[576,128]{1,0:T(8,128)(2,1)S(1)}) custom-call(bf16[4,80,1024]{2,1,0:T(8,128)(2,1)S(1)} %collective-permute-done.2.refs_0_, bf16[4,24,1024]{2,1,0:T(8,128)(2,1)S(1)} %collective-permute-done.4.refs_1_, f32[1,1024]{1,0:T(1,128)S(1)} %bitcast.4, ...), custom_call_target="tpu_custom_call" | custom-call | flops 3000000000 | bytes 3000000 | tf_op jit(solution)/shard_map/pallas_call | solution.py:604
  31.9 2.1 %collective-permute-start.6 = (bf16[576,128]{1,0:T(8,128)(2,1)S(1)}, bf16[576,128]{1,0:T(8,128)(2,1)S(1)}, u32[]{:S(2)}, u32[]{:S(2)}) collective-permute-start(bf16[576,128]{1,0:T(8,128)(2,1)S(1)} %get-tuple-element.61.refs_3_), channel_id=1, source_target_pairs={{1,2},{3,4},{5,6},{7,8},{9,10},{11,12},{13,14},{2,1},{4,3},{6,5},{... | collective-permute-start | bytes 442376 | tf_op jit(solution)/shard_map/ppermute | solution.py:622
  34.0 0.0 collective-permute-done.5.refs_4_
  34.1 0.0 copy-done
  34.1 0.0 copy-done.1
  34.1 1.6 %shard_map.123.early_ref = f32[576,768]{1,0:T(8,128)S(1)} custom-call(f32[512,768]{1,0:T(8,128)S(1)} %get-tuple-element.42.base_ref, bf16[64,768]{1,0:T(8,128)(2,1)S(1)} %collective-permute-done.3.base_edge_ref, f32[1,32]{1,0:T(1,128)S(1)} %bitcast.6, bf16[1152,768]{1,0:T(8,128)(2,1)S(1)} %copy-done.1, bf16[1152,768]{1,0:T(8,128)(2,1)S(1)} %copy-done, ...), custom_call_target="tpu_custom_call" | custom-call | flops 1600000000 | bytes 1600000 | tf_op jit(solution)/shard_map/pallas_call | solution.py:624
  35.6 3.8 %collective-permute-done.6.got_ref = bf16[576,128]{1,0:T(8,128)(2,1)S(1)} collective-permute-done((bf16[576,128]{1,0:T(8,128)(2,1)S(1)}, bf16[576,128]{1,0:T(8,128)(2,1)S(1)}, u32[]{:S(2)}, u32[]{:S(2)}) %collective-permute-start.6) | collective-permute-done | bytes 147488 | tf_op jit(solution)/shard_map/ppermute | solution.py:622
  39.4 0.6 %shard_map.124 = (f32[512,768]{1,0:T(8,128)S(1)}, bf16[64,768]{1,0:T(8,128)(2,1)S(1)}, f32[64,768]{1,0:T(8,128)S(1)}) custom-call(f32[576,768]{1,0:T(8,128)S(1)} %shard_map.123.early_ref, bf16[576,128]{1,0:T(8,128)(2,1)S(1)} %collective-permute-done.6.got_ref, f32[1,32]{1,0:T(1,128)S(1)} %bitcast.7, bf16[1152,768]{1,0:T(8,128)(2,1)S(1)} %copy-done.1, ...), custom_call_target="tpu_custom_call" | custom-call | flops 1000000000 | bytes 1000000 | tf_op jit(solution)/shard_map/pallas_call | solution.py:630
  40.0 0.8 %collective-permute-start.7 = (bf16[64,768]{1,0:T(8,128)(2,1)S(1)}, bf16[64,768]{1,0:T(8,128)(2,1)S(1)}, u32[]{:S(2)}, u32[]{:S(2)}) collective-permute-start(bf16[64,768]{1,0:T(8,128)(2,1)S(1)} %get-tuple-element.65), channel_id=1, source_target_pairs={{0,1},{1,0},{2,3},{3,2},{4,5},{5,4},{6,7},{7,6},{8,9},{9,8},{10,11... | collective-permute-start | bytes 294920 | tf_op jit(solution)/shard_map/ppermute | solution.py:639
  40.8 3.3 %shard_map.125 = (f32[512,768]{1,0:T(8,128)S(1)}, f32[512,768]{1,0:T(8,128)S(1)}) custom-call(f32[512,768]{1,0:T(8,128)S(1)} %get-tuple-element.62.field_ref), custom_call_target="tpu_custom_call" | custom-call | flops 4000000000 | bytes 4000000 | tf_op jit(solution)/shard_map/pallas_call | solution.py:642
  44.1 0.0 collective-permute-done.7.lon_ref
  44.2 1.9 %shard_map.126 = f32[32,16,768]{2,1,0:T(8,128)} custom-call(f32[512,768]{1,0:T(8,128)S(1)} %get-tuple-element.62.field_ref, f32[512,768]{1,0:T(8,128)S(1)} %get-tuple-element.63.first_ref, f32[512,768]{1,0:T(8,128)S(1)} %get-tuple-element.64.last_ref, bf16[64,768]{1,0:T(8,128)(2,1)S(1)} %collective-permute-done.7.lon_ref, ...), custom_call_target="tpu_custom_call" | custom-call | flops 2200000000 | bytes 2200000 | tf_op jit(solution)/shard_map/pallas_call | solution.py:643
  (2 shorter events, 0.0 us)
Async XLA Ops:
  0.0 3.8 %copy-start.3 = (f32[1024]{0:T(1024)S(1)}, f32[1024]{0:T(1024)}, u32[]{:S(2)}) copy-start(f32[1024]{0:T(1024)} %param.13) | copy-start | bytes 12292
  1.5 2.3 %collective-permute-start.1 = (bf16[8,16,1024]{2,1,0:T(8,128)(2,1)S(1)}, bf16[8,16,1024]{2,1,0:T(8,128)(2,1)S(1)}, u32[]{:S(2)}, u32[]{:S(2)}) collective-permute-start(bf16[8,16,1024]{2,1,0:T(8,128)(2,1)S(1)} %get-tuple-element.37), channel_id=1, source_target_pairs={{0,1},{1,0},{2,3},{3,2},{4,5},{5,4},{6,7},{7,6},{8,9},{9,8},{10,11... | collective-permute-start | bytes 786440 | tf_op jit(solution)/shard_map/ppermute | solution.py:550
  2.2 15.8 %collective-permute-start.2 = (bf16[4,80,1024]{2,1,0:T(8,128)(2,1)S(1)}, bf16[4,80,1024]{2,1,0:T(8,128)(2,1)S(1)}, u32[]{:S(2)}, u32[]{:S(2)}) collective-permute-start(bf16[4,80,1024]{2,1,0:T(8,128)(2,1)S(1)} %get-tuple-element.44), channel_id=1, source_target_pairs={{0,2},{2,4},{4,6},{6,8},{8,10},{10,12},{12,14},{14,15},{3,1},{5,3}... | collective-permute-start | bytes 1966088 | tf_op jit(solution)/shard_map/ppermute | solution.py:553
  2.5 9.2 %collective-permute-start = (f32[32,16,384]{2,1,0:T(8,128)S(1)}, f32[32,16,384]{2,1,0:T(8,128)S(1)}, u32[]{:S(2)}, u32[]{:S(2)}) collective-permute-start(f32[32,16,384]{2,1,0:T(8,128)S(1)} %get-tuple-element.36), channel_id=1, source_target_pairs={{0,1},{1,0},{2,3},{3,2},{4,5},{5,4},{6,7},{7,6},{8,9},{9,8},{10,11... | collective-permute-start | bytes 2359304 | tf_op jit(solution)/shard_map/ppermute | solution.py:554
  3.8 7.9 %copy-start.2 = (f32[32,32,384]{2,1,0:T(8,128)S(1)}, f32[32,32,384]{2,1,0:T(8,128)}, u32[]{:S(2)}) copy-start(f32[32,32,384]{2,1,0:T(8,128)} %state_ref.3) | copy-start | bytes 4718596
  3.8 7.9 %copy-start.4 = (f32[32]{0:T(128)S(1)}, f32[32]{0:T(128)}, u32[]{:S(2)}) copy-start(f32[32]{0:T(128)} %param.18) | copy-start | bytes 388
  3.9 7.9 %copy-start.5 = (bf16[768,768]{1,0:T(8,128)(2,1)S(1)}, bf16[768,768]{1,0:T(8,128)(2,1)}, u32[]{:S(2)}) copy-start(bf16[768,768]{1,0:T(8,128)(2,1)} %constant.21.clone.low_ref) | copy-start | bytes 3538948
  3.9 7.9 %copy-start.6 = (bf16[768,768]{1,0:T(8,128)(2,1)S(1)}, bf16[768,768]{1,0:T(8,128)(2,1)}, u32[]{:S(2)}) copy-start(bf16[768,768]{1,0:T(8,128)(2,1)} %constant.20.clone.high_ref) | copy-start | bytes 3538948
  14.5 14.0 %collective-permute-start.3 = (bf16[64,768]{1,0:T(8,128)(2,1)S(1)}, bf16[64,768]{1,0:T(8,128)(2,1)S(1)}, u32[]{:S(2)}, u32[]{:S(2)}) collective-permute-start(bf16[64,768]{1,0:T(8,128)(2,1)S(1)} %get-tuple-element.53), channel_id=1, source_target_pairs={{1,2},{3,4},{5,6},{7,8},{9,10},{11,12},{13,14},{2,1},{4,3},{6,5},{... | collective-permute-start | bytes 294920 | tf_op jit(solution)/shard_map/ppermute | solution.py:598
  17.6 11.0 %collective-permute-start.4 = (bf16[4,24,1024]{2,1,0:T(8,128)(2,1)S(1)}, bf16[4,24,1024]{2,1,0:T(8,128)(2,1)S(1)}, u32[]{:S(2)}, u32[]{:S(2)}) collective-permute-start(bf16[4,24,1024]{2,1,0:T(8,128)(2,1)S(1)} %pad_maximum_fusion), channel_id=1, source_target_pairs={{0,2},{2,4},{4,6},{6,8},{8,10},{10,12},{12,14},{14,15},{3,1},{5,3}... | collective-permute-start | bytes 589832 | tf_op jit(solution)/shard_map/ppermute | solution.py:600
  24.2 9.9 %collective-permute-start.5 = (bf16[576,256]{1,0:T(8,128)(2,1)S(1)}, bf16[576,256]{1,0:T(8,128)(2,1)S(1)}, u32[]{:S(2)}, u32[]{:S(2)}) collective-permute-start(bf16[576,256]{1,0:T(8,128)(2,1)S(1)} %get-tuple-element.60.refs_2_), channel_id=1, source_target_pairs={{1,2},{3,4},{5,6},{7,8},{9,10},{11,12},{13,14},{2,1},{4,3},{6,5},{... | collective-permute-start | bytes 884744 | tf_op jit(solution)/shard_map/ppermute | solution.py:622
  28.5 5.5 %copy-start = (bf16[1152,768]{1,0:T(8,128)(2,1)S(1)}, bf16[1152,768]{1,0:T(8,128)(2,1)}, u32[]{:S(2)}) copy-start(bf16[1152,768]{1,0:T(8,128)(2,1)} %constant.23.clone.low_ref) | copy-start | bytes 5308420
  28.6 5.5 %copy-start.1 = (bf16[1152,768]{1,0:T(8,128)(2,1)S(1)}, bf16[1152,768]{1,0:T(8,128)(2,1)}, u32[]{:S(2)}) copy-start(bf16[1152,768]{1,0:T(8,128)(2,1)} %constant.22.clone.high_ref) | copy-start | bytes 5308420
  31.9 7.5 %collective-permute-start.6 = (bf16[576,128]{1,0:T(8,128)(2,1)S(1)}, bf16[576,128]{1,0:T(8,128)(2,1)S(1)}, u32[]{:S(2)}, u32[]{:S(2)}) collective-permute-start(bf16[576,128]{1,0:T(8,128)(2,1)S(1)} %get-tuple-element.61.refs_3_), channel_id=1, source_target_pairs={{1,2},{3,4},{5,6},{7,8},{9,10},{11,12},{13,14},{2,1},{4,3},{6,5},{... | collective-permute-start | bytes 442376 | tf_op jit(solution)/shard_map/ppermute | solution.py:622
  40.0 4.1 %collective-permute-start.7 = (bf16[64,768]{1,0:T(8,128)(2,1)S(1)}, bf16[64,768]{1,0:T(8,128)(2,1)S(1)}, u32[]{:S(2)}, u32[]{:S(2)}) collective-permute-start(bf16[64,768]{1,0:T(8,128)(2,1)S(1)} %get-tuple-element.65), channel_id=1, source_target_pairs={{0,1},{1,0},{2,3},{3,2},{4,5},{5,4},{6,7},{7,6},{8,9},{9,8},{10,11... | collective-permute-start | bytes 294920 | tf_op jit(solution)/shard_map/ppermute | solution.py:639

commit v4 on v3

--- a/solution.py
+++ b/solution.py
@@ -84,8 +84,8 @@
     for pair in range(cols // (2 * WIN)):
         col = first + pair * 2 * WIN
         for r in range(HALF):
-            here = load(r, col, 2 * WIN).astype(F32)
-            after = load(r, col + 2 * WIN, WIN).astype(F32)
+            here = load(r, col, 2 * WIN)
+            after = load(r, col + 2 * WIN, WIN)
             emit(pair, r, jnp.where(lead, jnp.concatenate([here[WIN:], after], axis=0), here))
 
 
@@ -130,17 +130,47 @@
     return copies
 
 
-def pack_kernel(pieces, tok_ref, state_ref, *refs):
-    *give_refs, edge_ref, give_state_ref, sems = refs
+def pack_kernel(tok_ref, state_ref, give_ref, more_ref, edge_ref, give_state_ref, whole_ref, sems):
     lon = place()[0]
     rows = give_state_ref.shape[1]
-    pairs = []
-    for give_ref, (start, size) in zip(give_refs, pieces):
-        pairs.append((tok_ref.at[pl.ds(HALF * (1 - lon), HALF), pl.ds(start, size), :], give_ref))
-    pairs.append((tok_ref.at[:, pl.ds(0, edge_ref.shape[1]), :], edge_ref))
-    pairs.append((state_ref.at[:, pl.ds(pl.multiple_of(rows * (1 - lon), 8), rows), :], give_state_ref))
-    for copy in run_copies(sems, pairs):
+    give_rows = pl.ds(HALF * (1 - lon), HALF)
+    more = more_ref.shape[1]
+    pairs = [
+        (tok_ref.at[give_rows, pl.ds(0, whole_ref.shape[1]), :], whole_ref),
+        (tok_ref.at[give_rows, pl.ds(tok_ref.shape[1] - more, more), :], more_ref),
+        (tok_ref.at[:, pl.ds(0, edge_ref.shape[1]), :], edge_ref),
+        (state_ref.at[:, pl.ds(pl.multiple_of(rows * (1 - lon), 8), rows), :], give_state_ref),
+    ]
+    copies = run_copies(sems, pairs)
+    copies[0].wait()
+    give_ref[...] = whole_ref[:, : give_ref.shape[1], :]
+    for copy in copies[1:]:
         copy.wait()
+
+
+def edge_blocks(rows, width):
+    places = []
+    for block in range(rows * width[0] // (16 * 128)):
+        lane, row = divmod(block, rows // 16)
+        to_row, to_lane = divmod(block, width[1] // 128)
+        places.append(
+            (
+                (slice(row * 16, row * 16 + 16), slice(lane * 128, lane * 128 + 128)),
+                (slice(to_row * 16, to_row * 16 + 16), slice(to_lane * 128, to_lane * 128 + 128)),
+            )
+        )
+    return places
+
+
+def last_piece_kernel(cols, more_ref, edge_ref, base_edge_ref, out_ref):
+    lon = place()[0]
+    for r in range(HALF):
+        own = more_ref[r].astype(F32)[more_ref.shape[1] - cols + WIN :]
+        after = edge_ref[HALF * (1 - lon) + r, :WIN, :].astype(F32)
+        out_ref[r * cols : (r + 1) * cols, :] = jnp.concatenate([own, after], axis=0).astype(BF16)
+    for (rows, lanes), (to_rows, to_lanes) in edge_blocks(base_edge_ref.shape[0], (base_edge_ref.shape[1], out_ref.shape[1])):
+        at = slice(HALF * cols + to_rows.start, HALF * cols + to_rows.stop)
+        out_ref[at, to_lanes] = base_edge_ref[rows, lanes]
 
 
 def own_kernel(
@@ -151,12 +181,18 @@
     wkv_hbm,
     wout_hbm,
     wdec_hbm,
+    state_hbm,
+    high_hbm,
+    low_hbm,
     qkv_ref,
     wdec_t_ref,
     wmix_t_ref,
     decoded_ref,
     wq_ref,
     wkv_ref,
+    state_ref,
+    high_ref,
+    low_ref,
     tok_ref,
     raw_ref,
     normed_ref,
@@ -169,6 +205,7 @@
     width = wq_ref.shape[0]
     keys, values = pl.ds(0, width), pl.ds(width, width)
     own_rows = pl.ds(HALF * lon, HALF)
+    state_rows = pl.ds(pl.multiple_of(state_ref.shape[1] * lon, 8), state_ref.shape[1])
     copies = run_copies(
         sems,
         [
@@ -178,13 +215,16 @@
             (wkv_hbm.at[:, values], wkv_ref.at[:, values]),
             (wdec_hbm, wdec_ref),
             (wout_hbm, wout_ref),
+            (state_hbm.at[:, state_rows, :], state_ref),
+            (high_hbm, high_ref),
+            (low_hbm, low_ref),
         ],
     )
 
     def load(r, c, size):
         if c == cols:
-            return edge_ref[HALF * lon + r, :size, :]
-        return tok_ref[r, c : c + size, :]
+            return edge_ref[HALF * lon + r, :size, :].astype(F32)
+        return tok_ref[r, c : c + size, :].astype(F32)
 
     copies[0].wait()
     place_tokens(load, 0, cols, gain_ref[...], raw_ref, normed_ref)
@@ -200,6 +240,8 @@
     decoded_ref[...] = dot_nt(wdec_t_ref[...], raw_ref[...])
     copies[5].wait()
     wmix_t_ref[...] = dot_nt(wdec_t_ref[...], wout_ref[...]).astype(BF16)
+    for copy in copies[6:]:
+        copy.wait()
 
 
 def main_kernel(first, starts, *refs):
@@ -219,7 +261,13 @@
 
     def load(r, c, size):
         which = max(i for i in range(len(starts)) if starts[i] <= c)
-        return x_refs[which][r, c - starts[which] : c - starts[which] + size, :]
+        at = c - starts[which]
+        if which:
+            at += r * group_cols
+            return x_refs[which][at : at + size, :].astype(F32)
+        if at + size > x_refs[which].shape[1]:
+            return jnp.concatenate([load(r, c, size // 2), load(r, c + size // 2, size // 2)], axis=0)
+        return x_refs[which][r, at : at + size, :].astype(F32)
 
     def iota(shape, dim):
         return lax.broadcasted_iota(jnp.int32, shape, dim)
@@ -329,9 +377,8 @@
     own_lanes = pl.ds(pl.multiple_of(lon * cols, 128), cols)
     got_lanes = pl.ds(pl.multiple_of((1 - lon) * cols, 128), cols)
     for y in range(0, own_rows, 8):
-        own_part = pl.ds(pl.multiple_of(lon * own_rows + y, 8), 8)
         for ch in range(0, channels, 8):
-            own = jnp.swapaxes(state_ref[ch : ch + 8, own_part, :], 0, 1)
+            own = jnp.swapaxes(state_ref[ch : ch + 8, y : y + 8, :], 0, 1)
             got = jnp.swapaxes(got_ref[ch : ch + 8, y : y + 8, :], 0, 1)
             for i in range(8):
                 rows = slice((y + i) * channels + ch, (y + i) * channels + ch + 8)
@@ -351,35 +398,49 @@
     return dot(dec, high_ref[rows, :]) + dot(dec, low_ref[rows, :])
 
 
-def early_kernel(chunks, base_ref, base_edge_ref, nudge_ref, high_ref, low_ref, *refs):
-    keep_refs, send_refs, got_refs, out_ref = refs[:chunks], refs[chunks : 2 * chunks], refs[2 * chunks : -1], refs[-1]
+def early_kernel(base_ref, piece_ref, nudge_ref, high_ref, low_ref, *refs):
+    *refs, out_ref = refs
+    keep_refs, send_refs = refs[: len(refs) // 2], refs[len(refs) // 2 :]
     lon = place()[0]
     total = base_ref.shape[0]
-    edge = base_edge_ref.shape[0]
+    edge = out_ref.shape[0] - total
     far = pl.ds(pl.multiple_of((1 - lon) * (total - edge), edge), edge)
     own = [jnp.concatenate([keep[...], send[far, :]], axis=0) for keep, send in zip(keep_refs, send_refs)]
-    decoded = jnp.concatenate(own + [got[...] for got in got_refs], axis=1)
+    decoded = jnp.concatenate(own, axis=1)
     smooth = filter_rows(decoded, lon * (high_ref.shape[0] // 3), high_ref, low_ref)
     step = PATCH * nudge_ref.shape[1]
     strength = nudge_column(nudge_ref, step)
     for at in range(0, total, step):
         out_ref[at : at + step, :] = base_ref[at : at + step, :] + strength * smooth[at : at + step]
-    out_ref[total:, :] = base_edge_ref[...].astype(F32) + strength[:edge] * smooth[total:]
-
-
-def late_kernel(early_ref, got_ref, nudge_ref, high_ref, low_ref, out_ref, near_ref, lat_ref):
-    lon = place()[0]
-    total = out_ref.shape[0]
-    edge = lat_ref.shape[0]
-    part = high_ref.shape[0] // 3
-    smooth = filter_rows(got_ref[...], lon * part + 2 * part - got_ref.shape[1], high_ref, low_ref)
+    length, width = out_ref.shape[1], piece_ref.shape[1]
+    first = piece_ref.shape[0] - edge * length // width
+    for (rows, lanes), (at_rows, at_lanes) in edge_blocks(edge, (length, width)):
+        base_edge = piece_ref[first + at_rows.start : first + at_rows.stop, at_lanes].astype(F32)
+        term = strength[rows] * smooth[total + rows.start : total + rows.stop, lanes]
+        out_ref[total + rows.start : total + rows.stop, lanes] = base_edge + term
+
+
+def add_kernel(skip, early_ref, got_ref, nudge_ref, high_ref, low_ref, out_ref):
+    smooth = filter_rows(got_ref[...], place()[0] * (high_ref.shape[0] // 3) + high_ref.shape[0] // 3 + skip, high_ref, low_ref)
     step = PATCH * nudge_ref.shape[1]
     strength = nudge_column(nudge_ref, step)
-    for at in range(0, total, step):
-        out_ref[at : at + step, :] = early_ref[at : at + step, :] + strength * smooth[at : at + step]
-    lat_ref[...] = early_ref[total:, :] + strength[:edge] * smooth[total:]
+    for at in range(0, out_ref.shape[0], step):
+        rows = slice(at, min(at + step, out_ref.shape[0]))
+        out_ref[rows, :] = early_ref[rows, :] + strength[: rows.stop - at] * smooth[rows]
+
+
+def last_rows(high_ref, got_ref):
+    part = high_ref.shape[0] // 3
+    return place()[0] * part + 2 * part - got_ref.shape[1]
+
+
+def near_kernel(early_ref, got_ref, nudge_ref, high_ref, low_ref, near_ref):
+    lon = place()[0]
+    edge = near_ref.shape[0]
+    total = early_ref.shape[0] - edge
     far = pl.ds(pl.multiple_of((1 - lon) * (total - edge), edge), edge)
-    near_ref[...] = out_ref[far, :].astype(BF16)
+    smooth = filter_rows(got_ref[far, :], last_rows(high_ref, got_ref), high_ref, low_ref)
+    near_ref[...] = (early_ref[far, :] + nudge_column(nudge_ref, edge) * smooth).astype(BF16)
 
 
 def row_tile(ref, row, var):
@@ -387,11 +448,11 @@
     return pl.ds(at if isinstance(at, int) else pl.multiple_of(at, LEV), LEV)
 
 
-def tendency_row(south, centre, north, use):
+def tendency_row(south, centre, north, use, only=range(VARS)):
     push_u, push_v = (0.5 * time_step) * centre(0), (0.5 * time_step) * centre(1)
     calm = diffusion * time_step
     to_east, to_west, to_north, to_south = calm - push_u, calm + push_u, calm - push_v, calm + push_v
-    for var in range(VARS):
+    for var in only:
         field = centre(var)
         length = field.shape[1]
         step = to_east * pltpu.roll(field, length - 1, axis=1) + to_west * pltpu.roll(field, 1, axis=1)
@@ -399,8 +460,16 @@
         use(var, field, step - (4.0 * calm) * field)
 
 
-def inner_kernel(field_ref, first_ref, last_ref):
-    rows = field_ref.shape[0] // (VARS * LEV)
+def inner_kernel(early_ref, got_ref, nudge_ref, high_ref, low_ref, field_ref, lat_ref, first_ref, last_ref):
+    total = field_ref.shape[0]
+    edge = lat_ref.shape[0]
+    rows = total // (VARS * LEV)
+    smooth = filter_rows(got_ref[...], last_rows(high_ref, got_ref), high_ref, low_ref)
+    step = PATCH * nudge_ref.shape[1]
+    strength = nudge_column(nudge_ref, step)
+    for at in range(0, total, step):
+        field_ref[at : at + step, :] = early_ref[at : at + step, :] + strength * smooth[at : at + step]
+    lat_ref[...] = early_ref[total:, :] + strength[:edge] * smooth[total:]
 
     def reader(ref, row):
         return lambda var: ref[row_tile(ref, row, var), :]
@@ -408,26 +477,22 @@
     def section(ref, row, use):
         tendency_row(reader(ref, row - 1), reader(ref, row), reader(ref, row + 1), use)
 
-    def first_row(row, _):
-        def put(var, field, step):
+    for row in range(1, rows - 1):
+
+        def put_first(var, field, step):
             first_ref[row_tile(first_ref, row, var), :] = field + step
 
-        section(field_ref, row, put)
-        return 0
-
-    def last_row(row, _):
-        def put(var, field, step):
+        section(field_ref, row, put_first)
+    for row in range(2, rows - 2):
+
+        def put_last(var, field, step):
             nudged = field_ref[row_tile(field_ref, row, var), :]
             last_ref[row_tile(last_ref, row, var), :] = 0.5 * (nudged + field + step)
 
-        section(first_ref, row, put)
-        return 0
-
-    lax.fori_loop(1, rows - 1, first_row, 0)
-    lax.fori_loop(2, rows - 2, last_row, 0)
-
-
-def outer_kernel(field_ref, first_ref, last_ref, lon_ref, lat_ref, out_ref, ext_ref, edge_ref):
+        section(first_ref, row, put_last)
+
+
+def outer_kernel(field_ref, first_ref, last_ref, lon_ref, lat_ref, out_hbm, ext_ref, edge_ref, out_ref, sems):
     channels, rows, length = out_ref.shape
     lon, pole = place()
     is_top = lon == 0
@@ -471,20 +536,27 @@
             edge_ref[row_tile(edge_ref, at, var), :] = total if keep is None else total * keep
 
         tendency_row(field(row - 1), field(row), field(row + 1), put)
-    outer = {}
-    for row in (0, 1, rows - 2, rows - 1):
-
-        def put(var, value, step):
-            outer[row, var] = 0.5 * (field(row)(var) + value + step)
-
-        tendency_row(first(row - 1), first(row), first(row + 1), put)
-    for y in range(0, rows, 8):
-        for var in range(VARS):
+    copies = []
+    for var in range(VARS):
+        levels = slice(var * LEV, (var + 1) * LEV)
+        outer = {}
+        for row in (0, 1, rows - 2, rows - 1):
+
+            def put(var, value, step):
+                outer[row, var] = 0.5 * (field(row)(var) + value + step)
+
+            tendency_row(first(row - 1), first(row), first(row + 1), put, [var])
+        for y in range(0, rows, 8):
             block = []
             for row in range(y, y + 8):
                 tile = outer[row, var] if (row, var) in outer else last_ref[row_tile(last_ref, row, var), :]
                 block.append(tile[None])
-            out_ref[var * LEV : (var + 1) * LEV, y : y + 8, :] = jnp.swapaxes(jnp.concatenate(block, axis=0), 0, 1)
+            out_ref[levels, y : y + 8, :] = jnp.swapaxes(jnp.concatenate(block, axis=0), 0, 1)
+        part = pl.ds(var * LEV, LEV)
+        copies.append(pltpu.make_async_copy(out_ref.at[part], out_hbm.at[part], sems.at[var]))
+        copies[-1].start()
+    for copy in copies:
+        copy.wait()
 
 
 def work(micros):
@@ -531,26 +603,28 @@
     step = GROUP * WIN
     split = max(tok_cols - step, step)
     chunks = [(0, split)] + ([(split, step)] if split < tok_cols else [])
-    cuts = [0] + [split + 2 * WIN] * (len(chunks) - 1) + [tok_cols]
-    pieces = [(cuts[i], cuts[i + 1] - cuts[i]) for i in range(len(chunks))]
+    cuts = [0] + [split + WIN] * (len(chunks) - 1) + [tok_cols]
 
     hbm, vmem = pl.BlockSpec(memory_space=pltpu.HBM), pl.BlockSpec(memory_space=pltpu.VMEM)
     in_hbm = functools.partial(pltpu.with_memory_space_constraint, memory_space=pltpu.HBM)
-    shapes = [pltpu.VMEM((HALF, size, width), BF16) for _, size in pieces]
-    shapes.append(pltpu.VMEM((tok_rows, 2 * WIN, width), BF16))
-    shapes.append(pltpu.VMEM((channels, band_rows, state_cols), F32))
-    *give, give_edge, give_state = pl.pallas_call(
-        functools.partial(pack_kernel, pieces),
-        out_shape=shapes,
+    give, more, give_edge, give_state = pl.pallas_call(
+        pack_kernel,
+        out_shape=[
+            pltpu.VMEM((HALF, cuts[1], width), BF16),
+            pltpu.VMEM((HALF, step, width), BF16),
+            pltpu.VMEM((tok_rows, 2 * WIN, width), BF16),
+            pltpu.VMEM((channels, band_rows, state_cols), F32),
+        ],
         in_specs=[hbm, hbm],
-        out_specs=[vmem] * len(shapes),
-        scratch_shapes=[pltpu.SemaphoreType.DMA((len(shapes),))],
-        compiler_params=pltpu.CompilerParams(vmem_limit_bytes=8 * MIB),
+        out_specs=[vmem] * 4,
+        scratch_shapes=[
+            pltpu.VMEM((HALF, split + 2 * WIN, width), BF16),
+            pltpu.SemaphoreType.DMA((4,)),
+        ],
+        compiler_params=pltpu.CompilerParams(vmem_limit_bytes=12 * MIB),
     )(in_hbm(tokens), in_hbm(state))
     edge_tokens = lax.ppermute(give_edge, "lon", swap)
-    their_edge = lax.dynamic_slice(edge_tokens, (HALF * (1 - lon), 0, 0), (HALF, WIN, width))
-    give[-1] = jnp.concatenate([give[-1], their_edge], axis=1)
-    got_tokens = [lax.ppermute(give[0], both, shift)]
+    got_tokens = [lax.ppermute(give, both, shift)]
     got_state = lax.ppermute(give_state, "lon", swap)
 
     gain = ln_gain[None, :]
@@ -562,7 +636,7 @@
     dec_high, dec_low = (jnp.asarray(m) for m in split_high_low(matrix[order]))
 
     n_out = w_dec.shape[1]
-    qkv_own, w_dec_t, w_mix_t, decoded_own, *weights = pl.pallas_call(
+    qkv_own, w_dec_t, w_mix_t, decoded_own, *weights, own_state, high, low = pl.pallas_call(
         own_kernel,
         out_shape=[
             pltpu.VMEM((tokens_half, 3 * width), BF16),
@@ -571,20 +645,23 @@
             pltpu.VMEM((n_out, tokens_half), F32),
             pltpu.VMEM(w_query.shape, BF16),
             pltpu.VMEM(w_keyval.shape, BF16),
+            pltpu.VMEM((channels, band_rows, state_cols), F32),
+            pltpu.VMEM((length, length), BF16),
+            pltpu.VMEM((length, length), BF16),
         ],
-        in_specs=[hbm, vmem, vmem, hbm, hbm, hbm, hbm],
-        out_specs=[vmem] * 6,
+        in_specs=[hbm, vmem, vmem] + [hbm] * 7,
+        out_specs=[vmem] * 9,
         scratch_shapes=[
             pltpu.VMEM((HALF, tok_cols, width), BF16),
             pltpu.VMEM((tokens_half, width), BF16),
             pltpu.VMEM((tokens_half, width), BF16),
             pltpu.VMEM(w_dec.shape, BF16),
             pltpu.VMEM(w_out.shape, BF16),
-            pltpu.SemaphoreType.DMA((6,)),
+            pltpu.SemaphoreType.DMA((9,)),
         ],
         cost_estimate=work(7.5),
         compiler_params=pltpu.CompilerParams(vmem_limit_bytes=32 * MIB),
-    )(in_hbm(tokens), edge_tokens, gain, in_hbm(w_query), in_hbm(w_keyval), in_hbm(w_out), in_hbm(w_dec))
+    )(in_hbm(tokens), edge_tokens, gain, in_hbm(w_query), in_hbm(w_keyval), in_hbm(w_out), in_hbm(w_dec), in_hbm(state), in_hbm(high), in_hbm(low))
 
     edge_rows = 2 * channels
     got_state, qkv_own = lax.optimization_barrier((got_state, qkv_own))
@@ -594,10 +671,15 @@
         5,
         [pltpu.VMEM((band, length), F32)],
         micros=2.7,
-    )(state, got_state, nudge_row, high, low)
-    got_base_edge = lax.ppermute(base_edge, both, meet)
-    gain, base, *give[1:] = lax.optimization_barrier((gain, base, *give[1:]))
-    got_tokens += [lax.ppermute(part, both, shift) for part in give[1:]]
+    )(own_state, got_state, nudge_row, high, low)
+    their_base_edge = lax.ppermute(base_edge, "lon", swap)
+    last_cols = tok_cols - cuts[1] + WIN
+    last_rows = HALF * last_cols + edge_rows * length // width
+    last_piece = call(functools.partial(last_piece_kernel, last_cols), pltpu.VMEM((last_rows, width), BF16), 3, vmem=12)(
+        more, edge_tokens, their_base_edge
+    )
+    got_tokens.append(lax.ppermute(last_piece, both, shift))
+    gain, last_piece = lax.optimization_barrier((gain, last_piece))
 
     keep, send, got = [], [], []
     for i, (first, cols) in enumerate(chunks):
@@ -615,38 +697,40 @@
             micros=3.0 * (cols // step),
         )(*got_tokens[: i + 1], gain, qkv_own, decoded_own, *weights, w_mix_t, w_dec_t)
         gain, kept = lax.optimization_barrier((gain, kept))
-        if i == 0:
-            gain, got_base_edge = lax.optimization_barrier((gain, got_base_edge))
         keep.append(kept)
         send.append(sent)
         got.append(lax.ppermute(sent, both, meet_all))
 
-    early = call(
-        functools.partial(early_kernel, len(chunks)),
-        pltpu.VMEM((band + edge_rows, length), F32),
-        5 + 3 * len(chunks) - 1,
-        micros=1.6,
-    )(base, got_base_edge, nudge_row, dec_high, dec_low, *keep, *send, *got[:-1])
-    nudged, to_lon, from_lat = call(
-        late_kernel,
-        (
-            pltpu.VMEM((band, length), F32),
-            pltpu.VMEM((edge_rows, length), BF16),
-            pltpu.VMEM((edge_rows, length), F32),
-        ),
-        5,
-    )(early, got[-1], nudge_row, dec_high, dec_low)
+    sums = pltpu.VMEM((band + edge_rows, length), F32)
+    early = call(early_kernel, sums, 5 + 2 * len(chunks), micros=1.2)(
+        base, got_tokens[-1], nudge_row, dec_high, dec_low, *keep, *send
+    )
+    skip = 0
+    for part in got[:-1]:
+        early = call(functools.partial(add_kernel, skip), sums, 5)(early, part, nudge_row, dec_high, dec_low)
+        skip += part.shape[1]
+    late = (early, got[-1], nudge_row, dec_high, dec_low)
+    to_lon = call(near_kernel, pltpu.VMEM((edge_rows, length), BF16), 5)(*late)
     from_lon = lax.ppermute(to_lon, "lon", swap)
 
     field = pltpu.VMEM((band, length), F32)
-    first, last_rows = call(inner_kernel, (field, field), 1, micros=4.0)(nudged)
-    return call(
+    edge = pltpu.VMEM((edge_rows, length), F32)
+    nudged, from_lat, first, last_inner = call(inner_kernel, (field, edge, field, field), 5, micros=2.0)(*late)
+    result = (channels, band_rows, length)
+    return pl.pallas_call(
         outer_kernel,
-        jax.ShapeDtypeStruct((channels, band_rows, length), F32),
-        5,
-        [pltpu.VMEM((2 * edge_rows, length), F32), pltpu.VMEM((2 * edge_rows, length), F32)],
-        micros=2.2,
-    )(nudged, first, last_rows, from_lon, from_lat)
+        out_shape=jax.ShapeDtypeStruct(result, F32),
+        in_specs=[vmem] * 5,
+        out_specs=hbm,
+        scratch_shapes=[
+            pltpu.VMEM((2 * edge_rows, length), F32),
+            pltpu.VMEM((2 * edge_rows, length), F32),
+            pltpu.VMEM(result, F32),
+            pltpu.SemaphoreType.DMA((VARS,)),
+        ],
+        cost_estimate=work(1.5),
+        compiler_params=pltpu.CompilerParams(vmem_limit_bytes=24 * MIB),
+    )(nudged, first, last_inner, from_lon, from_lat)
 
 
 def solution(mesh):

time: 46.8 us -> 43.8 us (0.936)
  starting transfers between devices: 13.1 us -> 10.8 us
  Pallas kernels: 28.9 us -> 27 us
  waiting for transfers between devices: 3.77 us -> 5.01 us
    ppermute x3, starting transfers between devices: 3.73 us -> 1.62 us  [the longest x1 0.93 us: body(): their_base_edge = lax.ppermute(base_edge, 'lon', swap)]
    pallas_call x5 -> x7, Pallas kernels: 8.91 us -> 7.18 us  [the longest x1 2.02 us: body(): call(inner_kernel, (field, edge, field, field), 5, micros=2.0)(*late)]
    ppermute x1, starting transfers between devices: 1.36 us -> 0.08 us  [body(): got_state = lax.ppermute(give_state, 'lon', swap)]
    ppermute x2, starting transfers between devices: 6.46 us -> 7.55 us  [body(): got.append(lax.ppermute(sent, both, meet_all))]
    ppermute x3, waiting for transfers between devices: 0.01 us -> 0.95 us  [the longest x1 0.94 us: body(): their_base_edge = lax.ppermute(base_edge, 'lon', swap)]
    ppermute x1, waiting for transfers between devices: 0.01 us -> 0.86 us  [body(): edge_tokens = lax.ppermute(give_edge, 'lon', swap)]
    ppermute x2, waiting for transfers between devices: 3.76 us -> 3.2 us  [body(): got.append(lax.ppermute(sent, both, meet_all))]
  transfers between devices with their start and end apart: 8 -> 8, of which waited for: 1 -> 3; matrix products, arithmetic and copies ran while one was open for 0% -> 0% of each run, Pallas kernels for 54% -> 55%
where the time goes in v4:
time: 43.8 us; the launch traced here: 43.2 us
  Pallas kernels  27 us (62%)
  starting transfers between devices  10.8 us (25%)
  waiting for transfers between devices  5.01 us (11%)
    pallas_call x2, Pallas kernels, body(): call(functools.partial(main_kernel, first, cuts[:i + 1]), (pltpu.VMEM((ba...  9.43 us
    pallas_call x1, Pallas kernels, body(): pl.pallas_call(own_kernel, out_shape=[pltpu.VMEM((tokens_half, 3 * width)...  7.67 us
    ppermute x2, starting transfers between devices, body(): got.append(lax.ppermute(sent, both, meet_all))  7.55 us
    ppermute x2, waiting for transfers between devices, body(): got.append(lax.ppermute(sent, both, meet_all))  3.2 us
    pallas_call x1, Pallas kernels, body(): call(state_kernel, (pltpu.VMEM((band, length), F32), pltpu.VMEM((edge_row...  2.73 us
    pallas_call x1, Pallas kernels, body(): call(inner_kernel, (field, edge, field, field), 5, micros=2.0)(*late)  2.02 us
    pallas_call x1, Pallas kernels, body(): pl.pallas_call(outer_kernel, out_shape=jax.ShapeDtypeStruct(result, F32),...  1.63 us
    pallas_call x1, Pallas kernels, body(): pl.pallas_call(pack_kernel, out_shape=[pltpu.VMEM((HALF, cuts[1], width),...  1.54 us
  transfers between devices with their start and end apart: 8, of which 3 were waited for; matrix products, arithmetic and copies ran while one was open for 0% of the time, Pallas kernels for 55%

profile of v4, /device:TPU:15, one launch (start us, length us, event | category | flops | bytes accessed | tf_op | source)
XLA Modules:
  0.0 43.2 jit_solution(14517516566268706596)
XLA Ops:
  0.0 0.0 copy-start.3
  0.0 1.5 %shard_map.118 = (bf16[4,72,1024]{2,1,0:T(8,128)(2,1)S(1)}, bf16[4,32,1024]{2,1,0:T(8,128)(2,1)S(1)}, bf16[8,16,1024]{2,1,0:T(8,128)(2,1)S(1)}, f32[32,16,384]{2,1,0:T(8,128)S(1)}) custom-call(bf16[8,96,1024]{2,1,0:T(8,128)(2,1)} %tok_hbm.1, f32[32,32,384]{2,1,0:T(8,128)} %state_hbm.1), custom_call_target="tpu_custom_call" | custom-call | tf_op jit(solution)/shard_map/pallas_call | solution.py:610
  1.5 0.7 %collective-permute-start = (bf16[8,16,1024]{2,1,0:T(8,128)(2,1)S(1)}, bf16[8,16,1024]{2,1,0:T(8,128)(2,1)S(1)}, u32[]{:S(2)}, u32[]{:S(2)}) collective-permute-start(bf16[8,16,1024]{2,1,0:T(8,128)(2,1)S(1)} %get-tuple-element.34), channel_id=1, source_target_pairs={{0,1},{1,0},{2,3},{3,2},{4,5},{5,4},{6,7},{7,6},{8,9},{9,8},{10,11... | collective-permute-start | bytes 786440 | tf_op jit(solution)/shard_map/ppermute | solution.py:626
  2.3 0.1 collective-permute-start.1
  2.4 0.2 collective-permute-start.4
  2.6 0.9 %collective-permute-done.edge_ref = bf16[8,16,1024]{2,1,0:T(8,128)(2,1)S(1)} collective-permute-done((bf16[8,16,1024]{2,1,0:T(8,128)(2,1)S(1)}, bf16[8,16,1024]{2,1,0:T(8,128)(2,1)S(1)}, u32[]{:S(2)}, u32[]{:S(2)}) %collective-permute-start) | collective-permute-done | bytes 262176 | tf_op jit(solution)/shard_map/ppermute | solution.py:626
  3.5 0.0 copy-done.3
  3.5 0.0 copy-start.2
  3.5 7.7 %shard_map.119 = (bf16[384,3072]{1,0:T(8,128)(2,1)S(1)}, bf16[512,1024]{1,0:T(8,128)(2,1)S(1)}, bf16[512,1024]{1,0:T(8,128)(2,1)S(1)}, f32[512,384]{1,0:T(8,128)...) custom-call(bf16[8,96,1024]{2,1,0:T(8,128)(2,1)} %tok_hbm.1, ...), custom_call_target="tpu_custom_call" | custom-call | flops 7500000256 | bytes 7500000 | tf_op jit(solution)/shard_map/pallas_call | solution.py:639
  11.1 0.0 collective-permute-done.1.got_ref
  11.1 0.0 copy-done.2
  11.1 2.7 %shard_map.120 = (f32[512,768]{1,0:T(8,128)S(1)}, bf16[64,768]{1,0:T(8,128)(2,1)S(1)}) custom-call(f32[32,16,384]{2,1,0:T(8,128)S(1)} %get-tuple-element.35.state_ref, f32[32,16,384]{2,1,0:T(8,128)S(1)} %collective-permute-done.1.got_ref, f32[1,32]{1,0:T(1,128)S(1)} %bitcast.2, bf16[768,768]{1,0:T(8,128)(2,1)S(1)} %get-tuple-element.39.high_ref, ...), custom_call_target="tpu_custom_call" | custom-call | flops 2700000000 | bytes 2700000 | tf_op jit(solution)/shard_map/pallas_call | solution.py:668
  13.9 0.9 %collective-permute-start.2 = (bf16[64,768]{1,0:T(8,128)(2,1)S(1)}, bf16[64,768]{1,0:T(8,128)(2,1)S(1)}, u32[]{:S(2)}, u32[]{:S(2)}) collective-permute-start(bf16[64,768]{1,0:T(8,128)(2,1)S(1)} %get-tuple-element.43), channel_id=1, source_target_pairs={{0,1},{1,0},{2,3},{3,2},{4,5},{5,4},{6,7},{7,6},{8,9},{9,8},{10,11... | collective-permute-start | bytes 294920 | tf_op jit(solution)/shard_map/ppermute | solution.py:675
  14.8 0.9 %collective-permute-done.2.base_edge_ref = bf16[64,768]{1,0:T(8,128)(2,1)S(1)} collective-permute-done((bf16[64,768]{1,0:T(8,128)(2,1)S(1)}, bf16[64,768]{1,0:T(8,128)(2,1)S(1)}, u32[]{:S(2)}, u32[]{:S(2)}) %collective-permute-start.2) | collective-permute-done | bytes 98336 | tf_op jit(solution)/shard_map/ppermute | solution.py:675
  15.8 0.5 %collective-permute-start.3 = (bf16[176,1024]{1,0:T(8,128)(2,1)S(1)}, bf16[176,1024]{1,0:T(8,128)(2,1)S(1)}, u32[]{:S(2)}, u32[]{:S(2)}) collective-permute-start(bf16[176,1024]{1,0:T(8,128)(2,1)S(1)} %shard_map.121), channel_id=1, source_target_pairs={{0,2},{2,4},{4,6},{6,8},{8,10},{10,12},{12,14},{14,15},{3,1},{5,3}... | collective-permute-start | bytes 1081352 | tf_op jit(solution)/shard_map/ppermute | solution.py:681
  16.3 0.0 collective-permute-done.4.refs_0_
  16.3 6.1 %shard_map.122 = (bf16[512,256]{1,0:T(8,128)(2,1)S(1)}, bf16[576,256]{1,0:T(8,128)(2,1)S(1)}) custom-call(bf16[4,72,1024]{2,1,0:T(8,128)(2,1)S(1)} %collective-permute-done.4.refs_0_, f32[1,1024]{1,0:T(1,128)S(1)} %bitcast.8, bf16[384,3072]{1,0:T(8,128)(2,1)S(1)} %get-tuple-element.46.refs_2_.refs_3_, f32[512,384]{1,0:T(8,128)S(1)} %get-tuple-element.47.refs_3_.refs_4_, ...), custom_call_target="tpu_custom_call" | custom-call | flops 6000000000 | bytes 6000000 | tf_op jit(solution)/shard_map/pallas_call | solution.py:686
  22.4 0.0 copy-start
  22.4 0.0 copy-start.1
  22.4 5.1 %collective-permute-start.5 = (bf16[576,256]{1,0:T(8,128)(2,1)S(1)}, bf16[576,256]{1,0:T(8,128)(2,1)S(1)}, u32[]{:S(2)}, u32[]{:S(2)}) collective-permute-start(bf16[576,256]{1,0:T(8,128)(2,1)S(1)} %get-tuple-element.57.refs_2_), channel_id=1, source_target_pairs={{1,2},{3,4},{5,6},{7,8},{9,10},{11,12},{13,14},{2,1},{4,3},{6,5},{... | collective-permute-start | bytes 884744 | tf_op jit(solution)/shard_map/ppermute | solution.py:702
  27.5 0.0 collective-permute-done.3.refs_1_.piece_ref
  27.5 3.3 %shard_map.123 = (bf16[512,128]{1,0:T(8,128)(2,1)S(1)}, bf16[576,128]{1,0:T(8,128)(2,1)S(1)}) custom-call(bf16[4,72,1024]{2,1,0:T(8,128)(2,1)S(1)} %collective-permute-done.4.refs_0_, bf16[176,1024]{1,0:T(8,128)(2,1)S(1)} %collective-permute-done.3.refs_1_.piece_ref, f32[1,1024]{1,0:T(1,128)S(1)} %bitcast.9, ...), custom_call_target="tpu_custom_call" | custom-call | flops 3000000000 | bytes 3000000 | tf_op jit(solution)/shard_map/pallas_call | solution.py:686
  30.8 2.5 %collective-permute-start.6 = (bf16[576,128]{1,0:T(8,128)(2,1)S(1)}, bf16[576,128]{1,0:T(8,128)(2,1)S(1)}, u32[]{:S(2)}, u32[]{:S(2)}) collective-permute-start(bf16[576,128]{1,0:T(8,128)(2,1)S(1)} %get-tuple-element.58.refs_3_), channel_id=1, source_target_pairs={{1,2},{3,4},{5,6},{7,8},{9,10},{11,12},{13,14},{2,1},{4,3},{6,5},{... | collective-permute-start | bytes 442376 | tf_op jit(solution)/shard_map/ppermute | solution.py:702
  33.3 0.0 copy-done
  33.3 0.0 copy-done.1
  33.3 1.1 %shard_map.124.early_ref = f32[576,768]{1,0:T(8,128)S(1)} custom-call(f32[512,768]{1,0:T(8,128)S(1)} %get-tuple-element.41.base_ref, bf16[176,1024]{1,0:T(8,128)(2,1)S(1)} %collective-permute-done.3.refs_1_.piece_ref, f32[1,32]{1,0:T(1,128)S(1)} %bitcast.3, bf16[1152,768]{1,0:T(8,128)(2,1)S(1)} %copy-done.1, bf16[1152,768]{1,0:T(8,128)(2,1)S(1)} %copy-done, ...), custom_call_target="tpu_custom_call" | custom-call | flops 1200000000 | bytes 1200000 | tf_op jit(solution)/shard_map/pallas_call | solution.py:705
  34.4 0.0 collective-permute-done.5.got_ref
  34.4 0.6 %shard_map.125.early_ref = f32[576,768]{1,0:T(8,128)S(1)} custom-call(f32[576,768]{1,0:T(8,128)S(1)} %shard_map.124.early_ref, bf16[576,256]{1,0:T(8,128)(2,1)S(1)} %collective-permute-done.5.got_ref, f32[1,32]{1,0:T(1,128)S(1)} %bitcast.4, bf16[1152,768]{1,0:T(8,128)(2,1)S(1)} %copy-done.1, bf16[1152,768]{1,0:T(8,128)(2,1)S(1)} %copy-done), custom_call_target="tpu_custom_call" | custom-call | flops 1000000000 | bytes 1000000 | tf_op jit(solution)/shard_map/pallas_call | solution.py:710
  35.1 3.2 %collective-permute-done.6.got_ref = bf16[576,128]{1,0:T(8,128)(2,1)S(1)} collective-permute-done((bf16[576,128]{1,0:T(8,128)(2,1)S(1)}, bf16[576,128]{1,0:T(8,128)(2,1)S(1)}, u32[]{:S(2)}, u32[]{:S(2)}) %collective-permute-start.6) | collective-permute-done | bytes 147488 | tf_op jit(solution)/shard_map/ppermute | solution.py:702
  38.3 0.2 shard_map.127
  38.5 0.8 %collective-permute-start.7 = (bf16[64,768]{1,0:T(8,128)(2,1)S(1)}, bf16[64,768]{1,0:T(8,128)(2,1)S(1)}, u32[]{:S(2)}, u32[]{:S(2)}) collective-permute-start(bf16[64,768]{1,0:T(8,128)(2,1)S(1)} %shard_map.127), channel_id=1, source_target_pairs={{0,1},{1,0},{2,3},{3,2},{4,5},{5,4},{6,7},{7,6},{8,9},{9,8},{10,11... | collective-permute-start | bytes 294920 | tf_op jit(solution)/shard_map/ppermute | solution.py:714
  39.3 2.0 %shard_map.126 = (f32[512,768]{1,0:T(8,128)S(1)}, f32[64,768]{1,0:T(8,128)S(1)}, f32[512,768]{1,0:T(8,128)S(1)}, f32[512,768]{1,0:T(8,128)S(1)}) custom-call(f32[576,768]{1,0:T(8,128)S(1)} %shard_map.125.early_ref, bf16[576,128]{1,0:T(8,128)(2,1)S(1)} %collective-permute-done.6.got_ref, f32[1,32]{1,0:T(1,128)S(1)} %bitcast.6, ...), custom_call_target="tpu_custom_call" | custom-call | flops 2000000000 | bytes 2000000 | tf_op jit(solution)/shard_map/pallas_call | solution.py:718
  41.4 0.0 collective-permute-done.7.lon_ref
  41.4 1.6 %shard_map.128 = f32[32,16,768]{2,1,0:T(8,128)} custom-call(f32[512,768]{1,0:T(8,128)S(1)} %get-tuple-element.59.field_ref, f32[512,768]{1,0:T(8,128)S(1)} %get-tuple-element.60.first_ref, f32[512,768]{1,0:T(8,128)S(1)} %get-tuple-element.61.last_ref, bf16[64,768]{1,0:T(8,128)(2,1)S(1)} %collective-permute-done.7.lon_ref, ...), custom_call_target="tpu_custom_call" | custom-call | flops 1500000000 | bytes 1500000 | tf_op jit(solution)/shard_map/pallas_call | solution.py:720
  (1 shorter events, 0.0 us)
Async XLA Ops:
  0.0 3.5 %copy-start.3 = (f32[1024]{0:T(1024)S(1)}, f32[1024]{0:T(1024)}, u32[]{:S(2)}) copy-start(f32[1024]{0:T(1024)} %param.13) | copy-start | bytes 12292
  1.5 1.9 %collective-permute-start = (bf16[8,16,1024]{2,1,0:T(8,128)(2,1)S(1)}, bf16[8,16,1024]{2,1,0:T(8,128)(2,1)S(1)}, u32[]{:S(2)}, u32[]{:S(2)}) collective-permute-start(bf16[8,16,1024]{2,1,0:T(8,128)(2,1)S(1)} %get-tuple-element.34), channel_id=1, source_target_pairs={{0,1},{1,0},{2,3},{3,2},{4,5},{5,4},{6,7},{7,6},{8,9},{9,8},{10,11... | collective-permute-start | bytes 786440 | tf_op jit(solution)/shard_map/ppermute | solution.py:626
  2.3 8.8 %collective-permute-start.1 = (f32[32,16,384]{2,1,0:T(8,128)S(1)}, f32[32,16,384]{2,1,0:T(8,128)S(1)}, u32[]{:S(2)}, u32[]{:S(2)}) collective-permute-start(f32[32,16,384]{2,1,0:T(8,128)S(1)} %get-tuple-element.36), channel_id=1, source_target_pairs={{0,1},{1,0},{2,3},{3,2},{4,5},{5,4},{6,7},{7,6},{8,9},{9,8},{10,11... | collective-permute-start | bytes 2359304 | tf_op jit(solution)/shard_map/ppermute | solution.py:628
  2.4 13.9 %collective-permute-start.4 = (bf16[4,72,1024]{2,1,0:T(8,128)(2,1)S(1)}, bf16[4,72,1024]{2,1,0:T(8,128)(2,1)S(1)}, u32[]{:S(2)}, u32[]{:S(2)}) collective-permute-start(bf16[4,72,1024]{2,1,0:T(8,128)(2,1)S(1)} %get-tuple-element.45), channel_id=1, source_target_pairs={{0,2},{2,4},{4,6},{6,8},{8,10},{10,12},{12,14},{14,15},{3,1},{5,3}... | collective-permute-start | bytes 1769480 | tf_op jit(solution)/shard_map/ppermute | solution.py:627
  3.5 7.7 %copy-start.2 = (f32[32]{0:T(128)S(1)}, f32[32]{0:T(128)}, u32[]{:S(2)}) copy-start(f32[32]{0:T(128)} %param.18) | copy-start | bytes 388
  13.9 1.9 %collective-permute-start.2 = (bf16[64,768]{1,0:T(8,128)(2,1)S(1)}, bf16[64,768]{1,0:T(8,128)(2,1)S(1)}, u32[]{:S(2)}, u32[]{:S(2)}) collective-permute-start(bf16[64,768]{1,0:T(8,128)(2,1)S(1)} %get-tuple-element.43), channel_id=1, source_target_pairs={{0,1},{1,0},{2,3},{3,2},{4,5},{5,4},{6,7},{7,6},{8,9},{9,8},{10,11... | collective-permute-start | bytes 294920 | tf_op jit(solution)/shard_map/ppermute | solution.py:675
  15.8 11.7 %collective-permute-start.3 = (bf16[176,1024]{1,0:T(8,128)(2,1)S(1)}, bf16[176,1024]{1,0:T(8,128)(2,1)S(1)}, u32[]{:S(2)}, u32[]{:S(2)}) collective-permute-start(bf16[176,1024]{1,0:T(8,128)(2,1)S(1)} %shard_map.121), channel_id=1, source_target_pairs={{0,2},{2,4},{4,6},{6,8},{8,10},{10,12},{12,14},{14,15},{3,1},{5,3}... | collective-permute-start | bytes 1081352 | tf_op jit(solution)/shard_map/ppermute | solution.py:681
  22.4 10.9 %copy-start = (bf16[1152,768]{1,0:T(8,128)(2,1)S(1)}, bf16[1152,768]{1,0:T(8,128)(2,1)}, u32[]{:S(2)}) copy-start(bf16[1152,768]{1,0:T(8,128)(2,1)} %constant.11.clone.low_ref) | copy-start | bytes 5308420
  22.4 10.9 %copy-start.1 = (bf16[1152,768]{1,0:T(8,128)(2,1)S(1)}, bf16[1152,768]{1,0:T(8,128)(2,1)}, u32[]{:S(2)}) copy-start(bf16[1152,768]{1,0:T(8,128)(2,1)} %constant.10.clone.high_ref) | copy-start | bytes 5308420
  22.4 12.0 %collective-permute-start.5 = (bf16[576,256]{1,0:T(8,128)(2,1)S(1)}, bf16[576,256]{1,0:T(8,128)(2,1)S(1)}, u32[]{:S(2)}, u32[]{:S(2)}) collective-permute-start(bf16[576,256]{1,0:T(8,128)(2,1)S(1)} %get-tuple-element.57.refs_2_), channel_id=1, source_target_pairs={{1,2},{3,4},{5,6},{7,8},{9,10},{11,12},{13,14},{2,1},{4,3},{6,5},{... | collective-permute-start | bytes 884744 | tf_op jit(solution)/shard_map/ppermute | solution.py:702
  30.8 7.5 %collective-permute-start.6 = (bf16[576,128]{1,0:T(8,128)(2,1)S(1)}, bf16[576,128]{1,0:T(8,128)(2,1)S(1)}, u32[]{:S(2)}, u32[]{:S(2)}) collective-permute-start(bf16[576,128]{1,0:T(8,128)(2,1)S(1)} %get-tuple-element.58.refs_3_), channel_id=1, source_target_pairs={{1,2},{3,4},{5,6},{7,8},{9,10},{11,12},{13,14},{2,1},{4,3},{6,5},{... | collective-permute-start | bytes 442376 | tf_op jit(solution)/shard_map/ppermute | solution.py:702
  38.5 2.8 %collective-permute-start.7 = (bf16[64,768]{1,0:T(8,128)(2,1)S(1)}, bf16[64,768]{1,0:T(8,128)(2,1)S(1)}, u32[]{:S(2)}, u32[]{:S(2)}) collective-permute-start(bf16[64,768]{1,0:T(8,128)(2,1)S(1)} %shard_map.127), channel_id=1, source_target_pairs={{0,1},{1,0},{2,3},{3,2},{4,5},{5,4},{6,7},{7,6},{8,9},{9,8},{10,11... | collective-permute-start | bytes 294920 | tf_op jit(solution)/shard_map/ppermute | solution.py:714

commit v5 on v4

--- a/solution.py
+++ b/solution.py
@@ -79,14 +79,10 @@
     return lax.dot_general(a, b, (((1,), (1,)), ((), ())), preferred_element_type=F32)
 
 
-def window_tokens(load, first, cols, emit):
+def window_columns(here, after):
     lead = lax.broadcasted_iota(jnp.int32, (2 * WIN, 1), 0) % WIN < HALF
-    for pair in range(cols // (2 * WIN)):
-        col = first + pair * 2 * WIN
-        for r in range(HALF):
-            here = load(r, col, 2 * WIN)
-            after = load(r, col + 2 * WIN, WIN)
-            emit(pair, r, jnp.where(lead, jnp.concatenate([here[WIN:], after], axis=0), here))
+    here, after = here.astype(F32), after.astype(F32)
+    return jnp.where(lead, jnp.concatenate([here[WIN:], after], axis=0), here)
 
 
 def normalise(block, gain):
@@ -95,7 +91,7 @@
     return centred * lax.rsqrt(variance + epsilon) * gain
 
 
-def place_tokens(load, first, cols, gain, raw_ref, normed_ref):
+def place_tokens(load, cols, gain, raw_ref, normed_ref):
     held = {}
 
     def emit(pair, r, block):
@@ -110,7 +106,9 @@
                 both = jnp.concatenate([held[0][part], held[1][part]], axis=0)
                 normed_ref[at : at + 2 * WIN, :] = both.astype(BF16)
 
-    window_tokens(load, first, cols, emit)
+    for pair in range(cols // (2 * WIN)):
+        for r in range(HALF):
+            emit(pair, r, load(pair, r))
 
 
 def project(normed_ref, wq_ref, wkv_ref, qkv_ref, copies=()):
@@ -143,7 +141,11 @@
     ]
     copies = run_copies(sems, pairs)
     copies[0].wait()
-    give_ref[...] = whole_ref[:, : give_ref.shape[1], :]
+    for r in range(HALF):
+        for at in range(0, give_ref.shape[1], 2 * WIN):
+            after = whole_ref[r, at + 2 * WIN : at + 3 * WIN, :]
+            columns = window_columns(whole_ref[r, at : at + 2 * WIN, :], after)
+            give_ref[r, at : at + 2 * WIN, :] = columns.astype(BF16)
     for copy in copies[1:]:
         copy.wait()
 
@@ -162,13 +164,19 @@
     return places
 
 
-def last_piece_kernel(cols, more_ref, edge_ref, base_edge_ref, out_ref):
+def last_piece_kernel(more_ref, edge_ref, base_edge_ref, out_ref):
     lon = place()[0]
+    cols = more_ref.shape[1]
     for r in range(HALF):
-        own = more_ref[r].astype(F32)[more_ref.shape[1] - cols + WIN :]
-        after = edge_ref[HALF * (1 - lon) + r, :WIN, :].astype(F32)
-        out_ref[r * cols : (r + 1) * cols, :] = jnp.concatenate([own, after], axis=0).astype(BF16)
-    for (rows, lanes), (to_rows, to_lanes) in edge_blocks(base_edge_ref.shape[0], (base_edge_ref.shape[1], out_ref.shape[1])):
+        for at in range(0, cols, 2 * WIN):
+            if at + 2 * WIN < cols:
+                after = more_ref[r, at + 2 * WIN : at + 3 * WIN, :]
+            else:
+                after = edge_ref[HALF * (1 - lon) + r, :WIN, :]
+            columns = window_columns(more_ref[r, at : at + 2 * WIN, :], after)
+            out_ref[r * cols + at : r * cols + at + 2 * WIN, :] = columns.astype(BF16)
+    widths = (base_edge_ref.shape[1], out_ref.shape[1])
+    for (rows, lanes), (to_rows, to_lanes) in edge_blocks(base_edge_ref.shape[0], widths):
         at = slice(HALF * cols + to_rows.start, HALF * cols + to_rows.stop)
         out_ref[at, to_lanes] = base_edge_ref[rows, lanes]
 
@@ -221,13 +229,16 @@
         ],
     )
 
-    def load(r, c, size):
-        if c == cols:
-            return edge_ref[HALF * lon + r, :size, :].astype(F32)
-        return tok_ref[r, c : c + size, :].astype(F32)
+    def load(pair, r):
+        at = pair * 2 * WIN
+        if at + 2 * WIN < cols:
+            after = tok_ref[r, at + 2 * WIN : at + 3 * WIN, :]
+        else:
+            after = edge_ref[HALF * lon + r, :WIN, :]
+        return window_columns(tok_ref[r, at : at + 2 * WIN, :], after)
 
     copies[0].wait()
-    place_tokens(load, 0, cols, gain_ref[...], raw_ref, normed_ref)
+    place_tokens(load, cols, gain_ref[...], raw_ref, normed_ref)
     project(normed_ref, wq_ref, wkv_ref, qkv_ref, copies[1:4])
     outs = wdec_ref.shape[1]
     band = outs // PATCH
@@ -244,8 +255,7 @@
         copy.wait()
 
 
-def main_kernel(first, starts, *refs):
-    x_refs, refs = refs[: len(starts)], refs[len(starts) :]
+def main_kernel(first, x_ref, *refs):
     gain_ref, qkv_own_ref, decoded_own_ref, wq_ref, wkv_ref, wmix_ref, wdec_ref, *refs = refs
     keep_ref, send_ref, raw_ref, normed_ref, qkv_ref, att_ref, decoded_ref = refs
     width = raw_ref.shape[1]
@@ -259,15 +269,11 @@
     group_cols = GROUP * WIN
     group_half = GROUP * half_cells
 
-    def load(r, c, size):
-        which = max(i for i in range(len(starts)) if starts[i] <= c)
-        at = c - starts[which]
-        if which:
-            at += r * group_cols
-            return x_refs[which][at : at + size, :].astype(F32)
-        if at + size > x_refs[which].shape[1]:
-            return jnp.concatenate([load(r, c, size // 2), load(r, c + size // 2, size // 2)], axis=0)
-        return x_refs[which][r, at : at + size, :].astype(F32)
+    def load(pair, r):
+        at = pair * 2 * WIN
+        if len(x_ref.shape) == 2:
+            return x_ref[r * cols + at : r * cols + at + 2 * WIN, :].astype(F32)
+        return x_ref[r, at : at + 2 * WIN, :].astype(F32)
 
     def iota(shape, dim):
         return lax.broadcasted_iota(jnp.int32, shape, dim)
@@ -338,7 +344,7 @@
                     placed = moved if placed is None else jnp.where(lane_part == b, moved, placed)
                 out_ref[r * band : (r + 1) * band, out_lanes] = placed.astype(BF16)
 
-    place_tokens(load, first, cols, gain_ref[...], raw_ref, normed_ref)
+    place_tokens(load, cols, gain_ref[...], raw_ref, normed_ref)
     project_quad(0)
     units = [(group, quad) for group in range(cols // group_cols) for quad in range(quads)]
     weights = None
@@ -371,15 +377,34 @@
     return field - strength * smooth
 
 
-def state_kernel(state_ref, got_ref, nudge_ref, high_ref, low_ref, out_ref, edge_ref, whole_ref):
+def edge_kernel(state_ref, got_ref, nudge_ref, high_ref, low_ref, edge_ref, whole_ref):
+    lon = place()[0]
+    channels, own_rows, cols = got_ref.shape
+    depth = edge_ref.shape[0] // channels
+    own_lanes = pl.ds(pl.multiple_of(lon * cols, 128), cols)
+    got_lanes = pl.ds(pl.multiple_of((1 - lon) * cols, 128), cols)
+    near = pl.ds(pl.multiple_of(lon * (own_rows - 8), 8), 8)
+    for ch in range(0, channels, 8):
+        own = jnp.swapaxes(state_ref[ch : ch + 8, near, :], 0, 1)
+        got = jnp.swapaxes(got_ref[ch : ch + 8, near, :], 0, 1)
+        for i in range(depth):
+            rows = slice(i * channels + ch, i * channels + ch + 8)
+            whole_ref[rows, own_lanes] = jnp.where(lon == 0, own[i], own[8 - depth + i])
+            whole_ref[rows, got_lanes] = jnp.where(lon == 0, got[i], got[8 - depth + i])
+    strength = nudge_column(nudge_ref, depth * channels)
+    edge_ref[...] = unfiltered(whole_ref[...], high_ref, low_ref, strength).astype(BF16)
+
+
+def state_kernel(first, state_ref, got_ref, nudge_ref, high_ref, low_ref, out_ref, whole_ref):
     lon = place()[0]
     channels, own_rows, cols = got_ref.shape
     own_lanes = pl.ds(pl.multiple_of(lon * cols, 128), cols)
     got_lanes = pl.ds(pl.multiple_of((1 - lon) * cols, 128), cols)
-    for y in range(0, own_rows, 8):
+    for y in range(0, out_ref.shape[0] // channels, 8):
+        part = slice(first + y, first + y + 8)
         for ch in range(0, channels, 8):
-            own = jnp.swapaxes(state_ref[ch : ch + 8, y : y + 8, :], 0, 1)
-            got = jnp.swapaxes(got_ref[ch : ch + 8, y : y + 8, :], 0, 1)
+            own = jnp.swapaxes(state_ref[ch : ch + 8, part, :], 0, 1)
+            got = jnp.swapaxes(got_ref[ch : ch + 8, part, :], 0, 1)
             for i in range(8):
                 rows = slice((y + i) * channels + ch, (y + i) * channels + ch + 8)
                 whole_ref[rows, own_lanes] = own[i]
@@ -388,9 +413,6 @@
     strength = nudge_column(nudge_ref, step)
     for at in range(0, out_ref.shape[0], step):
         out_ref[at : at + step, :] = unfiltered(whole_ref[at : at + step, :], high_ref, low_ref, strength)
-    edge = edge_ref.shape[0]
-    near = pl.ds(pl.multiple_of(lon * (out_ref.shape[0] - edge), edge), edge)
-    edge_ref[...] = out_ref[near, :].astype(BF16)
 
 
 def filter_rows(dec, first, high_ref, low_ref):
@@ -398,11 +420,12 @@
     return dot(dec, high_ref[rows, :]) + dot(dec, low_ref[rows, :])
 
 
-def early_kernel(base_ref, piece_ref, nudge_ref, high_ref, low_ref, *refs):
+def early_kernel(upper_ref, lower_ref, piece_ref, nudge_ref, high_ref, low_ref, *refs):
     *refs, out_ref = refs
     keep_refs, send_refs = refs[: len(refs) // 2], refs[len(refs) // 2 :]
     lon = place()[0]
-    total = base_ref.shape[0]
+    half = upper_ref.shape[0]
+    total = half + lower_ref.shape[0]
     edge = out_ref.shape[0] - total
     far = pl.ds(pl.multiple_of((1 - lon) * (total - edge), edge), edge)
     own = [jnp.concatenate([keep[...], send[far, :]], axis=0) for keep, send in zip(keep_refs, send_refs)]
@@ -411,7 +434,8 @@
     step = PATCH * nudge_ref.shape[1]
     strength = nudge_column(nudge_ref, step)
     for at in range(0, total, step):
-        out_ref[at : at + step, :] = base_ref[at : at + step, :] + strength * smooth[at : at + step]
+        base_ref, begin = (upper_ref, at) if at < half else (lower_ref, at - half)
+        out_ref[at : at + step, :] = base_ref[begin : begin + step, :] + strength * smooth[at : at + step]
     length, width = out_ref.shape[1], piece_ref.shape[1]
     first = piece_ref.shape[0] - edge * length // width
     for (rows, lanes), (at_rows, at_lanes) in edge_blocks(edge, (length, width)):
@@ -601,16 +625,15 @@
     meet_all = meet + [(at(0, 0), at(0, 0)), (at(last, 1), at(last, 1))]
 
     step = GROUP * WIN
-    split = max(tok_cols - step, step)
-    chunks = [(0, split)] + ([(split, step)] if split < tok_cols else [])
-    cuts = [0] + [split + WIN] * (len(chunks) - 1) + [tok_cols]
+    split = tok_cols - step
+    chunks = [(0, split), (split, step)]
 
     hbm, vmem = pl.BlockSpec(memory_space=pltpu.HBM), pl.BlockSpec(memory_space=pltpu.VMEM)
     in_hbm = functools.partial(pltpu.with_memory_space_constraint, memory_space=pltpu.HBM)
     give, more, give_edge, give_state = pl.pallas_call(
         pack_kernel,
         out_shape=[
-            pltpu.VMEM((HALF, cuts[1], width), BF16),
+            pltpu.VMEM((HALF, split, width), BF16),
             pltpu.VMEM((HALF, step, width), BF16),
             pltpu.VMEM((tok_rows, 2 * WIN, width), BF16),
             pltpu.VMEM((channels, band_rows, state_cols), F32),
@@ -623,8 +646,8 @@
         ],
         compiler_params=pltpu.CompilerParams(vmem_limit_bytes=12 * MIB),
     )(in_hbm(tokens), in_hbm(state))
+    got_tokens = [lax.ppermute(give, both, shift)]
     edge_tokens = lax.ppermute(give_edge, "lon", swap)
-    got_tokens = [lax.ppermute(give, both, shift)]
     got_state = lax.ppermute(give_state, "lon", swap)
 
     gain = ln_gain[None, :]
@@ -665,17 +688,24 @@
 
     edge_rows = 2 * channels
     got_state, qkv_own = lax.optimization_barrier((got_state, qkv_own))
-    base, base_edge = call(
-        state_kernel,
-        (pltpu.VMEM((band, length), F32), pltpu.VMEM((edge_rows, length), BF16)),
+    base_edge = call(
+        edge_kernel,
+        pltpu.VMEM((edge_rows, length), BF16),
         5,
-        [pltpu.VMEM((band, length), F32)],
-        micros=2.7,
+        [pltpu.VMEM((edge_rows, length), F32)],
     )(own_state, got_state, nudge_row, high, low)
     their_base_edge = lax.ppermute(base_edge, "lon", swap)
-    last_cols = tok_cols - cuts[1] + WIN
-    last_rows = HALF * last_cols + edge_rows * length // width
-    last_piece = call(functools.partial(last_piece_kernel, last_cols), pltpu.VMEM((last_rows, width), BF16), 3, vmem=12)(
+
+    def state_half(first, rows):
+        half = pltpu.VMEM((band // 2, length), F32)
+        kernel = functools.partial(state_kernel, first)
+        return call(kernel, half, 5, [half], micros=1.4)(rows, got_state, nudge_row, high, low)
+
+    own_state, base_edge = lax.optimization_barrier((own_state, base_edge))
+    upper = state_half(0, own_state)
+    more, upper = lax.optimization_barrier((more, upper))
+    last_rows = HALF * step + edge_rows * length // width
+    last_piece = call(last_piece_kernel, pltpu.VMEM((last_rows, width), BF16), 3, vmem=12)(
         more, edge_tokens, their_base_edge
     )
     got_tokens.append(lax.ppermute(last_piece, both, shift))
@@ -684,9 +714,9 @@
     keep, send, got = [], [], []
     for i, (first, cols) in enumerate(chunks):
         kept, sent = call(
-            functools.partial(main_kernel, first, cuts[: i + 1]),
+            functools.partial(main_kernel, first),
             (pltpu.VMEM((band, cols * PATCH), BF16), pltpu.VMEM((band + edge_rows, cols * PATCH), BF16)),
-            7 + i + 1,
+            8,
             [
                 pltpu.VMEM((cols * HALF, width), BF16),
                 pltpu.VMEM((cols * HALF, width), BF16),
@@ -695,15 +725,16 @@
                 pltpu.VMEM((n_out, cols * HALF), F32),
             ],
             micros=3.0 * (cols // step),
-        )(*got_tokens[: i + 1], gain, qkv_own, decoded_own, *weights, w_mix_t, w_dec_t)
-        gain, kept = lax.optimization_barrier((gain, kept))
+        )(got_tokens[i], gain, qkv_own, decoded_own, *weights, w_mix_t, w_dec_t)
+        gain, kept, own_state = lax.optimization_barrier((gain, kept, own_state))
         keep.append(kept)
         send.append(sent)
         got.append(lax.ppermute(sent, both, meet_all))
 
+    lower = state_half(band_rows // 2, own_state)
     sums = pltpu.VMEM((band + edge_rows, length), F32)
-    early = call(early_kernel, sums, 5 + 2 * len(chunks), micros=1.2)(
-        base, got_tokens[-1], nudge_row, dec_high, dec_low, *keep, *send
+    early = call(early_kernel, sums, 6 + 2 * len(chunks), micros=1.2)(
+        upper, lower, got_tokens[-1], nudge_row, dec_high, dec_low, *keep, *send
     )
     skip = 0
     for part in got[:-1]:

time: 43.8 us -> 42.4 us (0.968)
  the two profiles are of different devices: /device:TPU:15 before, /device:TPU:0 now
where the time goes in v5:
time: 42.4 us; the launch traced here: 42.3 us
  Pallas kernels  27.9 us (66%)
  starting transfers between devices  12 us (28%)
  waiting for transfers between devices  2.03 us (5%)
    pallas_call x2, Pallas kernels, body(): call(functools.partial(main_kernel, first), (pltpu.VMEM((band, cols * PAT...  9.45 us
    pallas_call x1, Pallas kernels, body(): pl.pallas_call(own_kernel, out_shape=[pltpu.VMEM((tokens_half, 3 * width)...  7.67 us
    ppermute x1, starting transfers between devices, body(): from_lon = lax.ppermute(to_lon, 'lon', swap)  4.92 us
    ppermute x1, starting transfers between devices, body(): got_tokens = [lax.ppermute(give, both, shift)]  2.95 us
    pallas_call x2, Pallas kernels, state_half(): call(kernel, half, 5, [half], micros=1.4)  2.74 us
    pallas_call x1, Pallas kernels, body(): call(inner_kernel, (field, edge, field, field), 5, micros=2.0)(*late)  2.02 us
    ppermute x1, starting transfers between devices, body(): got_tokens.append(lax.ppermute(last_piece, both, shift))  1.76 us
    ppermute x2, starting transfers between devices, body(): got.append(lax.ppermute(sent, both, meet_all))  1.7 us
  transfers between devices with their start and end apart: 8, of which 2 were waited for; matrix products, arithmetic and copies ran while one was open for 0% of the time, Pallas kernels for 58%

profile of v5, /device:TPU:0, one launch (start us, length us, event | category | flops | bytes accessed | tf_op | source)
XLA Modules:
  0.0 42.3 jit_solution(16166212416545969388)
XLA Ops:
  0.0 0.0 copy-start.3
  0.0 1.5 %shard_map.118 = (bf16[4,64,1024]{2,1,0:T(8,128)(2,1)S(1)}, bf16[4,32,1024]{2,1,0:T(8,128)(2,1)S(1)}, bf16[8,16,1024]{2,1,0:T(8,128)(2,1)S(1)}, f32[32,16,384]{2,1,0:T(8,128)S(1)}) custom-call(bf16[8,96,1024]{2,1,0:T(8,128)(2,1)} %tok_hbm.1, f32[32,32,384]{2,1,0:T(8,128)} %state_hbm.1), custom_call_target="tpu_custom_call" | custom-call | tf_op jit(solution)/shard_map/pallas_call | solution.py:633
  1.5 0.5 %collective-permute-start = (bf16[8,16,1024]{2,1,0:T(8,128)(2,1)S(1)}, bf16[8,16,1024]{2,1,0:T(8,128)(2,1)S(1)}, u32[]{:S(2)}, u32[]{:S(2)}) collective-permute-start(bf16[8,16,1024]{2,1,0:T(8,128)(2,1)S(1)} %get-tuple-element.38), channel_id=1, source_target_pairs={{0,1},{1,0},{2,3},{3,2},{4,5},{5,4},{6,7},{7,6},{8,9},{9,8},{10,11... | collective-permute-start | bytes 786440 | tf_op jit(solution)/shard_map/ppermute | solution.py:650
  2.1 0.1 collective-permute-start.1
  2.1 2.9 %collective-permute-start.3 = (bf16[4,64,1024]{2,1,0:T(8,128)(2,1)S(1)}, bf16[4,64,1024]{2,1,0:T(8,128)(2,1)S(1)}, u32[]{:S(2)}, u32[]{:S(2)}) collective-permute-start(bf16[4,64,1024]{2,1,0:T(8,128)(2,1)S(1)} %get-tuple-element.49), channel_id=1, source_target_pairs={{0,2},{2,4},{4,6},{6,8},{8,10},{10,12},{12,14},{14,15},{3,1},{5,3}... | collective-permute-start | bytes 1572872 | tf_op jit(solution)/shard_map/ppermute | solution.py:649
  5.1 0.0 collective-permute-done.edge_ref
  5.1 0.0 copy-done.3
  5.1 0.0 copy-start.2
  5.1 7.7 %shard_map.119 = (bf16[384,3072]{1,0:T(8,128)(2,1)S(1)}, bf16[512,1024]{1,0:T(8,128)(2,1)S(1)}, bf16[512,1024]{1,0:T(8,128)(2,1)S(1)}, f32[512,384]{1,0:T(8,128)...) custom-call(bf16[8,96,1024]{2,1,0:T(8,128)(2,1)} %tok_hbm.1, ...), custom_call_target="tpu_custom_call" | custom-call | flops 7500000256 | bytes 7500000 | tf_op jit(solution)/shard_map/pallas_call | solution.py:662
  12.8 0.0 collective-permute-done.1.got_ref
  12.8 0.0 copy-done.2
  12.8 0.8 %shard_map.120 = bf16[64,768]{1,0:T(8,128)(2,1)S(1)} custom-call(f32[32,16,384]{2,1,0:T(8,128)S(1)} %get-tuple-element.60.state_ref, f32[32,16,384]{2,1,0:T(8,128)S(1)} %collective-permute-done.1.got_ref, f32[1,32]{1,0:T(1,128)S(1)} %bitcast.2, bf16[768,768]{1,0:T(8,128)(2,1)S(1)} %get-tuple-element.43.high_ref, bf16[768,768]{1,0:T(8,128)(2,1)S(1)} %get-tuple-element.44.low_ref), custom_call_target="tpu_custom_call" | custom-call | flops 1000000000 | bytes 1000000 | tf_op jit(solution)/shard_map/pallas_call | solution.py:691
  13.6 0.1 collective-permute-start.2
  13.7 1.4 %shard_map.121.upper_ref = f32[256,768]{1,0:T(8,128)S(1)} custom-call(f32[32,16,384]{2,1,0:T(8,128)S(1)} %get-tuple-element.60.state_ref, f32[32,16,384]{2,1,0:T(8,128)S(1)} %collective-permute-done.1.got_ref, f32[1,32]{1,0:T(1,128)S(1)} %bitcast.3, bf16[768,768]{1,0:T(8,128)(2,1)S(1)} %get-tuple-element.43.high_ref, ...), custom_call_target="tpu_custom_call" | custom-call | flops 1400000000 | bytes 1400000 | tf_op jit(solution)/shard_map/pallas_call | solution.py:702
  15.0 0.0 collective-permute-done.2.base_edge_ref
  15.1 0.1 shard_map.122
  15.1 1.8 %collective-permute-start.4 = (bf16[176,1024]{1,0:T(8,128)(2,1)S(1)}, bf16[176,1024]{1,0:T(8,128)(2,1)S(1)}, u32[]{:S(2)}, u32[]{:S(2)}) collective-permute-start(bf16[176,1024]{1,0:T(8,128)(2,1)S(1)} %shard_map.122), channel_id=1, source_target_pairs={{0,2},{2,4},{4,6},{6,8},{8,10},{10,12},{12,14},{14,15},{3,1},{5,3}... | collective-permute-start | bytes 1081352 | tf_op jit(solution)/shard_map/ppermute | solution.py:711
  16.9 0.5 %collective-permute-done.3.x_ref = bf16[4,64,1024]{2,1,0:T(8,128)(2,1)S(1)} collective-permute-done((bf16[4,64,1024]{2,1,0:T(8,128)(2,1)S(1)}, bf16[4,64,1024]{2,1,0:T(8,128)(2,1)S(1)}, u32[]{:S(2)}, u32[]{:S(2)}) %collective-permute-start.3) | collective-permute-done | bytes 524320 | tf_op jit(solution)/shard_map/ppermute | solution.py:649
  17.4 6.1 %shard_map.123 = (bf16[512,256]{1,0:T(8,128)(2,1)S(1)}, bf16[576,256]{1,0:T(8,128)(2,1)S(1)}) custom-call(bf16[4,64,1024]{2,1,0:T(8,128)(2,1)S(1)} %collective-permute-done.3.x_ref, f32[1,1024]{1,0:T(1,128)S(1)} %bitcast.10, bf16[384,3072]{1,0:T(8,128)(2,1)S(1)} %get-tuple-element.50.refs_1_, f32[512,384]{1,0:T(8,128)S(1)} %get-tuple-element.51.refs_2_, ...), custom_call_target="tpu_custom_call" | custom-call | flops 6000000000 | bytes 6000000 | tf_op jit(solution)/shard_map/pallas_call | solution.py:716
  23.5 0.7 %collective-permute-start.5 = (bf16[576,256]{1,0:T(8,128)(2,1)S(1)}, bf16[576,256]{1,0:T(8,128)(2,1)S(1)}, u32[]{:S(2)}, u32[]{:S(2)}) collective-permute-start(bf16[576,256]{1,0:T(8,128)(2,1)S(1)} %get-tuple-element.63.refs_2_), channel_id=1, source_target_pairs={{1,2},{3,4},{5,6},{7,8},{9,10},{11,12},{13,14},{2,1},{4,3},{6,5},{... | collective-permute-start | bytes 884744 | tf_op jit(solution)/shard_map/ppermute | solution.py:732
  24.2 1.5 %collective-permute-done.4.x_ref.piece_ref = bf16[176,1024]{1,0:T(8,128)(2,1)S(1)} collective-permute-done((bf16[176,1024]{1,0:T(8,128)(2,1)S(1)}, bf16[176,1024]{1,0:T(8,128)(2,1)S(1)}, u32[]{:S(2)}, u32[]{:S(2)}) %collective-permute-start.4) | collective-permute-done | bytes 360480 | tf_op jit(solution)/shard_map/ppermute | solution.py:711
  25.7 3.4 %shard_map.124 = (bf16[512,128]{1,0:T(8,128)(2,1)S(1)}, bf16[576,128]{1,0:T(8,128)(2,1)S(1)}) custom-call(bf16[176,1024]{1,0:T(8,128)(2,1)S(1)} %collective-permute-done.4.x_ref.piece_ref, f32[1,1024]{1,0:T(1,128)S(1)} %bitcast.11, bf16[384,3072]{1,0:T(8,128)(2,1)S(1)} %get-tuple-element.50.refs_1_, f32[512,384]{1,0:T(8,128)S(1)} %get-tuple-element.51.refs_2_, ...), custom_call_target="tpu_custom_call" | custom-call | flops 3000000000 | bytes 3000000 | tf_op jit(solution)/shard_map/pallas_call | solution.py:716
  29.1 0.0 copy-start
  29.1 0.0 copy-start.1
  29.1 1.0 %collective-permute-start.6 = (bf16[576,128]{1,0:T(8,128)(2,1)S(1)}, bf16[576,128]{1,0:T(8,128)(2,1)S(1)}, u32[]{:S(2)}, u32[]{:S(2)}) collective-permute-start(bf16[576,128]{1,0:T(8,128)(2,1)S(1)} %get-tuple-element.64.refs_3_), channel_id=1, source_target_pairs={{1,2},{3,4},{5,6},{7,8},{9,10},{11,12},{13,14},{2,1},{4,3},{6,5},{... | collective-permute-start | bytes 442376 | tf_op jit(solution)/shard_map/ppermute | solution.py:732
  30.1 1.4 %shard_map.125.lower_ref = f32[256,768]{1,0:T(8,128)S(1)} custom-call(f32[32,16,384]{2,1,0:T(8,128)S(1)} %get-tuple-element.60.state_ref, f32[32,16,384]{2,1,0:T(8,128)S(1)} %collective-permute-done.1.got_ref, f32[1,32]{1,0:T(1,128)S(1)} %bitcast.4, bf16[768,768]{1,0:T(8,128)(2,1)S(1)} %get-tuple-element.43.high_ref, ...), custom_call_target="tpu_custom_call" | custom-call | flops 1400000000 | bytes 1400000 | tf_op jit(solution)/shard_map/pallas_call | solution.py:702
  31.5 0.0 copy-done
  31.5 0.0 copy-done.1
  31.5 1.1 %shard_map.126.early_ref = f32[576,768]{1,0:T(8,128)S(1)} custom-call(f32[256,768]{1,0:T(8,128)S(1)} %shard_map.121.upper_ref, f32[256,768]{1,0:T(8,128)S(1)} %shard_map.125.lower_ref, bf16[176,1024]{1,0:T(8,128)(2,1)S(1)} %collective-permute-done.4.x_ref.piece_ref, f32[1,32]{1,0:T(1,128)S(1)} %bitcast.5, bf16[1152,768]{1,0:T(8,128)(2,1)S(1)} %copy-done, ...), custom_call_target="tpu_custom_call" | custom-call | flops 1200000000 | bytes 1200000 | tf_op jit(solution)/shard_map/pallas_call | solution.py:736
  32.6 0.0 collective-permute-done.5.got_ref
  32.6 0.6 %shard_map.127.early_ref = f32[576,768]{1,0:T(8,128)S(1)} custom-call(f32[576,768]{1,0:T(8,128)S(1)} %shard_map.126.early_ref, bf16[576,256]{1,0:T(8,128)(2,1)S(1)} %collective-permute-done.5.got_ref, f32[1,32]{1,0:T(1,128)S(1)} %bitcast.6, bf16[1152,768]{1,0:T(8,128)(2,1)S(1)} %copy-done, bf16[1152,768]{1,0:T(8,128)(2,1)S(1)} %copy-done.1), custom_call_target="tpu_custom_call" | custom-call | flops 1000000000 | bytes 1000000 | tf_op jit(solution)/shard_map/pallas_call | solution.py:741
  33.3 0.0 collective-permute-done.6.got_ref
  33.3 0.2 shard_map.129
  33.5 4.9 %collective-permute-start.7 = (bf16[64,768]{1,0:T(8,128)(2,1)S(1)}, bf16[64,768]{1,0:T(8,128)(2,1)S(1)}, u32[]{:S(2)}, u32[]{:S(2)}) collective-permute-start(bf16[64,768]{1,0:T(8,128)(2,1)S(1)} %shard_map.129), channel_id=1, source_target_pairs={{0,1},{1,0},{2,3},{3,2},{4,5},{5,4},{6,7},{7,6},{8,9},{9,8},{10,11... | collective-permute-start | bytes 294920 | tf_op jit(solution)/shard_map/ppermute | solution.py:745
  38.4 2.0 %shard_map.128 = (f32[512,768]{1,0:T(8,128)S(1)}, f32[64,768]{1,0:T(8,128)S(1)}, f32[512,768]{1,0:T(8,128)S(1)}, f32[512,768]{1,0:T(8,128)S(1)}) custom-call(f32[576,768]{1,0:T(8,128)S(1)} %shard_map.127.early_ref, bf16[576,128]{1,0:T(8,128)(2,1)S(1)} %collective-permute-done.6.got_ref, f32[1,32]{1,0:T(1,128)S(1)} %bitcast.8, bf16[1152,768]{1,0:T(8,128)(2,1)S(1)} %copy-done, ...), custom_call_target="tpu_custom_call" | custom-call | flops 2000000000 | bytes 2000000 | tf_op jit(solution)/shard_map/pallas_call | solution.py:749
  40.5 0.0 collective-permute-done.7.lon_ref
  40.5 1.7 %shard_map.130 = f32[32,16,768]{2,1,0:T(8,128)} custom-call(f32[512,768]{1,0:T(8,128)S(1)} %get-tuple-element.65.field_ref, f32[512,768]{1,0:T(8,128)S(1)} %get-tuple-element.66.first_ref, f32[512,768]{1,0:T(8,128)S(1)} %get-tuple-element.67.last_ref, bf16[64,768]{1,0:T(8,128)(2,1)S(1)} %collective-permute-done.7.lon_ref, ...), custom_call_target="tpu_custom_call" | custom-call | flops 1500000000 | bytes 1500000 | tf_op jit(solution)/shard_map/pallas_call | solution.py:751
Async XLA Ops:
  0.0 5.1 %copy-start.3 = (f32[1024]{0:T(1024)S(1)}, f32[1024]{0:T(1024)}, u32[]{:S(2)}) copy-start(f32[1024]{0:T(1024)} %param.13) | copy-start | bytes 12292
  1.5 3.5 %collective-permute-start = (bf16[8,16,1024]{2,1,0:T(8,128)(2,1)S(1)}, bf16[8,16,1024]{2,1,0:T(8,128)(2,1)S(1)}, u32[]{:S(2)}, u32[]{:S(2)}) collective-permute-start(bf16[8,16,1024]{2,1,0:T(8,128)(2,1)S(1)} %get-tuple-element.38), channel_id=1, source_target_pairs={{0,1},{1,0},{2,3},{3,2},{4,5},{5,4},{6,7},{7,6},{8,9},{9,8},{10,11... | collective-permute-start | bytes 786440 | tf_op jit(solution)/shard_map/ppermute | solution.py:650
  2.1 10.7 %collective-permute-start.1 = (f32[32,16,384]{2,1,0:T(8,128)S(1)}, f32[32,16,384]{2,1,0:T(8,128)S(1)}, u32[]{:S(2)}, u32[]{:S(2)}) collective-permute-start(f32[32,16,384]{2,1,0:T(8,128)S(1)} %get-tuple-element.40), channel_id=1, source_target_pairs={{0,1},{1,0},{2,3},{3,2},{4,5},{5,4},{6,7},{7,6},{8,9},{9,8},{10,11... | collective-permute-start | bytes 2359304 | tf_op jit(solution)/shard_map/ppermute | solution.py:651
  2.1 15.3 %collective-permute-start.3 = (bf16[4,64,1024]{2,1,0:T(8,128)(2,1)S(1)}, bf16[4,64,1024]{2,1,0:T(8,128)(2,1)S(1)}, u32[]{:S(2)}, u32[]{:S(2)}) collective-permute-start(bf16[4,64,1024]{2,1,0:T(8,128)(2,1)S(1)} %get-tuple-element.49), channel_id=1, source_target_pairs={{0,2},{2,4},{4,6},{6,8},{8,10},{10,12},{12,14},{14,15},{3,1},{5,3}... | collective-permute-start | bytes 1572872 | tf_op jit(solution)/shard_map/ppermute | solution.py:649
  5.1 7.7 %copy-start.2 = (f32[32]{0:T(128)S(1)}, f32[32]{0:T(128)}, u32[]{:S(2)}) copy-start(f32[32]{0:T(128)} %param.18) | copy-start | bytes 388
  13.6 1.5 %collective-permute-start.2 = (bf16[64,768]{1,0:T(8,128)(2,1)S(1)}, bf16[64,768]{1,0:T(8,128)(2,1)S(1)}, u32[]{:S(2)}, u32[]{:S(2)}) collective-permute-start(bf16[64,768]{1,0:T(8,128)(2,1)S(1)} %shard_map.120), channel_id=1, source_target_pairs={{0,1},{1,0},{2,3},{3,2},{4,5},{5,4},{6,7},{7,6},{8,9},{9,8},{10,11... | collective-permute-start | bytes 294920 | tf_op jit(solution)/shard_map/ppermute | solution.py:697
  15.1 10.6 %collective-permute-start.4 = (bf16[176,1024]{1,0:T(8,128)(2,1)S(1)}, bf16[176,1024]{1,0:T(8,128)(2,1)S(1)}, u32[]{:S(2)}, u32[]{:S(2)}) collective-permute-start(bf16[176,1024]{1,0:T(8,128)(2,1)S(1)} %shard_map.122), channel_id=1, source_target_pairs={{0,2},{2,4},{4,6},{6,8},{8,10},{10,12},{12,14},{14,15},{3,1},{5,3}... | collective-permute-start | bytes 1081352 | tf_op jit(solution)/shard_map/ppermute | solution.py:711
  23.5 9.1 %collective-permute-start.5 = (bf16[576,256]{1,0:T(8,128)(2,1)S(1)}, bf16[576,256]{1,0:T(8,128)(2,1)S(1)}, u32[]{:S(2)}, u32[]{:S(2)}) collective-permute-start(bf16[576,256]{1,0:T(8,128)(2,1)S(1)} %get-tuple-element.63.refs_2_), channel_id=1, source_target_pairs={{1,2},{3,4},{5,6},{7,8},{9,10},{11,12},{13,14},{2,1},{4,3},{6,5},{... | collective-permute-start | bytes 884744 | tf_op jit(solution)/shard_map/ppermute | solution.py:732
  29.1 2.4 %copy-start = (bf16[1152,768]{1,0:T(8,128)(2,1)S(1)}, bf16[1152,768]{1,0:T(8,128)(2,1)}, u32[]{:S(2)}) copy-start(bf16[1152,768]{1,0:T(8,128)(2,1)} %constant.10.clone.high_ref) | copy-start | bytes 5308420
  29.1 2.4 %copy-start.1 = (bf16[1152,768]{1,0:T(8,128)(2,1)S(1)}, bf16[1152,768]{1,0:T(8,128)(2,1)}, u32[]{:S(2)}) copy-start(bf16[1152,768]{1,0:T(8,128)(2,1)} %constant.11.clone.low_ref) | copy-start | bytes 5308420
  29.1 4.2 %collective-permute-start.6 = (bf16[576,128]{1,0:T(8,128)(2,1)S(1)}, bf16[576,128]{1,0:T(8,128)(2,1)S(1)}, u32[]{:S(2)}, u32[]{:S(2)}) collective-permute-start(bf16[576,128]{1,0:T(8,128)(2,1)S(1)} %get-tuple-element.64.refs_3_), channel_id=1, source_target_pairs={{1,2},{3,4},{5,6},{7,8},{9,10},{11,12},{13,14},{2,1},{4,3},{6,5},{... | collective-permute-start | bytes 442376 | tf_op jit(solution)/shard_map/ppermute | solution.py:732
  33.5 7.0 %collective-permute-start.7 = (bf16[64,768]{1,0:T(8,128)(2,1)S(1)}, bf16[64,768]{1,0:T(8,128)(2,1)S(1)}, u32[]{:S(2)}, u32[]{:S(2)}) collective-permute-start(bf16[64,768]{1,0:T(8,128)(2,1)S(1)} %shard_map.129), channel_id=1, source_target_pairs={{0,1},{1,0},{2,3},{3,2},{4,5},{5,4},{6,7},{7,6},{8,9},{9,8},{10,11... | collective-permute-start | bytes 294920 | tf_op jit(solution)/shard_map/ppermute | solution.py:745

commit v6 on v5

--- a/solution.py
+++ b/solution.py
@@ -349,19 +349,21 @@
     units = [(group, quad) for group in range(cols // group_cols) for quad in range(quads)]
     weights = None
     for i in range(len(units) + 1):
+        held = weights
         if i < len(units):
             group, quad = units[i]
-            scores = [score(group * GROUP + w, quad) for w in range(GROUP)]
-            if group == 0 and quad + 1 < quads:
-                project_quad(quad + 1)
-            if i == quads - 1:
+            weights = []
+            for w in range(GROUP):
+                scores = score(group * GROUP + w, quad)
+                if w == 1 and group == 0 and quad + 1 < quads:
+                    project_quad(quad + 1)
+                weights.append(weigh(scores))
+            if i == 0:
                 decoded_ref[...] = dot_nt(wdec_ref[...], raw_ref[...])
         if i > 0:
-            mix(*units[i - 1], weights)
+            mix(*units[i - 1], held)
             if units[i - 1][1] == quads - 1:
                 decode(units[i - 1][0])
-        if i < len(units):
-            weights = [weigh(x) for x in scores]
 
     lon = place()[0]
     total_rows = keep_ref.shape[0]
@@ -488,12 +490,12 @@
     total = field_ref.shape[0]
     edge = lat_ref.shape[0]
     rows = total // (VARS * LEV)
-    smooth = filter_rows(got_ref[...], last_rows(high_ref, got_ref), high_ref, low_ref)
     step = PATCH * nudge_ref.shape[1]
     strength = nudge_column(nudge_ref, step)
-    for at in range(0, total, step):
-        field_ref[at : at + step, :] = early_ref[at : at + step, :] + strength * smooth[at : at + step]
-    lat_ref[...] = early_ref[total:, :] + strength[:edge] * smooth[total:]
+    first_lane = last_rows(high_ref, got_ref)
+
+    def smooth_rows(at, size):
+        return filter_rows(got_ref[at : at + size, :], first_lane, high_ref, low_ref)
 
     def reader(ref, row):
         return lambda var: ref[row_tile(ref, row, var), :]
@@ -501,19 +503,35 @@
     def section(ref, row, use):
         tendency_row(reader(ref, row - 1), reader(ref, row), reader(ref, row + 1), use)
 
-    for row in range(1, rows - 1):
-
-        def put_first(var, field, step):
+    def first_row(row):
+        def put(var, field, step):
             first_ref[row_tile(first_ref, row, var), :] = field + step
 
-        section(field_ref, row, put_first)
-    for row in range(2, rows - 2):
-
-        def put_last(var, field, step):
+        section(field_ref, row, put)
+
+    def last_row(row):
+        def put(var, field, step):
             nudged = field_ref[row_tile(field_ref, row, var), :]
             last_ref[row_tile(last_ref, row, var), :] = 0.5 * (nudged + field + step)
 
-        section(first_ref, row, put_last)
+        section(first_ref, row, put)
+
+    smooth = smooth_rows(0, step)
+    next_first, next_last = 1, 2
+    for at in range(0, total, step):
+        field_ref[at : at + step, :] = early_ref[at : at + step, :] + strength * smooth
+        if at + step < total:
+            smooth = smooth_rows(at + step, step)
+        else:
+            smooth = smooth_rows(total, edge)
+        ready = (at + step) // (VARS * LEV)
+        while next_first <= min(rows - 2, ready - 2):
+            first_row(next_first)
+            next_first += 1
+        while next_last <= min(rows - 3, next_first - 2):
+            last_row(next_last)
+            next_last += 1
+    lat_ref[...] = early_ref[total:, :] + strength[:edge] * smooth
 
 
 def outer_kernel(field_ref, first_ref, last_ref, lon_ref, lat_ref, out_hbm, ext_ref, edge_ref, out_ref, sems):

time: 42.4 us -> 42.3 us (level)
  the two profiles are of different devices: /device:TPU:0 before, /device:TPU:15 now
where the time goes in v6:
time: 42.3 us; the launch traced here: 41.6 us
  Pallas kernels  27.7 us (65%)
  starting transfers between devices  10.7 us (25%)
  waiting for transfers between devices  2.75 us (7%)
    pallas_call x2, Pallas kernels, body(): call(functools.partial(main_kernel, first), (pltpu.VMEM((band, cols * PAT...  9.29 us
    pallas_call x1, Pallas kernels, body(): pl.pallas_call(own_kernel, out_shape=[pltpu.VMEM((tokens_half, 3 * width)...  7.67 us
    ppermute x2, starting transfers between devices, body(): got.append(lax.ppermute(sent, both, meet_all))  7.54 us
    pallas_call x2, Pallas kernels, state_half(): call(kernel, half, 5, [half], micros=1.4)  2.74 us
    pallas_call x1, Pallas kernels, body(): call(inner_kernel, (field, edge, field, field), 5, micros=2.0)(*late)  1.98 us
    ppermute x2, waiting for transfers between devices, body(): got.append(lax.ppermute(sent, both, meet_all))  1.88 us
    pallas_call x1, Pallas kernels, body(): pl.pallas_call(outer_kernel, out_shape=jax.ShapeDtypeStruct(result, F32),...  1.65 us
    pallas_call x1, Pallas kernels, body(): pl.pallas_call(pack_kernel, out_shape=[pltpu.VMEM((HALF, split, width), B...  1.54 us
  transfers between devices with their start and end apart: 8, of which 2 were waited for; matrix products, arithmetic and copies ran while one was open for 0% of the time, Pallas kernels for 58%

profile of v6, /device:TPU:15, one launch (start us, length us, event | category | flops | bytes accessed | tf_op | source)
XLA Modules:
  0.0 41.6 jit_solution(5163034268001719614)
XLA Ops:
  0.0 0.0 copy-start.3
  0.0 1.5 %shard_map.118 = (bf16[4,64,1024]{2,1,0:T(8,128)(2,1)S(1)}, bf16[4,32,1024]{2,1,0:T(8,128)(2,1)S(1)}, bf16[8,16,1024]{2,1,0:T(8,128)(2,1)S(1)}, f32[32,16,384]{2,1,0:T(8,128)S(1)}) custom-call(bf16[8,96,1024]{2,1,0:T(8,128)(2,1)} %tok_hbm.1, f32[32,32,384]{2,1,0:T(8,128)} %state_hbm.1), custom_call_target="tpu_custom_call" | custom-call | tf_op jit(solution)/shard_map/pallas_call | solution.py:651
  1.5 0.7 %collective-permute-start = (bf16[8,16,1024]{2,1,0:T(8,128)(2,1)S(1)}, bf16[8,16,1024]{2,1,0:T(8,128)(2,1)S(1)}, u32[]{:S(2)}, u32[]{:S(2)}) collective-permute-start(bf16[8,16,1024]{2,1,0:T(8,128)(2,1)S(1)} %get-tuple-element.38), channel_id=1, source_target_pairs={{0,1},{1,0},{2,3},{3,2},{4,5},{5,4},{6,7},{7,6},{8,9},{9,8},{10,11... | collective-permute-start | bytes 786440 | tf_op jit(solution)/shard_map/ppermute | solution.py:668
  2.3 0.1 collective-permute-start.1
  2.4 0.2 collective-permute-start.3
  2.6 0.9 %collective-permute-done.edge_ref = bf16[8,16,1024]{2,1,0:T(8,128)(2,1)S(1)} collective-permute-done((bf16[8,16,1024]{2,1,0:T(8,128)(2,1)S(1)}, bf16[8,16,1024]{2,1,0:T(8,128)(2,1)S(1)}, u32[]{:S(2)}, u32[]{:S(2)}) %collective-permute-start) | collective-permute-done | bytes 262176 | tf_op jit(solution)/shard_map/ppermute | solution.py:668
  3.5 0.0 copy-done.3
  3.5 0.0 copy-start.2
  3.5 7.7 %shard_map.119 = (bf16[384,3072]{1,0:T(8,128)(2,1)S(1)}, bf16[512,1024]{1,0:T(8,128)(2,1)S(1)}, bf16[512,1024]{1,0:T(8,128)(2,1)S(1)}, f32[512,384]{1,0:T(8,128)...) custom-call(bf16[8,96,1024]{2,1,0:T(8,128)(2,1)} %tok_hbm.1, ...), custom_call_target="tpu_custom_call" | custom-call | flops 7500000256 | bytes 7500000 | tf_op jit(solution)/shard_map/pallas_call | solution.py:680
  11.1 0.0 collective-permute-done.1.got_ref
  11.1 0.0 copy-done.2
  11.2 0.8 %shard_map.120 = bf16[64,768]{1,0:T(8,128)(2,1)S(1)} custom-call(f32[32,16,384]{2,1,0:T(8,128)S(1)} %get-tuple-element.60.state_ref, f32[32,16,384]{2,1,0:T(8,128)S(1)} %collective-permute-done.1.got_ref, f32[1,32]{1,0:T(1,128)S(1)} %bitcast.2, bf16[768,768]{1,0:T(8,128)(2,1)S(1)} %get-tuple-element.43.high_ref, bf16[768,768]{1,0:T(8,128)(2,1)S(1)} %get-tuple-element.44.low_ref), custom_call_target="tpu_custom_call" | custom-call | flops 1000000000 | bytes 1000000 | tf_op jit(solution)/shard_map/pallas_call | solution.py:709
  12.0 0.9 %collective-permute-start.2 = (bf16[64,768]{1,0:T(8,128)(2,1)S(1)}, bf16[64,768]{1,0:T(8,128)(2,1)S(1)}, u32[]{:S(2)}, u32[]{:S(2)}) collective-permute-start(bf16[64,768]{1,0:T(8,128)(2,1)S(1)} %shard_map.120), channel_id=1, source_target_pairs={{0,1},{1,0},{2,3},{3,2},{4,5},{5,4},{6,7},{7,6},{8,9},{9,8},{10,11... | collective-permute-start | bytes 294920 | tf_op jit(solution)/shard_map/ppermute | solution.py:715
  12.9 1.4 %shard_map.121.upper_ref = f32[256,768]{1,0:T(8,128)S(1)} custom-call(f32[32,16,384]{2,1,0:T(8,128)S(1)} %get-tuple-element.60.state_ref, f32[32,16,384]{2,1,0:T(8,128)S(1)} %collective-permute-done.1.got_ref, f32[1,32]{1,0:T(1,128)S(1)} %bitcast.3, bf16[768,768]{1,0:T(8,128)(2,1)S(1)} %get-tuple-element.43.high_ref, ...), custom_call_target="tpu_custom_call" | custom-call | flops 1400000000 | bytes 1400000 | tf_op jit(solution)/shard_map/pallas_call | solution.py:720
  14.3 0.0 collective-permute-done.2.base_edge_ref
  14.3 0.1 shard_map.122
  14.3 0.5 %collective-permute-start.4 = (bf16[176,1024]{1,0:T(8,128)(2,1)S(1)}, bf16[176,1024]{1,0:T(8,128)(2,1)S(1)}, u32[]{:S(2)}, u32[]{:S(2)}) collective-permute-start(bf16[176,1024]{1,0:T(8,128)(2,1)S(1)} %shard_map.122), channel_id=1, source_target_pairs={{0,2},{2,4},{4,6},{6,8},{8,10},{10,12},{12,14},{14,15},{3,1},{5,3}... | collective-permute-start | bytes 1081352 | tf_op jit(solution)/shard_map/ppermute | solution.py:729
  14.8 0.0 collective-permute-done.3.x_ref
  14.8 6.1 %shard_map.123 = (bf16[512,256]{1,0:T(8,128)(2,1)S(1)}, bf16[576,256]{1,0:T(8,128)(2,1)S(1)}) custom-call(bf16[4,64,1024]{2,1,0:T(8,128)(2,1)S(1)} %collective-permute-done.3.x_ref, f32[1,1024]{1,0:T(1,128)S(1)} %bitcast.10, bf16[384,3072]{1,0:T(8,128)(2,1)S(1)} %get-tuple-element.50.refs_1_, f32[512,384]{1,0:T(8,128)S(1)} %get-tuple-element.51.refs_2_, ...), custom_call_target="tpu_custom_call" | custom-call | flops 6000000000 | bytes 6000000 | tf_op jit(solution)/shard_map/pallas_call | solution.py:734
  20.9 4.9 %collective-permute-start.5 = (bf16[576,256]{1,0:T(8,128)(2,1)S(1)}, bf16[576,256]{1,0:T(8,128)(2,1)S(1)}, u32[]{:S(2)}, u32[]{:S(2)}) collective-permute-start(bf16[576,256]{1,0:T(8,128)(2,1)S(1)} %get-tuple-element.63.refs_2_), channel_id=1, source_target_pairs={{1,2},{3,4},{5,6},{7,8},{9,10},{11,12},{13,14},{2,1},{4,3},{6,5},{... | collective-permute-start | bytes 884744 | tf_op jit(solution)/shard_map/ppermute | solution.py:750
  25.8 0.0 collective-permute-done.4.x_ref.piece_ref
  25.8 3.2 %shard_map.124 = (bf16[512,128]{1,0:T(8,128)(2,1)S(1)}, bf16[576,128]{1,0:T(8,128)(2,1)S(1)}) custom-call(bf16[176,1024]{1,0:T(8,128)(2,1)S(1)} %collective-permute-done.4.x_ref.piece_ref, f32[1,1024]{1,0:T(1,128)S(1)} %bitcast.11, bf16[384,3072]{1,0:T(8,128)(2,1)S(1)} %get-tuple-element.50.refs_1_, f32[512,384]{1,0:T(8,128)S(1)} %get-tuple-element.51.refs_2_, ...), custom_call_target="tpu_custom_call" | custom-call | flops 3000000000 | bytes 3000000 | tf_op jit(solution)/shard_map/pallas_call | solution.py:734
  29.0 0.0 copy-start
  29.0 0.0 copy-start.1
  29.0 2.7 %collective-permute-start.6 = (bf16[576,128]{1,0:T(8,128)(2,1)S(1)}, bf16[576,128]{1,0:T(8,128)(2,1)S(1)}, u32[]{:S(2)}, u32[]{:S(2)}) collective-permute-start(bf16[576,128]{1,0:T(8,128)(2,1)S(1)} %get-tuple-element.64.refs_3_), channel_id=1, source_target_pairs={{1,2},{3,4},{5,6},{7,8},{9,10},{11,12},{13,14},{2,1},{4,3},{6,5},{... | collective-permute-start | bytes 442376 | tf_op jit(solution)/shard_map/ppermute | solution.py:750
  31.7 1.4 %shard_map.125.lower_ref = f32[256,768]{1,0:T(8,128)S(1)} custom-call(f32[32,16,384]{2,1,0:T(8,128)S(1)} %get-tuple-element.60.state_ref, f32[32,16,384]{2,1,0:T(8,128)S(1)} %collective-permute-done.1.got_ref, f32[1,32]{1,0:T(1,128)S(1)} %bitcast.4, bf16[768,768]{1,0:T(8,128)(2,1)S(1)} %get-tuple-element.43.high_ref, ...), custom_call_target="tpu_custom_call" | custom-call | flops 1400000000 | bytes 1400000 | tf_op jit(solution)/shard_map/pallas_call | solution.py:720
  33.1 0.0 copy-done
  33.1 0.0 copy-done.1
  33.1 1.1 %shard_map.126.early_ref = f32[576,768]{1,0:T(8,128)S(1)} custom-call(f32[256,768]{1,0:T(8,128)S(1)} %shard_map.121.upper_ref, f32[256,768]{1,0:T(8,128)S(1)} %shard_map.125.lower_ref, bf16[176,1024]{1,0:T(8,128)(2,1)S(1)} %collective-permute-done.4.x_ref.piece_ref, f32[1,32]{1,0:T(1,128)S(1)} %bitcast.5, bf16[1152,768]{1,0:T(8,128)(2,1)S(1)} %copy-done, ...), custom_call_target="tpu_custom_call" | custom-call | flops 1200000000 | bytes 1200000 | tf_op jit(solution)/shard_map/pallas_call | solution.py:754
  34.2 0.0 collective-permute-done.5.got_ref
  34.2 0.6 %shard_map.127.early_ref = f32[576,768]{1,0:T(8,128)S(1)} custom-call(f32[576,768]{1,0:T(8,128)S(1)} %shard_map.126.early_ref, bf16[576,256]{1,0:T(8,128)(2,1)S(1)} %collective-permute-done.5.got_ref, f32[1,32]{1,0:T(1,128)S(1)} %bitcast.6, bf16[1152,768]{1,0:T(8,128)(2,1)S(1)} %copy-done, bf16[1152,768]{1,0:T(8,128)(2,1)S(1)} %copy-done.1), custom_call_target="tpu_custom_call" | custom-call | flops 1000000000 | bytes 1000000 | tf_op jit(solution)/shard_map/pallas_call | solution.py:759
  34.9 1.9 %collective-permute-done.6.got_ref = bf16[576,128]{1,0:T(8,128)(2,1)S(1)} collective-permute-done((bf16[576,128]{1,0:T(8,128)(2,1)S(1)}, bf16[576,128]{1,0:T(8,128)(2,1)S(1)}, u32[]{:S(2)}, u32[]{:S(2)}) %collective-permute-start.6) | collective-permute-done | bytes 147488 | tf_op jit(solution)/shard_map/ppermute | solution.py:750
  36.8 0.2 shard_map.129
  37.0 0.8 %collective-permute-start.7 = (bf16[64,768]{1,0:T(8,128)(2,1)S(1)}, bf16[64,768]{1,0:T(8,128)(2,1)S(1)}, u32[]{:S(2)}, u32[]{:S(2)}) collective-permute-start(bf16[64,768]{1,0:T(8,128)(2,1)S(1)} %shard_map.129), channel_id=1, source_target_pairs={{0,1},{1,0},{2,3},{3,2},{4,5},{5,4},{6,7},{7,6},{8,9},{9,8},{10,11... | collective-permute-start | bytes 294920 | tf_op jit(solution)/shard_map/ppermute | solution.py:763
  37.7 2.0 %shard_map.128 = (f32[512,768]{1,0:T(8,128)S(1)}, f32[64,768]{1,0:T(8,128)S(1)}, f32[512,768]{1,0:T(8,128)S(1)}, f32[512,768]{1,0:T(8,128)S(1)}) custom-call(f32[576,768]{1,0:T(8,128)S(1)} %shard_map.127.early_ref, bf16[576,128]{1,0:T(8,128)(2,1)S(1)} %collective-permute-done.6.got_ref, f32[1,32]{1,0:T(1,128)S(1)} %bitcast.8, bf16[1152,768]{1,0:T(8,128)(2,1)S(1)} %copy-done, ...), custom_call_target="tpu_custom_call" | custom-call | flops 2000000000 | bytes 2000000 | tf_op jit(solution)/shard_map/pallas_call | solution.py:767
  39.7 0.0 collective-permute-done.7.lon_ref
  39.7 1.7 %shard_map.130 = f32[32,16,768]{2,1,0:T(8,128)} custom-call(f32[512,768]{1,0:T(8,128)S(1)} %get-tuple-element.65.field_ref, f32[512,768]{1,0:T(8,128)S(1)} %get-tuple-element.66.first_ref, f32[512,768]{1,0:T(8,128)S(1)} %get-tuple-element.67.last_ref, bf16[64,768]{1,0:T(8,128)(2,1)S(1)} %collective-permute-done.7.lon_ref, ...), custom_call_target="tpu_custom_call" | custom-call | flops 1500000000 | bytes 1500000 | tf_op jit(solution)/shard_map/pallas_call | solution.py:769
Async XLA Ops:
  0.0 3.5 %copy-start.3 = (f32[1024]{0:T(1024)S(1)}, f32[1024]{0:T(1024)}, u32[]{:S(2)}) copy-start(f32[1024]{0:T(1024)} %param.13) | copy-start | bytes 12292
  1.5 1.9 %collective-permute-start = (bf16[8,16,1024]{2,1,0:T(8,128)(2,1)S(1)}, bf16[8,16,1024]{2,1,0:T(8,128)(2,1)S(1)}, u32[]{:S(2)}, u32[]{:S(2)}) collective-permute-start(bf16[8,16,1024]{2,1,0:T(8,128)(2,1)S(1)} %get-tuple-element.38), channel_id=1, source_target_pairs={{0,1},{1,0},{2,3},{3,2},{4,5},{5,4},{6,7},{7,6},{8,9},{9,8},{10,11... | collective-permute-start | bytes 786440 | tf_op jit(solution)/shard_map/ppermute | solution.py:668
  2.3 8.8 %collective-permute-start.1 = (f32[32,16,384]{2,1,0:T(8,128)S(1)}, f32[32,16,384]{2,1,0:T(8,128)S(1)}, u32[]{:S(2)}, u32[]{:S(2)}) collective-permute-start(f32[32,16,384]{2,1,0:T(8,128)S(1)} %get-tuple-element.40), channel_id=1, source_target_pairs={{0,1},{1,0},{2,3},{3,2},{4,5},{5,4},{6,7},{7,6},{8,9},{9,8},{10,11... | collective-permute-start | bytes 2359304 | tf_op jit(solution)/shard_map/ppermute | solution.py:669
  2.4 12.4 %collective-permute-start.3 = (bf16[4,64,1024]{2,1,0:T(8,128)(2,1)S(1)}, bf16[4,64,1024]{2,1,0:T(8,128)(2,1)S(1)}, u32[]{:S(2)}, u32[]{:S(2)}) collective-permute-start(bf16[4,64,1024]{2,1,0:T(8,128)(2,1)S(1)} %get-tuple-element.49), channel_id=1, source_target_pairs={{0,2},{2,4},{4,6},{6,8},{8,10},{10,12},{12,14},{14,15},{3,1},{5,3}... | collective-permute-start | bytes 1572872 | tf_op jit(solution)/shard_map/ppermute | solution.py:667
  3.5 7.7 %copy-start.2 = (f32[32]{0:T(128)S(1)}, f32[32]{0:T(128)}, u32[]{:S(2)}) copy-start(f32[32]{0:T(128)} %param.18) | copy-start | bytes 388
  12.0 2.3 %collective-permute-start.2 = (bf16[64,768]{1,0:T(8,128)(2,1)S(1)}, bf16[64,768]{1,0:T(8,128)(2,1)S(1)}, u32[]{:S(2)}, u32[]{:S(2)}) collective-permute-start(bf16[64,768]{1,0:T(8,128)(2,1)S(1)} %shard_map.120), channel_id=1, source_target_pairs={{0,1},{1,0},{2,3},{3,2},{4,5},{5,4},{6,7},{7,6},{8,9},{9,8},{10,11... | collective-permute-start | bytes 294920 | tf_op jit(solution)/shard_map/ppermute | solution.py:715
  14.3 11.4 %collective-permute-start.4 = (bf16[176,1024]{1,0:T(8,128)(2,1)S(1)}, bf16[176,1024]{1,0:T(8,128)(2,1)S(1)}, u32[]{:S(2)}, u32[]{:S(2)}) collective-permute-start(bf16[176,1024]{1,0:T(8,128)(2,1)S(1)} %shard_map.122), channel_id=1, source_target_pairs={{0,2},{2,4},{4,6},{6,8},{8,10},{10,12},{12,14},{14,15},{3,1},{5,3}... | collective-permute-start | bytes 1081352 | tf_op jit(solution)/shard_map/ppermute | solution.py:729
  20.9 13.3 %collective-permute-start.5 = (bf16[576,256]{1,0:T(8,128)(2,1)S(1)}, bf16[576,256]{1,0:T(8,128)(2,1)S(1)}, u32[]{:S(2)}, u32[]{:S(2)}) collective-permute-start(bf16[576,256]{1,0:T(8,128)(2,1)S(1)} %get-tuple-element.63.refs_2_), channel_id=1, source_target_pairs={{1,2},{3,4},{5,6},{7,8},{9,10},{11,12},{13,14},{2,1},{4,3},{6,5},{... | collective-permute-start | bytes 884744 | tf_op jit(solution)/shard_map/ppermute | solution.py:750
  29.0 4.1 %copy-start = (bf16[1152,768]{1,0:T(8,128)(2,1)S(1)}, bf16[1152,768]{1,0:T(8,128)(2,1)}, u32[]{:S(2)}) copy-start(bf16[1152,768]{1,0:T(8,128)(2,1)} %constant.10.clone.high_ref) | copy-start | bytes 5308420
  29.0 4.1 %copy-start.1 = (bf16[1152,768]{1,0:T(8,128)(2,1)S(1)}, bf16[1152,768]{1,0:T(8,128)(2,1)}, u32[]{:S(2)}) copy-start(bf16[1152,768]{1,0:T(8,128)(2,1)} %constant.11.clone.low_ref) | copy-start | bytes 5308420
  29.0 7.7 %collective-permute-start.6 = (bf16[576,128]{1,0:T(8,128)(2,1)S(1)}, bf16[576,128]{1,0:T(8,128)(2,1)S(1)}, u32[]{:S(2)}, u32[]{:S(2)}) collective-permute-start(bf16[576,128]{1,0:T(8,128)(2,1)S(1)} %get-tuple-element.64.refs_3_), channel_id=1, source_target_pairs={{1,2},{3,4},{5,6},{7,8},{9,10},{11,12},{13,14},{2,1},{4,3},{6,5},{... | collective-permute-start | bytes 442376 | tf_op jit(solution)/shard_map/ppermute | solution.py:750
  37.0 2.8 %collective-permute-start.7 = (bf16[64,768]{1,0:T(8,128)(2,1)S(1)}, bf16[64,768]{1,0:T(8,128)(2,1)S(1)}, u32[]{:S(2)}, u32[]{:S(2)}) collective-permute-start(bf16[64,768]{1,0:T(8,128)(2,1)S(1)} %shard_map.129), channel_id=1, source_target_pairs={{0,1},{1,0},{2,3},{3,2},{4,5},{5,4},{6,7},{7,6},{8,9},{9,8},{10,11... | collective-permute-start | bytes 294920 | tf_op jit(solution)/shard_map/ppermute | solution.py:763

commit v7 on v6

--- a/solution.py
+++ b/solution.py
@@ -128,14 +128,12 @@
     return copies
 
 
-def pack_kernel(tok_ref, state_ref, give_ref, more_ref, edge_ref, give_state_ref, whole_ref, sems):
+def pack_kernel(tok_ref, state_ref, give_ref, edge_ref, give_state_ref, whole_ref, sems):
     lon = place()[0]
     rows = give_state_ref.shape[1]
     give_rows = pl.ds(HALF * (1 - lon), HALF)
-    more = more_ref.shape[1]
     pairs = [
         (tok_ref.at[give_rows, pl.ds(0, whole_ref.shape[1]), :], whole_ref),
-        (tok_ref.at[give_rows, pl.ds(tok_ref.shape[1] - more, more), :], more_ref),
         (tok_ref.at[:, pl.ds(0, edge_ref.shape[1]), :], edge_ref),
         (state_ref.at[:, pl.ds(pl.multiple_of(rows * (1 - lon), 8), rows), :], give_state_ref),
     ]
@@ -201,6 +199,7 @@
     state_ref,
     high_ref,
     low_ref,
+    more_ref,
     tok_ref,
     raw_ref,
     normed_ref,
@@ -212,7 +211,8 @@
     cols = tok_ref.shape[1]
     width = wq_ref.shape[0]
     keys, values = pl.ds(0, width), pl.ds(width, width)
-    own_rows = pl.ds(HALF * lon, HALF)
+    own_rows, give_rows = pl.ds(HALF * lon, HALF), pl.ds(HALF * (1 - lon), HALF)
+    more = more_ref.shape[1]
     state_rows = pl.ds(pl.multiple_of(state_ref.shape[1] * lon, 8), state_ref.shape[1])
     copies = run_copies(
         sems,
@@ -226,6 +226,7 @@
             (state_hbm.at[:, state_rows, :], state_ref),
             (high_hbm, high_ref),
             (low_hbm, low_ref),
+            (tok_hbm.at[give_rows, pl.ds(cols - more, more), :], more_ref),
         ],
     )
 
@@ -648,19 +649,18 @@
 
     hbm, vmem = pl.BlockSpec(memory_space=pltpu.HBM), pl.BlockSpec(memory_space=pltpu.VMEM)
     in_hbm = functools.partial(pltpu.with_memory_space_constraint, memory_space=pltpu.HBM)
-    give, more, give_edge, give_state = pl.pallas_call(
+    give, give_edge, give_state = pl.pallas_call(
         pack_kernel,
         out_shape=[
             pltpu.VMEM((HALF, split, width), BF16),
-            pltpu.VMEM((HALF, step, width), BF16),
             pltpu.VMEM((tok_rows, 2 * WIN, width), BF16),
             pltpu.VMEM((channels, band_rows, state_cols), F32),
         ],
         in_specs=[hbm, hbm],
-        out_specs=[vmem] * 4,
+        out_specs=[vmem] * 3,
         scratch_shapes=[
             pltpu.VMEM((HALF, split + 2 * WIN, width), BF16),
-            pltpu.SemaphoreType.DMA((4,)),
+            pltpu.SemaphoreType.DMA((3,)),
         ],
         compiler_params=pltpu.CompilerParams(vmem_limit_bytes=12 * MIB),
     )(in_hbm(tokens), in_hbm(state))
@@ -677,7 +677,7 @@
     dec_high, dec_low = (jnp.asarray(m) for m in split_high_low(matrix[order]))
 
     n_out = w_dec.shape[1]
-    qkv_own, w_dec_t, w_mix_t, decoded_own, *weights, own_state, high, low = pl.pallas_call(
+    qkv_own, w_dec_t, w_mix_t, decoded_own, *weights, own_state, high, low, more = pl.pallas_call(
         own_kernel,
         out_shape=[
             pltpu.VMEM((tokens_half, 3 * width), BF16),
@@ -689,16 +689,17 @@
             pltpu.VMEM((channels, band_rows, state_cols), F32),
             pltpu.VMEM((length, length), BF16),
             pltpu.VMEM((length, length), BF16),
+            pltpu.VMEM((HALF, step, width), BF16),
         ],
         in_specs=[hbm, vmem, vmem] + [hbm] * 7,
-        out_specs=[vmem] * 9,
+        out_specs=[vmem] * 10,
         scratch_shapes=[
             pltpu.VMEM((HALF, tok_cols, width), BF16),
             pltpu.VMEM((tokens_half, width), BF16),
             pltpu.VMEM((tokens_half, width), BF16),
             pltpu.VMEM(w_dec.shape, BF16),
             pltpu.VMEM(w_out.shape, BF16),
-            pltpu.SemaphoreType.DMA((9,)),
+            pltpu.SemaphoreType.DMA((10,)),
         ],
         cost_estimate=work(7.5),
         compiler_params=pltpu.CompilerParams(vmem_limit_bytes=32 * MIB),

time: 42.3 us -> 42.2 us (level)
  the two profiles are of different devices: /device:TPU:15 before, /device:TPU:0 now
where the time goes in v7:
time: 42.2 us; the launch traced here: 42 us
  Pallas kernels  27.6 us (65%)
  starting transfers between devices  12 us (28%)
  waiting for transfers between devices  2.06 us (5%)
    pallas_call x2, Pallas kernels, body(): call(functools.partial(main_kernel, first), (pltpu.VMEM((band, cols * PAT...  9.29 us
    pallas_call x1, Pallas kernels, body(): pl.pallas_call(own_kernel, out_shape=[pltpu.VMEM((tokens_half, 3 * width)...  7.68 us
    ppermute x1, starting transfers between devices, body(): from_lon = lax.ppermute(to_lon, 'lon', swap)  4.89 us
    ppermute x1, starting transfers between devices, body(): got_tokens = [lax.ppermute(give, both, shift)]  2.95 us
    pallas_call x2, Pallas kernels, state_half(): call(kernel, half, 5, [half], micros=1.4)  2.74 us
    pallas_call x1, Pallas kernels, body(): call(inner_kernel, (field, edge, field, field), 5, micros=2.0)(*late)  1.98 us
    ppermute x1, starting transfers between devices, body(): got_tokens.append(lax.ppermute(last_piece, both, shift))  1.77 us
    ppermute x2, starting transfers between devices, body(): got.append(lax.ppermute(sent, both, meet_all))  1.7 us
  transfers between devices with their start and end apart: 8, of which 2 were waited for; matrix products, arithmetic and copies ran while one was open for 0% of the time, Pallas kernels for 58%

profile of v7, /device:TPU:0, one launch (start us, length us, event | category | flops | bytes accessed | tf_op | source)
XLA Modules:
  0.0 42.0 jit_solution(12286188240030203740)
XLA Ops:
  0.0 0.0 copy-start.3
  0.0 1.4 %shard_map.118 = (bf16[4,64,1024]{2,1,0:T(8,128)(2,1)S(1)}, bf16[8,16,1024]{2,1,0:T(8,128)(2,1)S(1)}, f32[32,16,384]{2,1,0:T(8,128)S(1)}) custom-call(bf16[8,96,1024]{2,1,0:T(8,128)(2,1)} %tok_hbm.1, f32[32,32,384]{2,1,0:T(8,128)} %state_hbm.1), custom_call_target="tpu_custom_call" | custom-call | tf_op jit(solution)/shard_map/pallas_call | solution.py:652
  1.5 0.5 %collective-permute-start = (bf16[8,16,1024]{2,1,0:T(8,128)(2,1)S(1)}, bf16[8,16,1024]{2,1,0:T(8,128)(2,1)S(1)}, u32[]{:S(2)}, u32[]{:S(2)}) collective-permute-start(bf16[8,16,1024]{2,1,0:T(8,128)(2,1)S(1)} %get-tuple-element.37), channel_id=1, source_target_pairs={{0,1},{1,0},{2,3},{3,2},{4,5},{5,4},{6,7},{7,6},{8,9},{9,8},{10,11... | collective-permute-start | bytes 786440 | tf_op jit(solution)/shard_map/ppermute | solution.py:668
  2.0 0.1 collective-permute-start.1
  2.1 2.9 %collective-permute-start.3 = (bf16[4,64,1024]{2,1,0:T(8,128)(2,1)S(1)}, bf16[4,64,1024]{2,1,0:T(8,128)(2,1)S(1)}, u32[]{:S(2)}, u32[]{:S(2)}) collective-permute-start(bf16[4,64,1024]{2,1,0:T(8,128)(2,1)S(1)} %get-tuple-element.49), channel_id=1, source_target_pairs={{0,2},{2,4},{4,6},{6,8},{8,10},{10,12},{12,14},{14,15},{3,1},{5,3}... | collective-permute-start | bytes 1572872 | tf_op jit(solution)/shard_map/ppermute | solution.py:667
  5.0 0.0 collective-permute-done.edge_ref
  5.0 0.0 copy-done.3
  5.0 0.0 copy-start.2
  5.0 7.7 %shard_map.119 = (bf16[384,3072]{1,0:T(8,128)(2,1)S(1)}, bf16[512,1024]{1,0:T(8,128)(2,1)S(1)}, bf16[512,1024]{1,0:T(8,128)(2,1)S(1)}, f32[512,384]{1,0:T(8,128)...) custom-call(bf16[8,96,1024]{2,1,0:T(8,128)(2,1)} %tok_hbm.1, ...), custom_call_target="tpu_custom_call" | custom-call | flops 7500000256 | bytes 7500000 | tf_op jit(solution)/shard_map/pallas_call | solution.py:680
  12.7 0.0 collective-permute-done.1.got_ref
  12.7 0.0 copy-done.2
  12.7 0.8 %shard_map.120 = bf16[64,768]{1,0:T(8,128)(2,1)S(1)} custom-call(f32[32,16,384]{2,1,0:T(8,128)S(1)} %get-tuple-element.60.state_ref, f32[32,16,384]{2,1,0:T(8,128)S(1)} %collective-permute-done.1.got_ref, f32[1,32]{1,0:T(1,128)S(1)} %bitcast.2, bf16[768,768]{1,0:T(8,128)(2,1)S(1)} %get-tuple-element.43.high_ref, bf16[768,768]{1,0:T(8,128)(2,1)S(1)} %get-tuple-element.44.low_ref), custom_call_target="tpu_custom_call" | custom-call | flops 1000000000 | bytes 1000000 | tf_op jit(solution)/shard_map/pallas_call | solution.py:710
  13.5 0.1 collective-permute-start.2
  13.6 1.4 %shard_map.121.upper_ref = f32[256,768]{1,0:T(8,128)S(1)} custom-call(f32[32,16,384]{2,1,0:T(8,128)S(1)} %get-tuple-element.60.state_ref, f32[32,16,384]{2,1,0:T(8,128)S(1)} %collective-permute-done.1.got_ref, f32[1,32]{1,0:T(1,128)S(1)} %bitcast.3, bf16[768,768]{1,0:T(8,128)(2,1)S(1)} %get-tuple-element.43.high_ref, ...), custom_call_target="tpu_custom_call" | custom-call | flops 1400000000 | bytes 1400000 | tf_op jit(solution)/shard_map/pallas_call | solution.py:721
  15.0 0.0 collective-permute-done.2.base_edge_ref
  15.0 0.1 shard_map.122
  15.0 1.8 %collective-permute-start.4 = (bf16[176,1024]{1,0:T(8,128)(2,1)S(1)}, bf16[176,1024]{1,0:T(8,128)(2,1)S(1)}, u32[]{:S(2)}, u32[]{:S(2)}) collective-permute-start(bf16[176,1024]{1,0:T(8,128)(2,1)S(1)} %shard_map.122), channel_id=1, source_target_pairs={{0,2},{2,4},{4,6},{6,8},{8,10},{10,12},{12,14},{14,15},{3,1},{5,3}... | collective-permute-start | bytes 1081352 | tf_op jit(solution)/shard_map/ppermute | solution.py:730
  16.8 0.5 %collective-permute-done.3.x_ref = bf16[4,64,1024]{2,1,0:T(8,128)(2,1)S(1)} collective-permute-done((bf16[4,64,1024]{2,1,0:T(8,128)(2,1)S(1)}, bf16[4,64,1024]{2,1,0:T(8,128)(2,1)S(1)}, u32[]{:S(2)}, u32[]{:S(2)}) %collective-permute-start.3) | collective-permute-done | bytes 524320 | tf_op jit(solution)/shard_map/ppermute | solution.py:667
  17.3 6.1 %shard_map.123 = (bf16[512,256]{1,0:T(8,128)(2,1)S(1)}, bf16[576,256]{1,0:T(8,128)(2,1)S(1)}) custom-call(bf16[4,64,1024]{2,1,0:T(8,128)(2,1)S(1)} %collective-permute-done.3.x_ref, f32[1,1024]{1,0:T(1,128)S(1)} %bitcast.10, bf16[384,3072]{1,0:T(8,128)(2,1)S(1)} %get-tuple-element.50.refs_1_, f32[512,384]{1,0:T(8,128)S(1)} %get-tuple-element.51.refs_2_, ...), custom_call_target="tpu_custom_call" | custom-call | flops 6000000000 | bytes 6000000 | tf_op jit(solution)/shard_map/pallas_call | solution.py:735
  23.4 0.7 %collective-permute-start.5 = (bf16[576,256]{1,0:T(8,128)(2,1)S(1)}, bf16[576,256]{1,0:T(8,128)(2,1)S(1)}, u32[]{:S(2)}, u32[]{:S(2)}) collective-permute-start(bf16[576,256]{1,0:T(8,128)(2,1)S(1)} %get-tuple-element.63.refs_2_), channel_id=1, source_target_pairs={{1,2},{3,4},{5,6},{7,8},{9,10},{11,12},{13,14},{2,1},{4,3},{6,5},{... | collective-permute-start | bytes 884744 | tf_op jit(solution)/shard_map/ppermute | solution.py:751
  24.1 1.5 %collective-permute-done.4.x_ref.piece_ref = bf16[176,1024]{1,0:T(8,128)(2,1)S(1)} collective-permute-done((bf16[176,1024]{1,0:T(8,128)(2,1)S(1)}, bf16[176,1024]{1,0:T(8,128)(2,1)S(1)}, u32[]{:S(2)}, u32[]{:S(2)}) %collective-permute-start.4) | collective-permute-done | bytes 360480 | tf_op jit(solution)/shard_map/ppermute | solution.py:730
  25.6 3.2 %shard_map.124 = (bf16[512,128]{1,0:T(8,128)(2,1)S(1)}, bf16[576,128]{1,0:T(8,128)(2,1)S(1)}) custom-call(bf16[176,1024]{1,0:T(8,128)(2,1)S(1)} %collective-permute-done.4.x_ref.piece_ref, f32[1,1024]{1,0:T(1,128)S(1)} %bitcast.11, bf16[384,3072]{1,0:T(8,128)(2,1)S(1)} %get-tuple-element.50.refs_1_, f32[512,384]{1,0:T(8,128)S(1)} %get-tuple-element.51.refs_2_, ...), custom_call_target="tpu_custom_call" | custom-call | flops 3000000000 | bytes 3000000 | tf_op jit(solution)/shard_map/pallas_call | solution.py:735
  28.8 0.0 copy-start
  28.9 0.0 copy-start.1
  28.9 1.0 %collective-permute-start.6 = (bf16[576,128]{1,0:T(8,128)(2,1)S(1)}, bf16[576,128]{1,0:T(8,128)(2,1)S(1)}, u32[]{:S(2)}, u32[]{:S(2)}) collective-permute-start(bf16[576,128]{1,0:T(8,128)(2,1)S(1)} %get-tuple-element.64.refs_3_), channel_id=1, source_target_pairs={{1,2},{3,4},{5,6},{7,8},{9,10},{11,12},{13,14},{2,1},{4,3},{6,5},{... | collective-permute-start | bytes 442376 | tf_op jit(solution)/shard_map/ppermute | solution.py:751
  29.9 1.4 %shard_map.125.lower_ref = f32[256,768]{1,0:T(8,128)S(1)} custom-call(f32[32,16,384]{2,1,0:T(8,128)S(1)} %get-tuple-element.60.state_ref, f32[32,16,384]{2,1,0:T(8,128)S(1)} %collective-permute-done.1.got_ref, f32[1,32]{1,0:T(1,128)S(1)} %bitcast.4, bf16[768,768]{1,0:T(8,128)(2,1)S(1)} %get-tuple-element.43.high_ref, ...), custom_call_target="tpu_custom_call" | custom-call | flops 1400000000 | bytes 1400000 | tf_op jit(solution)/shard_map/pallas_call | solution.py:721
  31.3 0.0 copy-done
  31.3 0.0 copy-done.1
  31.3 1.1 %shard_map.126.early_ref = f32[576,768]{1,0:T(8,128)S(1)} custom-call(f32[256,768]{1,0:T(8,128)S(1)} %shard_map.121.upper_ref, f32[256,768]{1,0:T(8,128)S(1)} %shard_map.125.lower_ref, bf16[176,1024]{1,0:T(8,128)(2,1)S(1)} %collective-permute-done.4.x_ref.piece_ref, f32[1,32]{1,0:T(1,128)S(1)} %bitcast.5, bf16[1152,768]{1,0:T(8,128)(2,1)S(1)} %copy-done, ...), custom_call_target="tpu_custom_call" | custom-call | flops 1200000000 | bytes 1200000 | tf_op jit(solution)/shard_map/pallas_call | solution.py:755
  32.4 0.0 collective-permute-done.5.got_ref
  32.4 0.6 %shard_map.127.early_ref = f32[576,768]{1,0:T(8,128)S(1)} custom-call(f32[576,768]{1,0:T(8,128)S(1)} %shard_map.126.early_ref, bf16[576,256]{1,0:T(8,128)(2,1)S(1)} %collective-permute-done.5.got_ref, f32[1,32]{1,0:T(1,128)S(1)} %bitcast.6, bf16[1152,768]{1,0:T(8,128)(2,1)S(1)} %copy-done, bf16[1152,768]{1,0:T(8,128)(2,1)S(1)} %copy-done.1), custom_call_target="tpu_custom_call" | custom-call | flops 1000000000 | bytes 1000000 | tf_op jit(solution)/shard_map/pallas_call | solution.py:760
  33.1 0.0 collective-permute-done.6.got_ref
  33.1 0.2 shard_map.129
  33.3 4.9 %collective-permute-start.7 = (bf16[64,768]{1,0:T(8,128)(2,1)S(1)}, bf16[64,768]{1,0:T(8,128)(2,1)S(1)}, u32[]{:S(2)}, u32[]{:S(2)}) collective-permute-start(bf16[64,768]{1,0:T(8,128)(2,1)S(1)} %shard_map.129), channel_id=1, source_target_pairs={{0,1},{1,0},{2,3},{3,2},{4,5},{5,4},{6,7},{7,6},{8,9},{9,8},{10,11... | collective-permute-start | bytes 294920 | tf_op jit(solution)/shard_map/ppermute | solution.py:764
  38.2 2.0 %shard_map.128 = (f32[512,768]{1,0:T(8,128)S(1)}, f32[64,768]{1,0:T(8,128)S(1)}, f32[512,768]{1,0:T(8,128)S(1)}, f32[512,768]{1,0:T(8,128)S(1)}) custom-call(f32[576,768]{1,0:T(8,128)S(1)} %shard_map.127.early_ref, bf16[576,128]{1,0:T(8,128)(2,1)S(1)} %collective-permute-done.6.got_ref, f32[1,32]{1,0:T(1,128)S(1)} %bitcast.8, bf16[1152,768]{1,0:T(8,128)(2,1)S(1)} %copy-done, ...), custom_call_target="tpu_custom_call" | custom-call | flops 2000000000 | bytes 2000000 | tf_op jit(solution)/shard_map/pallas_call | solution.py:768
  40.2 0.0 collective-permute-done.7.lon_ref
  40.2 1.7 %shard_map.130 = f32[32,16,768]{2,1,0:T(8,128)} custom-call(f32[512,768]{1,0:T(8,128)S(1)} %get-tuple-element.65.field_ref, f32[512,768]{1,0:T(8,128)S(1)} %get-tuple-element.66.first_ref, f32[512,768]{1,0:T(8,128)S(1)} %get-tuple-element.67.last_ref, bf16[64,768]{1,0:T(8,128)(2,1)S(1)} %collective-permute-done.7.lon_ref, ...), custom_call_target="tpu_custom_call" | custom-call | flops 1500000000 | bytes 1500000 | tf_op jit(solution)/shard_map/pallas_call | solution.py:770
Async XLA Ops:
  0.0 5.0 %copy-start.3 = (f32[1024]{0:T(1024)S(1)}, f32[1024]{0:T(1024)}, u32[]{:S(2)}) copy-start(f32[1024]{0:T(1024)} %param.13) | copy-start | bytes 12292
  1.5 3.5 %collective-permute-start = (bf16[8,16,1024]{2,1,0:T(8,128)(2,1)S(1)}, bf16[8,16,1024]{2,1,0:T(8,128)(2,1)S(1)}, u32[]{:S(2)}, u32[]{:S(2)}) collective-permute-start(bf16[8,16,1024]{2,1,0:T(8,128)(2,1)S(1)} %get-tuple-element.37), channel_id=1, source_target_pairs={{0,1},{1,0},{2,3},{3,2},{4,5},{5,4},{6,7},{7,6},{8,9},{9,8},{10,11... | collective-permute-start | bytes 786440 | tf_op jit(solution)/shard_map/ppermute | solution.py:668
  2.0 10.7 %collective-permute-start.1 = (f32[32,16,384]{2,1,0:T(8,128)S(1)}, f32[32,16,384]{2,1,0:T(8,128)S(1)}, u32[]{:S(2)}, u32[]{:S(2)}) collective-permute-start(f32[32,16,384]{2,1,0:T(8,128)S(1)} %get-tuple-element.40), channel_id=1, source_target_pairs={{0,1},{1,0},{2,3},{3,2},{4,5},{5,4},{6,7},{7,6},{8,9},{9,8},{10,11... | collective-permute-start | bytes 2359304 | tf_op jit(solution)/shard_map/ppermute | solution.py:669
  2.1 15.3 %collective-permute-start.3 = (bf16[4,64,1024]{2,1,0:T(8,128)(2,1)S(1)}, bf16[4,64,1024]{2,1,0:T(8,128)(2,1)S(1)}, u32[]{:S(2)}, u32[]{:S(2)}) collective-permute-start(bf16[4,64,1024]{2,1,0:T(8,128)(2,1)S(1)} %get-tuple-element.49), channel_id=1, source_target_pairs={{0,2},{2,4},{4,6},{6,8},{8,10},{10,12},{12,14},{14,15},{3,1},{5,3}... | collective-permute-start | bytes 1572872 | tf_op jit(solution)/shard_map/ppermute | solution.py:667
  5.0 7.7 %copy-start.2 = (f32[32]{0:T(128)S(1)}, f32[32]{0:T(128)}, u32[]{:S(2)}) copy-start(f32[32]{0:T(128)} %param.18) | copy-start | bytes 388
  13.5 1.5 %collective-permute-start.2 = (bf16[64,768]{1,0:T(8,128)(2,1)S(1)}, bf16[64,768]{1,0:T(8,128)(2,1)S(1)}, u32[]{:S(2)}, u32[]{:S(2)}) collective-permute-start(bf16[64,768]{1,0:T(8,128)(2,1)S(1)} %shard_map.120), channel_id=1, source_target_pairs={{0,1},{1,0},{2,3},{3,2},{4,5},{5,4},{6,7},{7,6},{8,9},{9,8},{10,11... | collective-permute-start | bytes 294920 | tf_op jit(solution)/shard_map/ppermute | solution.py:716
  15.0 10.6 %collective-permute-start.4 = (bf16[176,1024]{1,0:T(8,128)(2,1)S(1)}, bf16[176,1024]{1,0:T(8,128)(2,1)S(1)}, u32[]{:S(2)}, u32[]{:S(2)}) collective-permute-start(bf16[176,1024]{1,0:T(8,128)(2,1)S(1)} %shard_map.122), channel_id=1, source_target_pairs={{0,2},{2,4},{4,6},{6,8},{8,10},{10,12},{12,14},{14,15},{3,1},{5,3}... | collective-permute-start | bytes 1081352 | tf_op jit(solution)/shard_map/ppermute | solution.py:730
  23.4 9.0 %collective-permute-start.5 = (bf16[576,256]{1,0:T(8,128)(2,1)S(1)}, bf16[576,256]{1,0:T(8,128)(2,1)S(1)}, u32[]{:S(2)}, u32[]{:S(2)}) collective-permute-start(bf16[576,256]{1,0:T(8,128)(2,1)S(1)} %get-tuple-element.63.refs_2_), channel_id=1, source_target_pairs={{1,2},{3,4},{5,6},{7,8},{9,10},{11,12},{13,14},{2,1},{4,3},{6,5},{... | collective-permute-start | bytes 884744 | tf_op jit(solution)/shard_map/ppermute | solution.py:751
  28.8 2.4 %copy-start = (bf16[1152,768]{1,0:T(8,128)(2,1)S(1)}, bf16[1152,768]{1,0:T(8,128)(2,1)}, u32[]{:S(2)}) copy-start(bf16[1152,768]{1,0:T(8,128)(2,1)} %constant.10.clone.high_ref) | copy-start | bytes 5308420
  28.9 2.4 %copy-start.1 = (bf16[1152,768]{1,0:T(8,128)(2,1)S(1)}, bf16[1152,768]{1,0:T(8,128)(2,1)}, u32[]{:S(2)}) copy-start(bf16[1152,768]{1,0:T(8,128)(2,1)} %constant.11.clone.low_ref) | copy-start | bytes 5308420
  28.9 4.2 %collective-permute-start.6 = (bf16[576,128]{1,0:T(8,128)(2,1)S(1)}, bf16[576,128]{1,0:T(8,128)(2,1)S(1)}, u32[]{:S(2)}, u32[]{:S(2)}) collective-permute-start(bf16[576,128]{1,0:T(8,128)(2,1)S(1)} %get-tuple-element.64.refs_3_), channel_id=1, source_target_pairs={{1,2},{3,4},{5,6},{7,8},{9,10},{11,12},{13,14},{2,1},{4,3},{6,5},{... | collective-permute-start | bytes 442376 | tf_op jit(solution)/shard_map/ppermute | solution.py:751
  33.3 6.9 %collective-permute-start.7 = (bf16[64,768]{1,0:T(8,128)(2,1)S(1)}, bf16[64,768]{1,0:T(8,128)(2,1)S(1)}, u32[]{:S(2)}, u32[]{:S(2)}) collective-permute-start(bf16[64,768]{1,0:T(8,128)(2,1)S(1)} %shard_map.129), channel_id=1, source_target_pairs={{0,1},{1,0},{2,3},{3,2},{4,5},{5,4},{6,7},{7,6},{8,9},{9,8},{10,11... | collective-permute-start | bytes 294920 | tf_op jit(solution)/shard_map/ppermute | solution.py:764
